TPU v7x, 32 devices: a whole 2x2x4 slice. The times are simulated.
32 devices in a mesh: groups: 2 (over x), tok: 16 (over z, y, core).
Axes of the slice: x: 2, y: 2, z: 4, core: 2. Of those that a mesh axis runs over, the one named last changes fastest.
Arguments:
- tokens: bfloat16 [4, 8192, 512], P('groups', 'tok'), parts along dimension 0, may hold values from -28 to 28
- w_query: bfloat16 [512, 512], replicated, may hold values from -0.25 to 0.25
- w_key: bfloat16 [512, 512], replicated, may hold values from -0.25 to 0.25
- w_value: bfloat16 [512, 512], replicated, may hold values from -0.25 to 0.25
- w_out: bfloat16 [512, 512], replicated, may hold values from -0.25 to 0.25
- partner_block: int32 [16, 4], P('tok'), may hold values from 0 to 3
- head_masks: int32 [16, 4, 8], P('tok'), may hold values 0 or 1
- cotangent: bfloat16 [4, 8192, 512], P('groups', 'tok'), parts along dimension 0, may hold values from -6 to 6
Outputs:
- output: bfloat16 [4, 8192, 512], P('groups', 'tok'), parts along dimension 0
- grad_tokens: bfloat16 [4, 8192, 512], P('groups', 'tok'), parts along dimension 0
- grad_query: float32 [1024, 512], P('groups'), parts along dimension 0
- grad_key: float32 [1024, 512], P('groups'), parts along dimension 0
- grad_value: float32 [1024, 512], P('groups'), parts along dimension 0
- grad_out: float32 [1024, 512], P('groups'), parts along dimension 0
There are 2 independent parts, one for each index of `groups`. A program takes and returns all parts, laid end to end along the dimension named above; an argument that names none is the same for every part. Nothing has to cross between parts.
All inputs are finite; a program needn't handle non-finite values. No bound on the sum of `head_masks` on one device may be relied on, other than what follows from the above.
Results may differ from a plain program's by a relative error of at most 0.015.
The roundings to bfloat16 on the way count: a program that leaves them out, or rounds other values in their place, can miss the bound.
Values may be sent and summed in bfloat16 or wider, within the bound.
No kernel may reach another device: no remote copies, remote signals or barrier semaphores. Data moves between devices by JAX's collectives and lax.ppermute only.
A program may use at most 128 MiB of HBM per device.

v0:
```python
import math

import jax
import jax.numpy as jnp
from jax import lax
from jax.sharding import PartitionSpec as P

SUB = 128


def partner(x, axis, stride):
    return lax.ppermute(x, axis, [(i, i ^ 1 << stride) for i in range(lax.axis_size(axis))])


def attend(queries, gathered, mask_rows, grad_output, w_out, score_scale):
    samples, block_rows, model_width = queries.shape
    head_count = mask_rows.shape[1]
    head_width = model_width // head_count
    key_count = gathered.shape[1]
    sub_rows = (key_count - block_rows) // 4
    f32 = jnp.float32
    query_heads = queries.reshape(samples, block_rows, head_count, head_width)
    key_heads = gathered[..., :model_width].reshape(samples, key_count, head_count, head_width)
    value_heads = gathered[..., model_width:].reshape(samples, key_count, head_count, head_width)
    visible = (
        jnp.concatenate(
            [
                jnp.ones((head_count, block_rows), jnp.int32),
                jnp.repeat(mask_rows.T, sub_rows, axis=1),
            ],
            1,
        )
        > 0
    )
    scores = (
        jnp.einsum("sqhd,skhd->shqk", query_heads, key_heads, preferred_element_type=f32)
        * score_scale
    )
    scores = jnp.where(visible[None, :, None, :], scores, -jnp.inf)
    row_max = jnp.max(scores, axis=-1, keepdims=True)
    expo_terms = jnp.exp(scores - row_max)
    probability = expo_terms / jnp.sum(expo_terms, axis=-1, keepdims=True)
    prob_half = probability.astype(jnp.bfloat16)
    context = jnp.einsum(
        "shqk,skhd->sqhd", prob_half, value_heads, preferred_element_type=f32
    ).astype(jnp.bfloat16)
    context_rows = context.reshape(samples * block_rows, model_width)
    output = jnp.dot(context_rows, w_out, preferred_element_type=f32).astype(jnp.bfloat16)
    grad_rows = grad_output.reshape(samples * block_rows, model_width)
    grad_context = jnp.dot(grad_rows, w_out.T, preferred_element_type=f32).astype(jnp.bfloat16)
    grad_context = grad_context.reshape(samples, block_rows, head_count, head_width)
    grad_prob = jnp.einsum("sqhd,skhd->shqk", grad_context, value_heads, preferred_element_type=f32)
    row_dot = jnp.sum(grad_context.astype(f32) * context.astype(f32), axis=-1).transpose(0, 2, 1)
    grad_score = (probability * (grad_prob - row_dot[..., None]) * score_scale).astype(jnp.bfloat16)
    grad_q = jnp.einsum(
        "shqk,skhd->sqhd", grad_score, key_heads, preferred_element_type=f32
    ).astype(jnp.bfloat16)
    grad_k = jnp.einsum("shqk,sqhd->skhd", grad_score, query_heads, preferred_element_type=f32)
    grad_v = jnp.einsum("shqk,sqhd->skhd", prob_half, grad_context, preferred_element_type=f32)
    key_grads = jnp.concatenate(
        [
            grad_k.reshape(samples, key_count, model_width),
            grad_v.reshape(samples, key_count, model_width),
        ],
        -1,
    )
    return (
        output.reshape(samples, block_rows, model_width),
        context_rows.reshape(samples, block_rows, model_width),
        grad_q.reshape(samples, block_rows, model_width),
        key_grads,
    )


def per_device(tokens, w_query, w_key, w_value, w_out, partner_block, head_masks, cotangent):
    f32 = jnp.float32
    samples, block_rows, model_width = tokens.shape
    levels = lax.axis_size("tok").bit_length() - 1
    sub_rows = SUB
    score_scale = 1.0 / math.sqrt(model_width // head_masks.shape[2])
    sent_starts = []
    for section in range(4):
        theirs = partner(partner_block, "tok", levels - 4 + section)
        sent_starts.append(theirs[0, section] * sub_rows)
    token_rows = tokens.reshape(samples * block_rows, model_width)
    queries = (
        jnp.dot(token_rows, w_query, preferred_element_type=f32)
        .astype(jnp.bfloat16)
        .reshape(samples, block_rows, model_width)
    )
    w_key_value = jnp.concatenate([w_key, w_value], 1)
    key_value = (
        jnp.dot(token_rows, w_key_value, preferred_element_type=f32)
        .astype(jnp.bfloat16)
        .reshape(samples, block_rows, 2 * model_width)
    )
    pieces = [key_value]
    for section in range(4):
        bit_number = levels - 4 + section
        chosen = lax.dynamic_slice_in_dim(tokens, sent_starts[section], sub_rows, 1)
        arrived = partner(chosen, "tok", bit_number)
        projected = jnp.dot(
            arrived.reshape(samples * sub_rows, model_width),
            w_key_value,
            preferred_element_type=f32,
        )
        pieces.append(projected.astype(jnp.bfloat16).reshape(samples, sub_rows, 2 * model_width))
    gathered = jnp.concatenate(pieces, 1)
    results = [
        attend(
            queries[sample : sample + 1],
            gathered[sample : sample + 1],
            head_masks[0],
            cotangent[sample : sample + 1],
            w_out,
            score_scale,
        )
        for sample in range(samples)
    ]
    output = jnp.concatenate([item[0] for item in results], 0)
    context = jnp.concatenate([item[1] for item in results], 0)
    grad_q = jnp.concatenate([item[2] for item in results], 0)
    key_grads = jnp.concatenate([item[3] for item in results], 0)
    own_grads = key_grads[:, :block_rows]
    for section in range(4):
        bit_number = levels - 4 + section
        first_row = block_rows + section * sub_rows
        part_grad = key_grads[:, first_row : first_row + sub_rows]
        returned = partner(part_grad, "tok", bit_number)
        current = lax.dynamic_slice_in_dim(own_grads, sent_starts[section], sub_rows, 1)
        own_grads = lax.dynamic_update_slice_in_dim(
            own_grads, current + returned, sent_starts[section], 1
        )
    grad_q_rows = grad_q.reshape(samples * block_rows, model_width)
    grad_kv_rows = own_grads.astype(jnp.bfloat16).reshape(samples * block_rows, 2 * model_width)
    grad_tokens = (
        jnp.dot(grad_q_rows, w_query.T, preferred_element_type=f32)
        + jnp.dot(grad_kv_rows, w_key_value.T, preferred_element_type=f32)
    ).astype(jnp.bfloat16)
    grad_query = jnp.dot(token_rows.T, grad_q_rows, preferred_element_type=f32)
    grad_pair = jnp.dot(token_rows.T, grad_kv_rows, preferred_element_type=f32)
    grad_out = jnp.dot(
        context.reshape(samples * block_rows, model_width).T,
        cotangent.reshape(samples * block_rows, model_width),
        preferred_element_type=f32,
    )
    summed = lax.psum(
        (grad_query, grad_pair[:, :model_width], grad_pair[:, model_width:], grad_out), "tok"
    )
    return (
        output,
        grad_tokens.reshape(samples, block_rows, model_width),
        summed[0],
        summed[1],
        summed[2],
        summed[3],
    )


def solution(mesh):
    placed = (
        P("groups", "tok", None),
        P(),
        P(),
        P(),
        P(),
        P("tok", None),
        P("tok", None, None),
        P("groups", "tok", None),
    )
    return jax.shard_map(
        per_device,
        mesh=mesh,
        in_specs=placed,
        out_specs=(
            P("groups", "tok", None),
            P("groups", "tok", None),
            P("groups", None),
            P("groups", None),
            P("groups", None),
            P("groups", None),
        ),
        check_vma=False,
    )
```

profile of v0, /device:TPU:0, one launch (start us, length us, event | category | flops | bytes accessed | tf_op | source)
XLA Modules:
  0.0 336.8 jit_solution(179325345437837072)
XLA Ops:
  7.2 3.0 collective-permute-start.2
  21.3 3.1 convolution_convert_fusion.1
  34.4 11.3 %collective-permute-done.7 = bf16[2,128,512]{2,1,0:T(8,128)(2,1)S(1)} collective-permute-done((bf16[2,128,512]{2,1,0:T(8,128)(2,1)S(1)}, bf16[2,128,512]{2,1,0:T(8,128)(2,1)S(1)}, u32[]{:S(2)}, u32[]{:S(2)}) %collective-permute-start.7) | collective-permute-done | bytes 262176 | tf_op jit(solution)/shard_map/ppermute | solution.py:12
  54.8 9.4 %fusion.35 = (f32[8,512]{1,0:T(8,128)S(1)}, f32[8,512,1024]{2,1,0:T(8,128)}) fusion(pred[8,1024]{1,0:T(8,128)(4,1)S(1)} %pad_compare_fusion, bf16[512,8,64]{0,2,1:T(8,128)(2,1)} %bitcast.188, bf16[1024,8,64]{0,2,1:T(8,128)(2,1)S(1)} %bitcast.173), kind=kOutput, calls=%fused_computation.85 | convolution fusion | flops 553649152 | bytes 18374656 | tf_op jit(solution)/shard_map/sub | solution.py:41
  64.1 7.0 %fusion.11 = bf16[8,512,1024]{2,1,0:T(8,128)(2,1)S(1)} fusion(f32[8,512,1024]{2,1,0:T(8,128)} %get-tuple-element.39, f32[8,512]{1,0:T(8,128)S(1)} %get-tuple-element.38), kind=kLoop, calls=%fused_computation.20 | loop fusion | flops 8388608 | bytes 25182208 | tf_op jit(solution)/shard_map/convert_element_type | solution.py:43
  71.2 2.9 fusion.41
  74.1 3.5 %fusion.17 = (f32[512,8]{0,1:T(8,128)S(1)}, bf16[8,64,512]{2,1,0:T(8,128)(2,1)}) fusion(bf16[1,512,8,64]{1,3,2,0:T(8,128)(2,1)S(1)} %bitcast.184, bf16[1024,8,64]{0,2,1:T(8,128)(2,1)S(1)} %bitcast.177, bf16[8,512,1024]{2,1,0:T(8,128)(2,1)S(1)} %fusion.11), kind=kOutput, calls=%fused_computation.51 | convolution fusion | flops 538177536 | bytes 10502144 | tf_op jit(solution)/shard_map/shqk,skhd->sqhd/dot_general | solution.py:44
  77.6 7.6 %multiply_convert_fusion = bf16[8,512,1024]{2,1,0:T(8,128)(2,1)S(1)} fusion(bf16[512,8,64]{0,2,1:T(8,128)(2,1)S(1)} %bitcast.185, bf16[1024,8,64]{0,2,1:T(8,128)(2,1)S(1)} %bitcast.178, f32[8,512]{1,0:T(8,128)S(1)} %bitcast.210, f32[8,512,1024]{2,1,0:T(8,128)} %get-tuple-element.39, f32[8,512]{1,0:T(8,128)S(1)} %get-tuple-element.38), kind=kOutput, calls=%fused_computation.2 | convolution fusion | flops 557842432 | bytes 26771456 | tf_op jit(solution)/shard_map/sqhd,skhd->shqk/dot_general | solution.py:52
  85.2 3.5 %convolution_convert_fusion.2 = bf16[8,64,512]{2,1,0:T(8,128)(2,1)} fusion(bf16[1024,8,64]{0,2,1:T(8,128)(2,1)S(1)} %bitcast.174, bf16[8,512,1024]{2,1,0:T(8,128)(2,1)S(1)} %multiply_convert_fusion), kind=kOutput, calls=%fused_computation.27 | convolution fusion | flops 537133056 | bytes 9961472 | tf_op jit(solution)/shard_map/shqk,skhd->sqhd/dot_general | solution.py:55
  95.3 3.1 copy.28
  101.3 9.4 %fusion.36 = (f32[8,512]{1,0:T(8,128)S(1)}, f32[8,512,1024]{2,1,0:T(8,128)}) fusion(pred[8,1024]{1,0:T(8,128)(4,1)S(1)} %pad_compare_fusion, bf16[512,8,64]{0,2,1:T(8,128)(2,1)} %bitcast.186, bf16[1024,8,64]{0,2,1:T(8,128)(2,1)S(1)} %bitcast.171), kind=kOutput, calls=%fused_computation.86 | convolution fusion | flops 553649152 | bytes 18374656 | tf_op jit(solution)/shard_map/sub | solution.py:41
  110.6 7.0 %fusion.10 = bf16[8,512,1024]{2,1,0:T(8,128)(2,1)S(1)} fusion(f32[8,512,1024]{2,1,0:T(8,128)} %get-tuple-element.41, f32[8,512]{1,0:T(8,128)S(1)} %get-tuple-element.40), kind=kLoop, calls=%fused_computation.19 | loop fusion | flops 8388608 | bytes 25182208 | tf_op jit(solution)/shard_map/convert_element_type | solution.py:43
  117.6 2.9 fusion.39
  120.6 3.5 %fusion.18 = (f32[512,8]{0,1:T(8,128)S(1)}, bf16[8,64,512]{2,1,0:T(8,128)(2,1)}) fusion(bf16[1,512,8,64]{1,3,2,0:T(8,128)(2,1)S(1)} %bitcast.181, bf16[1024,8,64]{0,2,1:T(8,128)(2,1)S(1)} %bitcast.175, bf16[8,512,1024]{2,1,0:T(8,128)(2,1)S(1)} %fusion.10), kind=kOutput, calls=%fused_computation.53 | convolution fusion | flops 538177536 | bytes 10502144 | tf_op jit(solution)/shard_map/shqk,skhd->sqhd/dot_general | solution.py:44
  124.0 7.7 %multiply_convert_fusion.1 = bf16[8,512,1024]{2,1,0:T(8,128)(2,1)S(1)} fusion(bf16[512,8,64]{0,2,1:T(8,128)(2,1)S(1)} %bitcast.182, bf16[1024,8,64]{0,2,1:T(8,128)(2,1)S(1)} %bitcast.176, f32[8,512]{1,0:T(8,128)S(1)} %bitcast.211, f32[8,512,1024]{2,1,0:T(8,128)} %get-tuple-element.41, f32[8,512]{1,0:T(8,128)S(1)} %get-tuple-element.40), kind=kOutput, calls=%fused_computation.3 | convolution fusion | flops 557842432 | bytes 26771456 | tf_op jit(solution)/shard_map/sqhd,skhd->shqk/dot_general | solution.py:52
  131.7 3.3 copy-done.1
  135.0 2.9 fusion.38
  137.9 3.0 copy.26
  140.9 3.1 copy.27
  146.9 6.8 %convolution_convert_fusion.4 = bf16[8,64,512]{2,1,0:T(8,128)(2,1)S(1)} fusion(bf16[1024,8,64]{0,2,1:T(8,128)(2,1)S(1)} %bitcast.172, bf16[8,512,1024]{2,1,0:T(8,128)(2,1)} %copy-done.1), kind=kOutput, calls=%fused_computation.29 | convolution fusion | flops 537133056 | bytes 9961472 | tf_op jit(solution)/shard_map/shqk,skhd->sqhd/dot_general | solution.py:55
  162.3 16.3 %collective-permute-done.9 = f32[2,128,1024]{2,1,0:T(8,128)S(1)} collective-permute-done((f32[2,128,1024]{2,1,0:T(8,128)S(1)}, f32[2,128,1024]{2,1,0:T(8,128)S(1)}, u32[]{:S(2)}, u32[]{:S(2)}) %collective-permute-start.9) | collective-permute-done | bytes 1048608 | tf_op jit(solution)/shard_map/ppermute | solution.py:12
  178.9 19.2 %collective-permute-done.10 = f32[2,128,1024]{2,1,0:T(8,128)S(1)} collective-permute-done((f32[2,128,1024]{2,1,0:T(8,128)S(1)}, f32[2,128,1024]{2,1,0:T(8,128)S(1)}, u32[]{:S(2)}, u32[]{:S(2)}) %collective-permute-start.10) | collective-permute-done | bytes 1048608 | tf_op jit(solution)/shard_map/ppermute | solution.py:12
  198.3 5.4 %collective-permute-done.11 = f32[2,128,1024]{2,1,0:T(8,128)S(1)} collective-permute-done((f32[2,128,1024]{2,1,0:T(8,128)S(1)}, f32[2,128,1024]{2,1,0:T(8,128)S(1)}, u32[]{:S(2)}, u32[]{:S(2)}) %collective-permute-start.11) | collective-permute-done | bytes 1048608 | tf_op jit(solution)/shard_map/ppermute | solution.py:12
  219.4 100.3 %all-reduce.4.cloned.1.call-done = (f32[512,512]{0,1:T(8,128)}, f32[512,512]{0,1:T(8,128)}, f32[512,512]{0,1:T(8,128)}, f32[512,512]{1,0:T(8,128)}) async-done(((f32[512,512]{0,1:T(8,128)}, f32[512,512]{0,1:T(8,128)}, f32[512,512]{0,1:T(8,128)}, f32[512,512]{1,0:T(8,128)}), (f32[512,512]{0,1:T(8,128)}, f32[512,512]{0,1:T(8,128)}, f32[512,512]{0,1:T(8,128)}, ...) | async-done | bytes 4194320 | tf_op jit(solution)/shard_map/psum | solution.py:147
  (111 shorter events, 74.7 us)
Async XLA Ops:
  7.2 7.3 %copy-start = (bf16[512,512]{1,0:T(8,128)(2,1)S(1)}, bf16[512,512]{1,0:T(8,128)(2,1)}, u32[]{:S(2)}) copy-start(bf16[512,512]{1,0:T(8,128)(2,1)} %param.12) | copy-start | bytes 1572868
  7.2 17.2 %copy-start.15 = (bf16[2,512,512]{2,1,0:T(8,128)(2,1)S(1)}, bf16[2,512,512]{2,1,0:T(8,128)(2,1)}, u32[]{:S(2)}) copy-start(bf16[2,512,512]{2,1,0:T(8,128)(2,1)} %param.8) | copy-start | bytes 3145732
  7.2 312.5 %all-reduce.4.cloned.1.call-start = ((), (), s32[]{:S(2)}) async-start(), calls=%async_computation | async-start | bytes 8388608 | tf_op jit(solution)/shard_map/psum | solution.py:147
  7.2 19.9 %collective-permute-start.2 = (s32[1,4]{1,0:T(1,128)}, s32[1,4]{1,0:T(1,128)S(1)}, u32[]{:S(2)}, u32[]{:S(2)}) collective-permute-start(s32[1,4]{1,0:T(1,128)} %param.13), channel_id=1, source_target_pairs={{0,2},{1,3},{2,0},{3,1},{4,6},{5,7},{6,4},{7,5},{8,10},{9,11},{10,... | collective-permute-start | bytes 56 | tf_op jit(solution)/shard_map/ppermute | solution.py:12
  10.3 18.1 %collective-permute-start = (s32[1,4]{1,0:T(1,128)}, s32[1,4]{1,0:T(1,128)S(1)}, u32[]{:S(2)}, u32[]{:S(2)}) collective-permute-start(s32[1,4]{1,0:T(1,128)} %param.13), channel_id=1, source_target_pairs={{0,1},{1,0},{2,3},{3,2},{4,5},{5,4},{6,7},{7,6},{8,9},{9,8},{10,11... | collective-permute-start | bytes 56 | tf_op jit(solution)/shard_map/ppermute | solution.py:12
  10.3 18.1 %collective-permute-start.6 = (s32[1,4]{1,0:T(1,128)}, s32[1,4]{1,0:T(1,128)S(1)}, u32[]{:S(2)}, u32[]{:S(2)}) collective-permute-start(s32[1,4]{1,0:T(1,128)} %param.13), channel_id=1, source_target_pairs={{0,8},{1,9},{2,10},{3,11},{4,12},{5,13},{6,14},{7,15},{8,0},{9,1},... | collective-permute-start | bytes 56 | tf_op jit(solution)/shard_map/ppermute | solution.py:12
  12.9 16.8 %collective-permute-start.4 = (s32[1,4]{1,0:T(1,128)}, s32[1,4]{1,0:T(1,128)S(1)}, u32[]{:S(2)}, u32[]{:S(2)}) collective-permute-start(s32[1,4]{1,0:T(1,128)} %param.13), channel_id=1, source_target_pairs={{0,4},{1,5},{2,6},{3,7},{4,0},{5,1},{6,2},{7,3},{8,12},{9,13},{10,... | collective-permute-start | bytes 56 | tf_op jit(solution)/shard_map/ppermute | solution.py:12
  30.9 17.7 %copy-start.6 = (bf16[2,1024,1024]{2,1,0:T(8,128)(2,1)S(1)}, bf16[2,1024,1024]{2,1,0:T(8,128)(2,1)}, u32[]{:S(2)}) copy-start(bf16[2,1024,1024]{2,1,0:T(8,128)(2,1)} %constant_dynamic-update-slice_fusion.6) | copy-start | bytes 12582916
  31.0 14.7 %collective-permute-start.7 = (bf16[2,128,512]{2,1,0:T(8,128)(2,1)S(1)}, bf16[2,128,512]{2,1,0:T(8,128)(2,1)S(1)}, u32[]{:S(2)}, u32[]{:S(2)}) collective-permute-start(bf16[2,128,512]{2,1,0:T(8,128)(2,1)S(1)} %get-tuple-element.34), channel_id=1, source_target_pairs={{0,8},{1,9},{2,10},{3,11},{4,12},{5,13},{6,14},{7,15},{8,0},{9,1},... | collective-permute-start | bytes 786440 | tf_op jit(solution)/shard_map/ppermute | solution.py:12
  33.9 13.3 %collective-permute-start.5 = (bf16[2,128,512]{2,1,0:T(8,128)(2,1)S(1)}, bf16[2,128,512]{2,1,0:T(8,128)(2,1)S(1)}, u32[]{:S(2)}, u32[]{:S(2)}) collective-permute-start(bf16[2,128,512]{2,1,0:T(8,128)(2,1)S(1)} %get-tuple-element.35), channel_id=1, source_target_pairs={{0,4},{1,5},{2,6},{3,7},{4,0},{5,1},{6,2},{7,3},{8,12},{9,13},{10,... | collective-permute-start | bytes 786440 | tf_op jit(solution)/shard_map/ppermute | solution.py:12
  34.4 13.3 %collective-permute-start.3 = (bf16[2,128,512]{2,1,0:T(8,128)(2,1)S(1)}, bf16[2,128,512]{2,1,0:T(8,128)(2,1)S(1)}, u32[]{:S(2)}, u32[]{:S(2)}) collective-permute-start(bf16[2,128,512]{2,1,0:T(8,128)(2,1)S(1)} %get-tuple-element.36), channel_id=1, source_target_pairs={{0,2},{1,3},{2,0},{3,1},{4,6},{5,7},{6,4},{7,5},{8,10},{9,11},{10,... | collective-permute-start | bytes 786440 | tf_op jit(solution)/shard_map/ppermute | solution.py:12
  34.4 13.7 %collective-permute-start.1 = (bf16[2,128,512]{2,1,0:T(8,128)(2,1)S(1)}, bf16[2,128,512]{2,1,0:T(8,128)(2,1)S(1)}, u32[]{:S(2)}, u32[]{:S(2)}) collective-permute-start(bf16[2,128,512]{2,1,0:T(8,128)(2,1)S(1)} %get-tuple-element.37), channel_id=1, source_target_pairs={{0,1},{1,0},{2,3},{3,2},{4,5},{5,4},{6,7},{7,6},{8,9},{9,8},{10,11... | collective-permute-start | bytes 786440 | tf_op jit(solution)/shard_map/ppermute | solution.py:12
  64.1 7.1 %copy-start.9 = (bf16[512,512]{0,1:T(8,128)(2,1)S(1)}, bf16[512,512]{0,1:T(8,128)(2,1)}, u32[]{:S(2)}) copy-start(bf16[512,512]{0,1:T(8,128)(2,1)} %convolution_convert_fusion.3) | copy-start | bytes 1572868
  124.0 11.0 %copy-start.10 = (bf16[512,512]{0,1:T(8,128)(2,1)S(1)}, bf16[512,512]{0,1:T(8,128)(2,1)}, u32[]{:S(2)}) copy-start(bf16[512,512]{0,1:T(8,128)(2,1)} %get-tuple-element.32) | copy-start | bytes 1572868
  144.0 10.4 %copy-start.2 = (f32[1,1024,512]{2,1,0:T(8,128)S(1)}, f32[1,1024,512]{2,1,0:T(8,128)}, u32[]{:S(2)}) copy-start(f32[1,1024,512]{2,1,0:T(8,128)} %copy.28) | copy-start | bytes 6291460
  144.0 10.4 %copy-start.3 = (f32[1,1024,512]{2,1,0:T(8,128)S(1)}, f32[1,1024,512]{2,1,0:T(8,128)}, u32[]{:S(2)}) copy-start(f32[1,1024,512]{2,1,0:T(8,128)} %copy.29) | copy-start | bytes 6291460
  144.0 10.4 %copy-start.4 = (f32[1,1024,512]{2,1,0:T(8,128)S(1)}, f32[1,1024,512]{2,1,0:T(8,128)}, u32[]{:S(2)}) copy-start(f32[1,1024,512]{2,1,0:T(8,128)} %copy.26) | copy-start | bytes 6291460
  144.0 10.4 %copy-start.5 = (f32[1,1024,512]{2,1,0:T(8,128)S(1)}, f32[1,1024,512]{2,1,0:T(8,128)}, u32[]{:S(2)}) copy-start(f32[1,1024,512]{2,1,0:T(8,128)} %copy.27) | copy-start | bytes 6291460
  146.9 14.1 %collective-permute-start.8 = (f32[2,128,1024]{2,1,0:T(8,128)S(1)}, f32[2,128,1024]{2,1,0:T(8,128)}, u32[]{:S(2)}, u32[]{:S(2)}) collective-permute-start(f32[2,128,1024]{2,1,0:T(8,128)S(1)} %get-tuple-element.25), channel_id=1, source_target_pairs={{0,1},{1,0},{2,3},{3,2},{4,5},{5,4},{6,7},{7,6},{8,9},{9,8},{10,11... | collective-permute-start | bytes 3145736 | tf_op jit(solution)/shard_map/ppermute | solution.py:12
  153.8 44.4 %collective-permute-start.10 = (f32[2,128,1024]{2,1,0:T(8,128)S(1)}, f32[2,128,1024]{2,1,0:T(8,128)S(1)}, u32[]{:S(2)}, u32[]{:S(2)}) collective-permute-start(f32[2,128,1024]{2,1,0:T(8,128)S(1)} %get-tuple-element.23), channel_id=1, source_target_pairs={{0,4},{1,5},{2,6},{3,7},{4,0},{5,1},{6,2},{7,3},{8,12},{9,13},{10,... | collective-permute-start | bytes 3145736 | tf_op jit(solution)/shard_map/ppermute | solution.py:12
  153.8 24.8 %collective-permute-start.9 = (f32[2,128,1024]{2,1,0:T(8,128)S(1)}, f32[2,128,1024]{2,1,0:T(8,128)S(1)}, u32[]{:S(2)}, u32[]{:S(2)}) collective-permute-start(f32[2,128,1024]{2,1,0:T(8,128)S(1)} %get-tuple-element.24), channel_id=1, source_target_pairs={{0,2},{1,3},{2,0},{3,1},{4,6},{5,7},{6,4},{7,5},{8,10},{9,11},{10,... | collective-permute-start | bytes 3145736 | tf_op jit(solution)/shard_map/ppermute | solution.py:12
  155.4 3.9 %copy-start.14 = (bf16[8,64,512]{2,1,0:T(8,128)(2,1)S(1)}, bf16[8,64,512]{2,1,0:T(8,128)(2,1)}, u32[]{:S(2)}) copy-start(bf16[8,64,512]{2,1,0:T(8,128)(2,1)} %convolution_convert_fusion.2) | copy-start | bytes 1572868
  155.7 48.0 %collective-permute-start.11 = (f32[2,128,1024]{2,1,0:T(8,128)S(1)}, f32[2,128,1024]{2,1,0:T(8,128)S(1)}, u32[]{:S(2)}, u32[]{:S(2)}) collective-permute-start(f32[2,128,1024]{2,1,0:T(8,128)S(1)} %get-tuple-element.22), channel_id=1, source_target_pairs={{0,8},{1,9},{2,10},{3,11},{4,12},{5,13},{6,14},{7,15},{8,0},{9,1},... | collective-permute-start | bytes 3145736 | tf_op jit(solution)/shard_map/ppermute | solution.py:12
  210.9 6.2 %copy-start.13 = (bf16[2,512,1024]{2,1,0:T(8,128)(2,1)S(1)}, bf16[2,512,1024]{2,1,0:T(8,128)(2,1)}, u32[]{:S(2)}) copy-start(bf16[2,512,1024]{2,1,0:T(8,128)(2,1)} %copy-done.12) | copy-start | bytes 6291460
  (9 other events, 24.3 us)
Sparse Core Ops, SparseCore 0:
  208.5 111.1 all-reduce.3
where the time goes:
time: 342 us; the launch traced here: 337 us
  waiting for transfers between devices  154 us (45%)
  matrix products  84.8 us (25%)
  local copies, waits for them, and re-layouts  48.6 us (14%)
  other arithmetic  22.2 us (6%)
  between operations  17 us (5%)
  starting transfers between devices  10.7 us (3%)
    psum x1, waiting for transfers between devices, per_device(): lax.psum((grad_query, grad_pair[:, :model_width], grad_pair[:, model_widt...  100 us
    ppermute x12, waiting for transfers between devices, partner(): lax.ppermute(x, axis, [(i, i ^ 1 << stride) for i in range(lax.axis_size(...  53.3 us
    sub x2, matrix products, attend(): expo_terms = jnp.exp(scores - row_max)  18.7 us
    unnamed x49, local copies, waits for them, and re-layouts  17.2 us
    dot_general x2, matrix products, attend(): jnp.einsum('sqhd,skhd->shqk', grad_context, value_heads, preferred_elemen...  15.3 us
    convert_element_type x2, other arithmetic, attend(): prob_half = probability.astype(jnp.bfloat16)  14 us
    ppermute x12, starting transfers between devices, partner(): lax.ppermute(x, axis, [(i, i ^ 1 << stride) for i in range(lax.axis_size(...  10.7 us
    dot_general x2, matrix products, attend(): jnp.einsum('shqk,skhd->sqhd', grad_score, key_heads, preferred_element_ty...  10.3 us
  transfers between devices with their start and end apart: 13, of which 6 were waited for; matrix products, arithmetic and copies ran while one was open for 12% of the time, Pallas kernels for 0%

commit v1 on v0

v1 whole, which is shorter than its diff:
```python
import functools

import jax
import jax.numpy as jnp
from jax import lax
from jax.experimental import pallas as pl
from jax.experimental.pallas import tpu as pltpu
from jax.sharding import PartitionSpec as P

SUB = 128
GROUPS = 1
VMEM = 48 * 1024 * 1024
F32 = jnp.float32
BF16 = jnp.bfloat16
OFF = 1e30


def partner(x, stride):
    return lax.ppermute(x, "tok", [(i, i ^ 1 << stride) for i in range(lax.axis_size("tok"))])


def nn(a, b):
    return lax.dot_general(a, b, (((1,), (0,)), ((), ())), preferred_element_type=F32)


def nt(a, b):
    return lax.dot_general(a, b, (((1,), (1,)), ((), ())), preferred_element_type=F32)


def tn(a, b):
    return lax.dot_general(a, b, (((0,), (0,)), ((), ())), preferred_element_type=F32)


def tt(a, b):
    return lax.dot_general(a, b, (((0,), (1,)), ((), ())), preferred_element_type=F32)


def params(*semantics):
    return pltpu.CompilerParams(vmem_limit_bytes=VMEM, dimension_semantics=semantics or None)


def head_rows(pair_rows, which, head_width):
    row = lax.broadcasted_iota(jnp.int32, pair_rows.shape, 0)
    keep = (row >= which * head_width) & (row < (which + 1) * head_width)
    return jnp.where(keep, pair_rows, jnp.zeros_like(pair_rows))


def project_kernel(scale, x_ref, c_ref, wq_ref, wk_ref, wv_ref, wo_ref, qt_ref, k_ref, v_ref, kt_ref, vt_ref, dot_ref):
    x = x_ref[0]
    qt_ref[0] = (tt(wq_ref[...], x).astype(BF16).astype(F32) * scale).astype(BF16)
    k = nn(x, wk_ref[...])
    v = nn(x, wv_ref[...])
    k_ref[0] = k.astype(BF16)
    v_ref[0] = v.astype(BF16)
    kt_ref[0] = k.T.astype(BF16)
    vt_ref[0] = v.T.astype(BF16)
    dot_ref[0] = nt(wo_ref[...], c_ref[0]).astype(BF16)


def project(tokens, cotangent, w_query, w_key, w_value, w_out, scale):
    samples, rows, width = tokens.shape
    row_block = pl.BlockSpec((1, rows, width), lambda s: (s, 0, 0))
    col_block = pl.BlockSpec((1, width, rows), lambda s: (s, 0, 0))
    whole = pl.BlockSpec((width, width), lambda s: (0, 0))
    by_row = jax.ShapeDtypeStruct((samples, rows, width), BF16)
    by_col = jax.ShapeDtypeStruct((samples, width, rows), BF16)
    return pl.pallas_call(
        functools.partial(project_kernel, scale),
        grid=(samples,),
        in_specs=[row_block, row_block] + [whole] * 4,
        out_specs=[col_block, row_block, row_block, col_block, col_block, col_block],
        out_shape=[by_col, by_row, by_row, by_col, by_col, by_col],
        compiler_params=params("arbitrary"),
    )(tokens, cotangent, w_query, w_key, w_value, w_out)


def project_partner_kernel(x0, x1, x2, x3, wk_ref, wv_ref, k_ref, v_ref, kt_ref, vt_ref):
    x = jnp.concatenate([x0[0], x1[0], x2[0], x3[0]], 0)
    k = nn(x, wk_ref[...])
    v = nn(x, wv_ref[...])
    k_ref[0] = k.astype(BF16)
    v_ref[0] = v.astype(BF16)
    kt_ref[0] = k.T.astype(BF16)
    vt_ref[0] = v.T.astype(BF16)


def project_partner(arrived, w_key, w_value):
    samples, sub_rows, width = arrived[0].shape
    rows = sub_rows * len(arrived)
    part = pl.BlockSpec((1, sub_rows, width), lambda s: (s, 0, 0))
    row_block = pl.BlockSpec((1, rows, width), lambda s: (s, 0, 0))
    col_block = pl.BlockSpec((1, width, rows), lambda s: (s, 0, 0))
    whole = pl.BlockSpec((width, width), lambda s: (0, 0))
    by_row = jax.ShapeDtypeStruct((samples, rows, width), BF16)
    by_col = jax.ShapeDtypeStruct((samples, width, rows), BF16)
    return pl.pallas_call(
        project_partner_kernel,
        grid=(samples,),
        in_specs=[part] * 4 + [whole] * 2,
        out_specs=[row_block, row_block, col_block, col_block],
        out_shape=[by_row, by_row, by_col, by_col],
        compiler_params=params("arbitrary"),
    )(*arrived, w_key, w_value)


def own_kernel(head_width, qt_ref, k_ref, vt_ref, e_ref, o_ref, st_ref):
    k = k_ref[0]
    for which in range(2):
        s = nn(k, head_rows(qt_ref[0], which, head_width))
        top = jnp.max(s, axis=0, keepdims=True)
        e = jnp.exp(s - top)
        total = jnp.sum(e, axis=0, keepdims=True)
        e = e.astype(BF16)
        e_ref[0, which] = e
        o_ref[0, which] = nn(vt_ref[0, which * head_width : (which + 1) * head_width, :], e)
        st_ref[0, which] = jnp.concatenate([top, total, jnp.zeros((6, top.shape[1]), F32)], 0)


def own_part(qt, k, vt, head_count):
    samples, width, rows = qt.shape
    head_width = width // head_count
    col_pair = pl.BlockSpec((1, 2 * head_width, rows), lambda p, s: (s, p, 0))
    row_pair = pl.BlockSpec((1, rows, 2 * head_width), lambda p, s: (s, 0, p))

    def per_head(n):
        return pl.BlockSpec((1, 2, n, rows), lambda p, s: (s, p, 0, 0))

    return pl.pallas_call(
        functools.partial(own_kernel, head_width),
        grid=(head_count // 2, samples),
        in_specs=[col_pair, row_pair, col_pair],
        out_specs=[per_head(rows), per_head(head_width), per_head(8)],
        out_shape=[
            jax.ShapeDtypeStruct((samples, head_count, rows, rows), BF16),
            jax.ShapeDtypeStruct((samples, head_count, head_width, rows), F32),
            jax.ShapeDtypeStruct((samples, head_count, 8, rows), F32),
        ],
        compiler_params=params("arbitrary", "arbitrary"),
    )(qt, k, vt)


def attend_kernel(
    first_pair, head_width, scale, mask_ref, e_ref, o_ref, st_ref, qt_ref, dot_ref, ko_ref, vo_ref, kto_ref, kp_ref, vp_ref, ktp_ref,
    vtp_ref, ctx_ref, dqt_ref, dko_ref, dvo_ref, dkp_ref, dvp_ref,
):
    pair = first_pair + pl.program_id(0)
    sections = mask_ref.shape[0]
    sub = kp_ref.shape[1] // sections
    ko, vo, kp, vp = ko_ref[0], vo_ref[0], kp_ref[0], vp_ref[0]
    dko = dvo = dkp = dvp = None
    for which in range(2):
        rows = slice(which * head_width, (which + 1) * head_width)
        q_half = head_rows(qt_ref[0], which, head_width)
        s = nn(kp, q_half)
        top_own = st_ref[0, which, 0:1, :]
        total_own = st_ref[0, which, 1:2, :]
        offs = [jnp.where(mask_ref[i, 2 * pair + which] > 0, 0.0, OFF).astype(F32) for i in range(sections)]
        top = top_own
        for i in range(sections):
            top = jnp.maximum(top, jnp.max(s[i * sub : (i + 1) * sub], axis=0, keepdims=True) - offs[i])
        e_part = jnp.concatenate([jnp.exp(s[i * sub : (i + 1) * sub] - (top + offs[i])) for i in range(sections)], 0)
        fade = jnp.exp(top_own - top)
        total = fade * total_own + jnp.sum(e_part, axis=0, keepdims=True)
        e_part = e_part.astype(BF16)
        e_own = e_ref[0, which]
        inverse = 1.0 / total
        o = fade * o_ref[0, which] + nn(vtp_ref[0, rows, :], e_part)
        ctx = (o * inverse).astype(BF16)
        ctx_ref[0, rows, :] = ctx
        ctx = ctx.astype(F32)
        g = dot_ref[0, rows, :].astype(F32)
        g_part = (g * inverse).astype(BF16)
        g_own = (g * (inverse * fade)).astype(BF16)
        r_part = jnp.sum(g_part.astype(F32) * ctx, axis=0, keepdims=True)
        r_own = jnp.sum(g_own.astype(F32) * ctx, axis=0, keepdims=True)
        blank = jnp.zeros_like(g_part)
        g_part = jnp.concatenate([g_part, blank] if which == 0 else [blank, g_part], 0)
        g_own = jnp.concatenate([g_own, blank] if which == 0 else [blank, g_own], 0)
        ds_part = ((nn(vp, g_part) - r_part).astype(BF16) * e_part)
        ds_own = ((nn(vo, g_own) - r_own).astype(BF16) * e_own)
        dqt_ref[0, rows, :] = ((nn(kto_ref[0, rows, :], ds_own) + nn(ktp_ref[0, rows, :], ds_part)) * scale).astype(BF16)
        terms = (nt(ds_own, q_half), nt(e_own, g_own), nt(ds_part, q_half), nt(e_part, g_part))
        if which == 0:
            dko, dvo, dkp, dvp = terms
        else:
            dko, dvo, dkp, dvp = dko + terms[0], dvo + terms[1], dkp + terms[2], dvp + terms[3]
    dko_ref[0] = dko.astype(BF16)
    dvo_ref[0] = dvo.astype(BF16)
    dkp_ref[0] = dkp.astype(BF16)
    dvp_ref[0] = dvp.astype(BF16)


def attend(group, groups, head_masks, own, qt, dot, ko, vo, kto, partner_rows, head_count, scale):
    e, o, st = own
    kp, vp, ktp, vtp = partner_rows
    samples, width, rows = qt.shape
    head_width = width // head_count
    pairs = head_count // 2 // groups
    first = group * pairs
    col_in = pl.BlockSpec((1, 2 * head_width, rows), lambda p, s: (s, first + p, 0))
    row_in = pl.BlockSpec((1, rows, 2 * head_width), lambda p, s: (s, 0, first + p))
    col_out = pl.BlockSpec((1, 2 * head_width, rows), lambda p, s: (s, p, 0))
    row_out = pl.BlockSpec((1, rows, 2 * head_width), lambda p, s: (s, 0, p))

    def per_head(n):
        return pl.BlockSpec((1, 2, n, rows), lambda p, s: (s, first + p, 0, 0))

    by_col = jax.ShapeDtypeStruct((samples, width // groups, rows), BF16)
    by_row = jax.ShapeDtypeStruct((samples, rows, width // groups), BF16)
    return pl.pallas_call(
        functools.partial(attend_kernel, first, head_width, scale),
        grid=(pairs, samples),
        in_specs=[pl.BlockSpec(memory_space=pltpu.SMEM), per_head(rows), per_head(head_width), per_head(8)]
        + [col_in, col_in, row_in, row_in, col_in, row_in, row_in, col_in, col_in],
        out_specs=[col_out, col_out] + [row_out] * 4,
        out_shape=[by_col, by_col] + [by_row] * 4,
        compiler_params=params("arbitrary", "arbitrary"),
    )(head_masks, e, o, st, qt, dot, ko, vo, kto, kp, vp, ktp, vtp)


def weights_kernel(place_ref, x_ref, x0, x1, x2, x3, c_ref, ctx_ref, dqt_ref, dko_ref, dvo_ref, dkp_ref, dvp_ref, keep_ref, send_ref, all_ref):
    samples, rows, width = x_ref.shape
    cols = dko_ref.shape[2]
    chunk = keep_ref.shape[1]
    chunks = 2 * keep_ref.shape[0]
    per_type = chunks // 4

    def put(kind, value):
        for i in range(per_type):
            all_ref[(kind * per_type + i) ^ place_ref[0]] = value[i * chunk : (i + 1) * chunk].astype(BF16)

    own = samples * rows
    x_all = jnp.concatenate([x_ref[s] for s in range(samples)] + [x[s] for s in range(samples) for x in (x0, x1, x2, x3)], 0)
    xt = x_all.T
    ctx = jnp.concatenate([ctx_ref[s] for s in range(samples)], 1)
    go = nn(ctx, c_ref[...].reshape(own, width))
    put(3, jnp.concatenate([go[:, i : i + cols] for i in range(0, width, cols)], 0))
    dqt = jnp.concatenate([dqt_ref[s] for s in range(samples)], 1)
    put(0, nt(xt[:, :own], dqt))
    dk = jnp.concatenate([dko_ref[s] for s in range(samples)] + [dkp_ref[s] for s in range(samples)], 0)
    put(1, nn(xt, dk))
    dv = jnp.concatenate([dvo_ref[s] for s in range(samples)] + [dvp_ref[s] for s in range(samples)], 0)
    put(2, nn(xt, dv))
    keep_ref[...] = all_ref[: chunks // 2]
    send_ref[...] = all_ref[chunks // 2 :]


def weight_grads(place, devices, tokens, arrived, cotangent, parts):
    width = tokens.shape[2]
    cols = parts[0].shape[1]
    half = jax.ShapeDtypeStruct((devices // 2, 4 * width // devices, cols), BF16)
    whole = pl.BlockSpec(memory_space=pltpu.VMEM)
    return pl.pallas_call(
        weights_kernel,
        in_specs=[pl.BlockSpec(memory_space=pltpu.SMEM)] + [whole] * 12,
        out_shape=[half, half],
        scratch_shapes=[pltpu.VMEM((devices, 4 * width // devices, cols), BF16)],
        compiler_params=params(),
    )(place, tokens, *arrived, cotangent, *parts)


def plan_of(levels):
    return [[0], [1]] + [list(range(low, min(low + 2, levels))) for low in range(2, levels, 2)]


def spread(number, bits):
    return sum((number >> at & 1) << bit for at, bit in enumerate(bits))


def place_of(plan):
    index = lax.axis_index("tok")
    place = jnp.int32(0)
    for bits in plan:
        digit = sum((index >> bit & 1) << at for at, bit in enumerate(bits))
        place = (place << len(bits)) + digit
    return place.reshape(1)


def exchange(x, mask):
    return lax.ppermute(x, "tok", [(i, i ^ mask) for i in range(lax.axis_size("tok"))])


def reduce_all(plan, keep, send):
    sends = [send]
    kept = keep
    for number, bits in enumerate(plan):
        came = [exchange(piece, spread(m + 1, bits)) for m, piece in enumerate(sends)]
        total = kept.astype(F32)
        for piece in came:
            total = total + piece.astype(F32)
        if number + 1 < len(plan):
            share = total.shape[0] >> len(plan[number + 1])
            parts = [total[i : i + share].astype(BF16) for i in range(0, total.shape[0], share)]
            kept, sends = parts[0], parts[1:]
        else:
            kept = total.astype(BF16)
    pieces = [kept]
    for bits in reversed(plan):
        mine = pieces[0] if len(pieces) == 1 else jnp.concatenate(pieces, 0)
        pieces = [mine] + [exchange(mine, spread(m, bits)) for m in range(1, 1 << len(bits))]
    return pieces


def spread_kernel(groups, count, place_ref, *refs):
    piece_refs, out_refs, all_ref = refs[: groups * count], refs[groups * count : -1], refs[-1]
    kinds, per_type, chunk, width = 4, all_ref.shape[0] // 4, all_ref.shape[1], all_ref.shape[2]
    cols = width // groups
    for g in range(groups):
        slot = 0
        for ref in piece_refs[g * count : (g + 1) * count]:
            for i in range(ref.shape[0]):
                all_ref[slot ^ place_ref[0], :, g * cols : (g + 1) * cols] = ref[i].astype(F32)
                slot += 1
    for kind in range(3):
        out_refs[kind][...] = all_ref[kind * per_type : (kind + 1) * per_type].reshape(width, width)
    last = all_ref[3 * per_type :].reshape(groups, cols, width)
    for g in range(groups):
        for i in range(groups):
            out_refs[3][g * cols : (g + 1) * cols, i * cols : (i + 1) * cols] = last[i, :, g * cols : (g + 1) * cols]


def spread_grads(place, devices, width, pieces):
    groups, count = len(pieces), len(pieces[0])
    whole = pl.BlockSpec(memory_space=pltpu.VMEM)
    return pl.pallas_call(
        functools.partial(spread_kernel, groups, count),
        in_specs=[pl.BlockSpec(memory_space=pltpu.SMEM)] + [whole] * (groups * count),
        out_shape=[jax.ShapeDtypeStruct((width, width), F32)] * 4,
        scratch_shapes=[pltpu.VMEM((devices, 4 * width // devices, width), F32)],
        compiler_params=params(),
    )(place, *[piece for group in pieces for piece in group])


def back_kernel(groups, *refs):
    dks, dvs = refs[:groups], refs[groups : 2 * groups]
    wk_ref, wv_ref, *outs = refs[2 * groups :]
    dk = jnp.concatenate([r[0] for r in dks], 1)
    dv = jnp.concatenate([r[0] for r in dvs], 1)
    total = (nt(dk, wk_ref[...]) + nt(dv, wv_ref[...])).astype(BF16)
    sub = outs[0].shape[1]
    for i, out in enumerate(outs):
        out[0] = total[i * sub : (i + 1) * sub]


def back(dkps, dvps, w_key, w_value):
    groups = len(dkps)
    samples, rows, cols = dkps[0].shape
    width = w_key.shape[0]
    part = pl.BlockSpec((1, rows, cols), lambda s: (s, 0, 0))
    whole = pl.BlockSpec((width, width), lambda s: (0, 0))
    return pl.pallas_call(
        functools.partial(back_kernel, groups),
        grid=(samples,),
        in_specs=[part] * (2 * groups) + [whole] * 2,
        out_specs=[pl.BlockSpec((1, rows // 4, width), lambda s: (s, 0, 0))] * 4,
        out_shape=[jax.ShapeDtypeStruct((samples, rows // 4, width), BF16)] * 4,
        compiler_params=params("arbitrary"),
    )(*dkps, *dvps, w_key, w_value)


def finish_kernel(groups, *refs):
    ctxs, dqts, dks, dvs = (refs[i * groups : (i + 1) * groups] for i in range(4))
    wo_ref, wq_ref, wk_ref, wv_ref, out_ref, gt_ref = refs[4 * groups :]
    ctx = jnp.concatenate([r[0] for r in ctxs], 0)
    out_ref[0] = tn(ctx, wo_ref[...]).astype(BF16)
    dqt = jnp.concatenate([r[0] for r in dqts], 0)
    dk = jnp.concatenate([r[0] for r in dks], 1)
    dv = jnp.concatenate([r[0] for r in dvs], 1)
    gt_ref[0] = tt(dqt, wq_ref[...]) + nt(dk, wk_ref[...]) + nt(dv, wv_ref[...])


def finish(ctxs, dqts, dks, dvs, w_out, w_query, w_key, w_value):
    groups = len(ctxs)
    samples, cols, rows = ctxs[0].shape
    width = w_out.shape[0]
    part = pl.BlockSpec((1, cols, rows), lambda s: (s, 0, 0))
    row_part = pl.BlockSpec((1, rows, cols), lambda s: (s, 0, 0))
    whole = pl.BlockSpec((width, width), lambda s: (0, 0))
    row_block = pl.BlockSpec((1, rows, width), lambda s: (s, 0, 0))
    return pl.pallas_call(
        functools.partial(finish_kernel, groups),
        grid=(samples,),
        in_specs=[part] * (2 * groups) + [row_part] * (2 * groups) + [whole] * 4,
        out_specs=[row_block, row_block],
        out_shape=[jax.ShapeDtypeStruct((samples, rows, width), BF16), jax.ShapeDtypeStruct((samples, rows, width), F32)],
        compiler_params=params("arbitrary"),
    )(*ctxs, *dqts, *dks, *dvs, w_out, w_query, w_key, w_value)


def token_kernel(start_ref, gt_ref, b0, b1, b2, b3, out_ref, acc_ref):
    sub = b0.shape[1]
    acc_ref[...] = gt_ref[0]
    for section, came in enumerate((b0, b1, b2, b3)):
        acc_ref[pl.ds(pl.multiple_of(start_ref[section] * sub, sub), sub), :] += came[0].astype(F32)
    out_ref[0] = acc_ref[...].astype(BF16)


def token_grads(starts, partial, backs):
    samples, rows, width = partial.shape
    row_block = pl.BlockSpec((1, rows, width), lambda s: (s, 0, 0))
    came = pl.BlockSpec((1,) + backs[0].shape[1:], lambda s: (s, 0, 0))
    return pl.pallas_call(
        token_kernel,
        grid=(samples,),
        in_specs=[pl.BlockSpec(memory_space=pltpu.SMEM), row_block] + [came] * 4,
        out_specs=row_block,
        out_shape=jax.ShapeDtypeStruct((samples, rows, width), BF16),
        scratch_shapes=[pltpu.VMEM((rows, width), F32)],
        compiler_params=params("arbitrary"),
    )(starts, partial, *backs)


def per_device(tokens, w_query, w_key, w_value, w_out, partner_block, head_masks, cotangent):
    samples, rows, width = tokens.shape
    head_count = head_masks.shape[2]
    devices = lax.axis_size("tok")
    levels = devices.bit_length() - 1
    plan = plan_of(levels)
    place = place_of(plan)
    scale = (width // head_count) ** -0.5
    theirs = [partner(partner_block, levels - 4 + section)[0, section] for section in range(4)]
    qt, ko, vo, kto, vto, dot = project(tokens, cotangent, w_query, w_key, w_value, w_out, scale)
    arrived = [
        partner(lax.dynamic_slice_in_dim(tokens, theirs[section] * SUB, SUB, 1), levels - 4 + section) for section in range(4)
    ]
    own = own_part(qt, ko, vto, head_count)
    partner_rows = project_partner(arrived, w_key, w_value)
    done, sums = [], []
    for group in range(GROUPS):
        parts = attend(group, GROUPS, head_masks[0], own, qt, dot, ko, vo, kto, partner_rows, head_count, scale)
        done.append(parts)
        sums.append(reduce_all(plan, *weight_grads(place, devices, tokens, arrived, cotangent, parts)))
    ctxs, dqts, dkos, dvos, dkps, dvps = zip(*done)
    backs = [partner(piece, levels - 4 + i) for i, piece in enumerate(back(dkps, dvps, w_key, w_value))]
    output, partial = finish(ctxs, dqts, dkos, dvos, w_out, w_query, w_key, w_value)
    grad_tokens = token_grads(jnp.stack(theirs), partial, backs)
    return (output, grad_tokens, *spread_grads(place, devices, width, sums))


def solution(mesh):
    rows = P("groups", "tok", None)
    placed = (rows, P(), P(), P(), P(), P("tok", None), P("tok", None, None), rows)
    grads = P("groups", None)
    return jax.shard_map(
        per_device, mesh=mesh, in_specs=placed, out_specs=(rows, rows, grads, grads, grads, grads), check_vma=False
    )
```

time: 342 us -> 164 us (0.48); the launches traced: 337 us -> 164 us
  waiting for transfers between devices: 154 us -> 51.9 us
  matrix products: 84.8 us -> 0 us
  Pallas kernels: 0 us -> 63.2 us
  local copies, waits for them, and re-layouts: 48.6 us -> 16.8 us
  other arithmetic: 22.2 us -> 2.42 us
  starting transfers between devices: 10.7 us -> 26.9 us
  between operations: 17 us -> 2.76 us
    psum x1 -> x0, waiting for transfers between devices: 100 us -> none  [per_device(): lax.psum((grad_query, grad_pair[:, :model_width], grad_pair[:, model_widt...]
    dot_general x25 -> x0, matrix products: 66 us -> none  [the longest x2 15.3 us: attend(): jnp.einsum('sqhd,skhd->shqk', grad_context, value_heads, preferred_elemen...]
    pallas_call x0 -> x9, Pallas kernels: none -> 63.2 us  [the longest x1 28.4 us: attend(): pl.pallas_call(functools.partial(attend_kernel, first, head_width, scale)...]
    sub x2 -> x0, matrix products: 18.7 us -> none  [attend(): expo_terms = jnp.exp(scores - row_max)]
    ppermute x12 -> x22, starting transfers between devices: 10.7 us -> 26.9 us  [the longest x12 15.1 us: partner(): lax.ppermute(x, 'tok', [(i, i ^ 1 << stride) for i in range(lax.axis_size...]
    convert_element_type x3 -> x0, other arithmetic: 14.3 us -> none  [the longest x2 14 us: attend(): prob_half = probability.astype(jnp.bfloat16)]
    slice x11 -> x5, local copies, waits for them, and re-layouts: 15.8 us -> 1.8 us  [the longest x3 1.74 us: per_device(): partner(partner_block, levels - 4 + section)[0, section]]
    reshape x5 -> x0, local copies, waits for them, and re-layouts: 12.8 us -> none  [the longest x2 6.05 us: attend(): grad_k.reshape(samples, key_count, model_width)]
  transfers between devices with their start and end apart: 13 -> 22, of which waited for: 6 -> 10; matrix products, arithmetic and copies ran while one was open for 12% -> 2% of each run, Pallas kernels for 0% -> 14%
where the time goes in v1:
time: 164 us
  Pallas kernels  63.2 us (39%)
  waiting for transfers between devices  51.9 us (32%)
  starting transfers between devices  26.9 us (16%)
  local copies, waits for them, and re-layouts  16.8 us (10%)
  between operations  2.76 us (2%)
  other arithmetic  2.42 us (1%)
    ppermute x10, waiting for transfers between devices, exchange(): lax.ppermute(x, 'tok', [(i, i ^ mask) for i in range(lax.axis_size('tok'))])  45.9 us
    pallas_call x1, Pallas kernels, attend(): pl.pallas_call(functools.partial(attend_kernel, first, head_width, scale)...  28.4 us
    ppermute x12, starting transfers between devices, partner(): lax.ppermute(x, 'tok', [(i, i ^ 1 << stride) for i in range(lax.axis_size...  15.1 us
    unnamed x55, local copies, waits for them, and re-layouts  12.8 us
    ppermute x10, starting transfers between devices, exchange(): lax.ppermute(x, 'tok', [(i, i ^ mask) for i in range(lax.axis_size('tok'))])  11.7 us
    pallas_call x1, Pallas kernels, own_part(): pl.pallas_call(functools.partial(own_kernel, head_width), grid=(head_coun...  11.1 us
    pallas_call x1, Pallas kernels, weight_grads(): pl.pallas_call(weights_kernel, in_specs=[pl.BlockSpec(memory_space=pltpu....  6.35 us
    ppermute x12, waiting for transfers between devices, partner(): lax.ppermute(x, 'tok', [(i, i ^ 1 << stride) for i in range(lax.axis_size...  6.04 us
  transfers between devices with their start and end apart: 22, of which 10 were waited for; matrix products, arithmetic and copies ran while one was open for 2% of the time, Pallas kernels for 14%

profile of v1, /device:TPU:0, one launch (start us, length us, event | category | flops | bytes accessed | tf_op | source)
XLA Modules:
  0.0 164.0 jit_solution(4467195404221139419)
XLA Ops:
  0.7 3.0 %collective-permute-start.2 = (s32[1,4]{1,0:T(1,128)}, s32[1,4]{1,0:T(1,128)S(1)}, u32[]{:S(2)}, u32[]{:S(2)}) collective-permute-start(s32[1,4]{1,0:T(1,128)} %param.13), channel_id=1, source_target_pairs={{0,2},{1,3},{2,0},{3,1},{4,6},{5,7},{6,4},{7,5},{8,10},{9,11},{10,... | collective-permute-start | bytes 56 | tf_op jit(solution)/shard_map/ppermute | solution.py:19
  3.7 2.6 %collective-permute-start.6 = (s32[1,4]{1,0:T(1,128)}, s32[1,4]{1,0:T(1,128)S(1)}, u32[]{:S(2)}, u32[]{:S(2)}) collective-permute-start(s32[1,4]{1,0:T(1,128)} %param.13), channel_id=1, source_target_pairs={{0,8},{1,9},{2,10},{3,11},{4,12},{5,13},{6,14},{7,15},{8,0},{9,1},... | collective-permute-start | bytes 56 | tf_op jit(solution)/shard_map/ppermute | solution.py:19
  11.5 2.1 %constant_dynamic-slice_fusion = (bf16[2,128,512]{2,1,0:T(8,128)(2,1)}, bf16[2,128,512]{2,1,0:T(8,128)(2,1)}, bf16[2,128,512]{2,1,0:T(8,128)(2,1)}, bf16[2,128,512]{2,1,0:T(8,128)(2,1)S(1)}) fusion(bf16[2,512,512]{2,1,0:T(8,128)(2,1)} %x_ref.3, s32[]{:T(128)S(6)} %select_n.15, s32[]{:T(128)S(6)} %select_n.14, s32[]{:T(128)S(6)} %select_n.13, s32[]{:T(128)S(6)} %select_n.12), kind=kLoop, calls=%fused_computation.9 | loop fusion | bytes 2097168 | tf_op jit(solution)/shard_map/dynamic_slice | solution.py:424
  17.4 4.7 %shard_map.127 = (bf16[2,512,512]{2,1,0:T(8,128)(2,1)S(1)}, bf16[2,512,512]{2,1,0:T(8,128)(2,1)S(1)}, bf16[2,512,512]{2,1,0:T(8,128)(2,1)S(1)}, bf16[2,512,512]{...) custom-call(bf16[2,512,512]{2,1,0:T(8,128)(2,1)} %x_ref.3, bf16[2,512,512]{2,1,0:T(8,128)(2,1)} %c_ref.3, ...), custom_call_target="tpu_custom_call" | custom-call | tf_op jit(solution)/shard_map/pallas_call | solution.py:67
  22.2 2.0 %copy-done.20 = bf16[2,512,512]{2,1,0:T(8,128)(2,1)S(1)} copy-done((bf16[2,512,512]{2,1,0:T(8,128)(2,1)S(1)}, bf16[2,512,512]{2,1,0:T(8,128)(2,1)}, u32[]{:S(2)}) %copy-start.20) | copy-done | bytes 1048600
  24.2 11.1 %shard_map.128 = (bf16[2,8,512,512]{3,2,1,0:T(8,128)(2,1)}, f32[2,8,64,512]{3,2,1,0:T(8,128)S(1)}, f32[2,8,8,512]{3,2,1,0:T(8,128)S(1)}) custom-call(bf16[2,512,512]{2,1,0:T(8,128)(2,1)S(1)} %get-tuple-element.37.qt_ref, bf16[2,512,512]{2,1,0:T(8,128)(2,1)S(1)} %get-tuple-element.38.k_ref.ko_ref, bf16[2,512,512]{2,1,0:T(8,128)(2,1)S(1)} %copy-done.20), custom_call_target="tpu_custom_call" | custom-call | tf_op jit(solution)/shard_map/pallas_call | solution.py:128
  36.6 2.4 %shard_map.129 = (bf16[2,512,512]{2,1,0:T(8,128)(2,1)S(1)}, bf16[2,512,512]{2,1,0:T(8,128)(2,1)S(1)}, bf16[2,512,512]{2,1,0:T(8,128)(2,1)S(1)}, bf16[2,512,512]{2,1,0:T(8,128)(2,1)}) custom-call(bf16[2,128,512]{2,1,0:T(8,128)(2,1)S(1)} %collective-permute-done.1.x0, bf16[2,128,512]{2,1,0:T(8,128)(2,1)S(1)} %collective-permute-done.3.x1, ...), custom_call_target="tpu_custom_call" | custom-call | tf_op jit(solution)/shard_map/pallas_call | solution.py:96
  42.0 28.4 %shard_map.130 = (bf16[2,512,512]{2,1,0:T(8,128)(2,1)S(1)}, bf16[2,512,512]{2,1,0:T(8,128)(2,1)S(1)}, bf16[2,512,512]{2,1,0:T(8,128)(2,1)S(1)}, bf16[2,512,512]{...) custom-call(s32[4,8]{1,0:T(4,128)S(1)} %bitcast.11, ...), custom_call_target="tpu_custom_call" | custom-call | tf_op jit(solution)/shard_map/pallas_call | solution.py:210
  75.3 6.4 %shard_map.134 = (bf16[8,128,512]{2,1,0:T(8,128)(2,1)S(1)}, bf16[8,128,512]{2,1,0:T(8,128)(2,1)S(1)}) custom-call(s32[1]{0:T(128)} %bitcast.9.place_ref, bf16[2,512,512]{2,1,0:T(8,128)(2,1)S(1)} %copy-done, bf16[2,128,512]{2,1,0:T(8,128)(2,1)S(1)} %collective-permute-done.1.x0, bf16[2,128,512]{2,1,0:T(8,128)(2,1)S(1)} %collective-permute-done.3.x1, ...), custom_call_target="tpu_custom_call" | custom-call | tf_op jit(solution)/shard_map/pallas_call | solution.py:253
  82.2 2.3 %collective-permute-done.12 = bf16[8,128,512]{2,1,0:T(8,128)(2,1)S(1)} collective-permute-done((bf16[8,128,512]{2,1,0:T(8,128)(2,1)S(1)}, bf16[8,128,512]{2,1,0:T(8,128)(2,1)S(1)}, u32[]{:S(2)}, u32[]{:S(2)}) %collective-permute-start.12) | collective-permute-done | bytes 1048608 | tf_op jit(solution)/shard_map/ppermute | solution.py:280
  86.4 12.7 %collective-permute-done.13 = bf16[4,128,512]{2,1,0:T(8,128)(2,1)S(1)} collective-permute-done((bf16[4,128,512]{2,1,0:T(8,128)(2,1)S(1)}, bf16[4,128,512]{2,1,0:T(8,128)(2,1)S(1)}, u32[]{:S(2)}, u32[]{:S(2)}) %collective-permute-start.13) | collective-permute-done | bytes 524320 | tf_op jit(solution)/shard_map/ppermute | solution.py:280
  99.8 1.9 %collective-permute-start.16 = (bf16[1,128,512]{2,1,0:T(8,128)(2,1)S(1)}, bf16[1,128,512]{2,1,0:T(8,128)(2,1)S(1)}, u32[]{:S(2)}, u32[]{:S(2)}) collective-permute-start(bf16[1,128,512]{2,1,0:T(8,128)(2,1)S(1)} %get-tuple-element.75), channel_id=1, source_target_pairs={{0,12},{1,13},{2,14},{3,15},{4,8},{5,9},{6,10},{7,11},{8,4},{9,5},... | collective-permute-start | bytes 393224 | tf_op jit(solution)/shard_map/ppermute | solution.py:280
  102.9 2.5 %collective-permute-done.14 = bf16[1,128,512]{2,1,0:T(8,128)(2,1)S(1)} collective-permute-done((bf16[1,128,512]{2,1,0:T(8,128)(2,1)S(1)}, bf16[1,128,512]{2,1,0:T(8,128)(2,1)S(1)}, u32[]{:S(2)}, u32[]{:S(2)}) %collective-permute-start.14) | collective-permute-done | bytes 131104 | tf_op jit(solution)/shard_map/ppermute | solution.py:280
  105.3 3.4 %collective-permute-done.16 = bf16[1,128,512]{2,1,0:T(8,128)(2,1)S(1)} collective-permute-done((bf16[1,128,512]{2,1,0:T(8,128)(2,1)S(1)}, bf16[1,128,512]{2,1,0:T(8,128)(2,1)S(1)}, u32[]{:S(2)}, u32[]{:S(2)}) %collective-permute-start.16) | collective-permute-done | bytes 131104 | tf_op jit(solution)/shard_map/ppermute | solution.py:280
  108.8 5.4 %collective-permute-done.15 = bf16[1,128,512]{2,1,0:T(8,128)(2,1)S(1)} collective-permute-done((bf16[1,128,512]{2,1,0:T(8,128)(2,1)S(1)}, bf16[1,128,512]{2,1,0:T(8,128)(2,1)S(1)}, u32[]{:S(2)}, u32[]{:S(2)}) %collective-permute-start.15) | collective-permute-done | bytes 131104 | tf_op jit(solution)/shard_map/ppermute | solution.py:280
  115.4 3.3 %collective-permute-start.17 = (bf16[1,128,512]{2,1,0:T(8,128)(2,1)S(1)}, bf16[1,128,512]{2,1,0:T(8,128)(2,1)S(1)}, u32[]{:S(2)}, u32[]{:S(2)}) collective-permute-start(bf16[1,128,512]{2,1,0:T(8,128)(2,1)S(1)} %get-tuple-element.69), channel_id=1, source_target_pairs={{0,4},{1,5},{2,6},{3,7},{4,0},{5,1},{6,2},{7,3},{8,12},{9,13},{10,... | collective-permute-start | bytes 393224 | tf_op jit(solution)/shard_map/ppermute | solution.py:280
  118.7 3.9 %collective-permute-done.19 = bf16[1,128,512]{2,1,0:T(8,128)(2,1)S(1)} collective-permute-done((bf16[1,128,512]{2,1,0:T(8,128)(2,1)S(1)}, bf16[1,128,512]{2,1,0:T(8,128)(2,1)S(1)}, u32[]{:S(2)}, u32[]{:S(2)}) %collective-permute-start.19) | collective-permute-done | bytes 131104 | tf_op jit(solution)/shard_map/ppermute | solution.py:280
  122.6 3.3 %collective-permute-done.18 = bf16[1,128,512]{2,1,0:T(8,128)(2,1)S(1)} collective-permute-done((bf16[1,128,512]{2,1,0:T(8,128)(2,1)S(1)}, bf16[1,128,512]{2,1,0:T(8,128)(2,1)S(1)}, u32[]{:S(2)}, u32[]{:S(2)}) %collective-permute-start.18) | collective-permute-done | bytes 131104 | tf_op jit(solution)/shard_map/ppermute | solution.py:280
  127.7 12.3 %collective-permute-done.20 = bf16[4,128,512]{2,1,0:T(8,128)(2,1)S(1)} collective-permute-done((bf16[4,128,512]{2,1,0:T(8,128)(2,1)S(1)}, bf16[4,128,512]{2,1,0:T(8,128)(2,1)S(1)}, u32[]{:S(2)}, u32[]{:S(2)}) %collective-permute-start.20) | collective-permute-done | bytes 524320 | tf_op jit(solution)/shard_map/ppermute | solution.py:280
  143.6 2.1 %collective-permute-start.11 = (bf16[2,128,512]{2,1,0:T(8,128)(2,1)S(1)}, bf16[2,128,512]{2,1,0:T(8,128)(2,1)S(1)}, u32[]{:S(2)}, u32[]{:S(2)}) collective-permute-start(bf16[2,128,512]{2,1,0:T(8,128)(2,1)S(1)} %get-tuple-element.61), channel_id=1, source_target_pairs={{0,8},{1,9},{2,10},{3,11},{4,12},{5,13},{6,14},{7,15},{8,0},{9,1},... | collective-permute-start | bytes 786440 | tf_op jit(solution)/shard_map/ppermute | solution.py:19
  147.6 4.6 %shard_map.131 = (bf16[2,512,512]{2,1,0:T(8,128)(2,1)}, f32[2,512,512]{2,1,0:T(8,128)}) custom-call(bf16[2,512,512]{2,1,0:T(8,128)(2,1)S(1)} %copy-done.8, bf16[2,512,512]{2,1,0:T(8,128)(2,1)S(1)} %copy-done.10, bf16[2,512,512]{2,1,0:T(8,128)(2,1)S(1)} %copy-done.12, bf16[2,512,512]{2,1,0:T(8,128)(2,1)} %copy-done.13, bf16[512,512]{1,0:T(8,128)(2,1)S(1)} %copy-done.18, ...), custom_call_target="tpu_custom_call" | custom-call | tf_op jit(solution)/shard_map/pallas_call | solution.py:380
  152.2 4.0 %collective-permute-done.10.b2 = bf16[2,128,512]{2,1,0:T(8,128)(2,1)S(1)} collective-permute-done((bf16[2,128,512]{2,1,0:T(8,128)(2,1)S(1)}, bf16[2,128,512]{2,1,0:T(8,128)(2,1)S(1)}, u32[]{:S(2)}, u32[]{:S(2)}) %collective-permute-start.10) | collective-permute-done | bytes 262176 | tf_op jit(solution)/shard_map/ppermute | solution.py:19
  156.2 2.0 %collective-permute-done.11.b3 = bf16[2,128,512]{2,1,0:T(8,128)(2,1)S(1)} collective-permute-done((bf16[2,128,512]{2,1,0:T(8,128)(2,1)S(1)}, bf16[2,128,512]{2,1,0:T(8,128)(2,1)S(1)}, u32[]{:S(2)}, u32[]{:S(2)}) %collective-permute-start.11) | collective-permute-done | bytes 262176 | tf_op jit(solution)/shard_map/ppermute | solution.py:19
  161.6 2.3 %shard_map.135 = (f32[512,512]{1,0:T(8,128)}, f32[512,512]{1,0:T(8,128)}, f32[512,512]{1,0:T(8,128)}, f32[512,512]{1,0:T(8,128)}) custom-call(s32[1]{0:T(128)} %bitcast.9.place_ref, bf16[8,128,512]{2,1,0:T(8,128)(2,1)S(1)} %constant_dynamic-update-slice_fusion.refs_0_, bf16[8,128,512]{2,1,0:T(8,128)(2,1)S(1)} %collective-permute-done.21.refs_1_), custom_call_target="tpu_custom_call" | custom-call | tf_op jit(solution)/shard_map/pallas_call | solution.py:325
  (96 shorter events, 32.3 us)
Async XLA Ops:
  0.7 7.2 %collective-permute-start.2 = (s32[1,4]{1,0:T(1,128)}, s32[1,4]{1,0:T(1,128)S(1)}, u32[]{:S(2)}, u32[]{:S(2)}) collective-permute-start(s32[1,4]{1,0:T(1,128)} %param.13), channel_id=1, source_target_pairs={{0,2},{1,3},{2,0},{3,1},{4,6},{5,7},{6,4},{7,5},{8,10},{9,11},{10,... | collective-permute-start | bytes 56 | tf_op jit(solution)/shard_map/ppermute | solution.py:19
  3.7 5.4 %collective-permute-start = (s32[1,4]{1,0:T(1,128)}, s32[1,4]{1,0:T(1,128)S(1)}, u32[]{:S(2)}, u32[]{:S(2)}) collective-permute-start(s32[1,4]{1,0:T(1,128)} %param.13), channel_id=1, source_target_pairs={{0,1},{1,0},{2,3},{3,2},{4,5},{5,4},{6,7},{7,6},{8,9},{9,8},{10,11... | collective-permute-start | bytes 56 | tf_op jit(solution)/shard_map/ppermute | solution.py:19
  3.7 5.5 %collective-permute-start.6 = (s32[1,4]{1,0:T(1,128)}, s32[1,4]{1,0:T(1,128)S(1)}, u32[]{:S(2)}, u32[]{:S(2)}) collective-permute-start(s32[1,4]{1,0:T(1,128)} %param.13), channel_id=1, source_target_pairs={{0,8},{1,9},{2,10},{3,11},{4,12},{5,13},{6,14},{7,15},{8,0},{9,1},... | collective-permute-start | bytes 56 | tf_op jit(solution)/shard_map/ppermute | solution.py:19
  6.3 4.0 %collective-permute-start.4 = (s32[1,4]{1,0:T(1,128)}, s32[1,4]{1,0:T(1,128)S(1)}, u32[]{:S(2)}, u32[]{:S(2)}) collective-permute-start(s32[1,4]{1,0:T(1,128)} %param.13), channel_id=1, source_target_pairs={{0,4},{1,5},{2,6},{3,7},{4,0},{5,1},{6,2},{7,3},{8,12},{9,13},{10,... | collective-permute-start | bytes 56 | tf_op jit(solution)/shard_map/ppermute | solution.py:19
  13.6 23.0 %collective-permute-start.7 = (bf16[2,128,512]{2,1,0:T(8,128)(2,1)}, bf16[2,128,512]{2,1,0:T(8,128)(2,1)S(1)}, u32[]{:S(2)}, u32[]{:S(2)}) collective-permute-start(bf16[2,128,512]{2,1,0:T(8,128)(2,1)} %get-tuple-element.70), channel_id=1, source_target_pairs={{0,8},{1,9},{2,10},{3,11},{4,12},{5,13},{6,14},{7,15},{8,0},{9,1},... | collective-permute-start | bytes 786440 | tf_op jit(solution)/shard_map/ppermute | solution.py:19
  15.3 21.3 %collective-permute-start.5 = (bf16[2,128,512]{2,1,0:T(8,128)(2,1)}, bf16[2,128,512]{2,1,0:T(8,128)(2,1)S(1)}, u32[]{:S(2)}, u32[]{:S(2)}) collective-permute-start(bf16[2,128,512]{2,1,0:T(8,128)(2,1)} %get-tuple-element.71), channel_id=1, source_target_pairs={{0,4},{1,5},{2,6},{3,7},{4,0},{5,1},{6,2},{7,3},{8,12},{9,13},{10,... | collective-permute-start | bytes 786440 | tf_op jit(solution)/shard_map/ppermute | solution.py:19
  16.8 19.8 %collective-permute-start.3 = (bf16[2,128,512]{2,1,0:T(8,128)(2,1)}, bf16[2,128,512]{2,1,0:T(8,128)(2,1)S(1)}, u32[]{:S(2)}, u32[]{:S(2)}) collective-permute-start(bf16[2,128,512]{2,1,0:T(8,128)(2,1)} %get-tuple-element.72), channel_id=1, source_target_pairs={{0,2},{1,3},{2,0},{3,1},{4,6},{5,7},{6,4},{7,5},{8,10},{9,11},{10,... | collective-permute-start | bytes 786440 | tf_op jit(solution)/shard_map/ppermute | solution.py:19
  17.4 19.2 %collective-permute-start.1 = (bf16[2,128,512]{2,1,0:T(8,128)(2,1)S(1)}, bf16[2,128,512]{2,1,0:T(8,128)(2,1)S(1)}, u32[]{:S(2)}, u32[]{:S(2)}) collective-permute-start(bf16[2,128,512]{2,1,0:T(8,128)(2,1)S(1)} %get-tuple-element.73), channel_id=1, source_target_pairs={{0,1},{1,0},{2,3},{3,2},{4,5},{5,4},{6,7},{7,6},{8,9},{9,8},{10,11... | collective-permute-start | bytes 786440 | tf_op jit(solution)/shard_map/ppermute | solution.py:19
  81.6 2.8 %collective-permute-start.12 = (bf16[8,128,512]{2,1,0:T(8,128)(2,1)S(1)}, bf16[8,128,512]{2,1,0:T(8,128)(2,1)S(1)}, u32[]{:S(2)}, u32[]{:S(2)}) collective-permute-start(bf16[8,128,512]{2,1,0:T(8,128)(2,1)S(1)} %get-tuple-element.63), channel_id=1, source_target_pairs={{0,1},{1,0},{2,3},{3,2},{4,5},{5,4},{6,7},{7,6},{8,9},{9,8},{10,11... | collective-permute-start | bytes 3145736 | tf_op jit(solution)/shard_map/ppermute | solution.py:280
  84.8 14.3 %collective-permute-start.13 = (bf16[4,128,512]{2,1,0:T(8,128)(2,1)S(1)}, bf16[4,128,512]{2,1,0:T(8,128)(2,1)S(1)}, u32[]{:S(2)}, u32[]{:S(2)}) collective-permute-start(bf16[4,128,512]{2,1,0:T(8,128)(2,1)S(1)} %slice.47), channel_id=1, source_target_pairs={{0,2},{1,3},{2,0},{3,1},{4,6},{5,7},{6,4},{7,5},{8,10},{9,11},{10,... | collective-permute-start | bytes 1572872 | tf_op jit(solution)/shard_map/ppermute | solution.py:280
  99.3 40.8 %copy-start.4 = (bf16[2,512,512]{2,1,0:T(8,128)(2,1)S(1)}, bf16[2,512,512]{2,1,0:T(8,128)(2,1)}, u32[]{:S(2)}) copy-start(bf16[2,512,512]{2,1,0:T(8,128)(2,1)} %copy-done.3) | copy-start | bytes 3145732
  99.3 40.8 %copy-start.5 = (bf16[2,512,512]{2,1,0:T(8,128)(2,1)S(1)}, bf16[2,512,512]{2,1,0:T(8,128)(2,1)}, u32[]{:S(2)}) copy-start(bf16[2,512,512]{2,1,0:T(8,128)(2,1)} %get-tuple-element.57.refs_1_.dvp_ref) | copy-start | bytes 3145732
  99.3 6.0 %collective-permute-start.14 = (bf16[1,128,512]{2,1,0:T(8,128)(2,1)S(1)}, bf16[1,128,512]{2,1,0:T(8,128)(2,1)S(1)}, u32[]{:S(2)}, u32[]{:S(2)}) collective-permute-start(bf16[1,128,512]{2,1,0:T(8,128)(2,1)S(1)} %get-tuple-element.74), channel_id=1, source_target_pairs={{0,4},{1,5},{2,6},{3,7},{4,0},{5,1},{6,2},{7,3},{8,12},{9,13},{10,... | collective-permute-start | bytes 393224 | tf_op jit(solution)/shard_map/ppermute | solution.py:280
  99.8 9.0 %collective-permute-start.16 = (bf16[1,128,512]{2,1,0:T(8,128)(2,1)S(1)}, bf16[1,128,512]{2,1,0:T(8,128)(2,1)S(1)}, u32[]{:S(2)}, u32[]{:S(2)}) collective-permute-start(bf16[1,128,512]{2,1,0:T(8,128)(2,1)S(1)} %get-tuple-element.75), channel_id=1, source_target_pairs={{0,12},{1,13},{2,14},{3,15},{4,8},{5,9},{6,10},{7,11},{8,4},{9,5},... | collective-permute-start | bytes 393224 | tf_op jit(solution)/shard_map/ppermute | solution.py:280
  101.7 12.5 %collective-permute-start.15 = (bf16[1,128,512]{2,1,0:T(8,128)(2,1)S(1)}, bf16[1,128,512]{2,1,0:T(8,128)(2,1)S(1)}, u32[]{:S(2)}, u32[]{:S(2)}) collective-permute-start(bf16[1,128,512]{2,1,0:T(8,128)(2,1)S(1)} %get-tuple-element.76), channel_id=1, source_target_pairs={{0,8},{1,9},{2,10},{3,11},{4,12},{5,13},{6,14},{7,15},{8,0},{9,1},... | collective-permute-start | bytes 393224 | tf_op jit(solution)/shard_map/ppermute | solution.py:280
  114.3 8.4 %collective-permute-start.19 = (bf16[1,128,512]{2,1,0:T(8,128)(2,1)S(1)}, bf16[1,128,512]{2,1,0:T(8,128)(2,1)S(1)}, u32[]{:S(2)}, u32[]{:S(2)}) collective-permute-start(bf16[1,128,512]{2,1,0:T(8,128)(2,1)S(1)} %get-tuple-element.69), channel_id=1, source_target_pairs={{0,12},{1,13},{2,14},{3,15},{4,8},{5,9},{6,10},{7,11},{8,4},{9,5},... | collective-permute-start | bytes 393224 | tf_op jit(solution)/shard_map/ppermute | solution.py:280
  115.4 10.6 %collective-permute-start.18 = (bf16[1,128,512]{2,1,0:T(8,128)(2,1)S(1)}, bf16[1,128,512]{2,1,0:T(8,128)(2,1)S(1)}, u32[]{:S(2)}, u32[]{:S(2)}) collective-permute-start(bf16[1,128,512]{2,1,0:T(8,128)(2,1)S(1)} %get-tuple-element.69), channel_id=1, source_target_pairs={{0,8},{1,9},{2,10},{3,11},{4,12},{5,13},{6,14},{7,15},{8,0},{9,1},... | collective-permute-start | bytes 393224 | tf_op jit(solution)/shard_map/ppermute | solution.py:280
  115.4 10.6 %collective-permute-start.17 = (bf16[1,128,512]{2,1,0:T(8,128)(2,1)S(1)}, bf16[1,128,512]{2,1,0:T(8,128)(2,1)S(1)}, u32[]{:S(2)}, u32[]{:S(2)}) collective-permute-start(bf16[1,128,512]{2,1,0:T(8,128)(2,1)S(1)} %get-tuple-element.69), channel_id=1, source_target_pairs={{0,4},{1,5},{2,6},{3,7},{4,0},{5,1},{6,2},{7,3},{8,12},{9,13},{10,... | collective-permute-start | bytes 393224 | tf_op jit(solution)/shard_map/ppermute | solution.py:280
  126.0 13.9 %collective-permute-start.20 = (bf16[4,128,512]{2,1,0:T(8,128)(2,1)S(1)}, bf16[4,128,512]{2,1,0:T(8,128)(2,1)S(1)}, u32[]{:S(2)}, u32[]{:S(2)}) collective-permute-start(bf16[4,128,512]{2,1,0:T(8,128)(2,1)S(1)} %pad_maximum_fusion), channel_id=1, source_target_pairs={{0,2},{1,3},{2,0},{3,1},{4,6},{5,7},{6,4},{7,5},{8,10},{9,11},{10,... | collective-permute-start | bytes 1572872 | tf_op jit(solution)/shard_map/ppermute | solution.py:280
  140.0 21.6 %collective-permute-start.21 = (bf16[8,128,512]{2,1,0:T(8,128)(2,1)S(1)}, bf16[8,128,512]{2,1,0:T(8,128)(2,1)S(1)}, u32[]{:S(2)}, u32[]{:S(2)}) collective-permute-start(bf16[8,128,512]{2,1,0:T(8,128)(2,1)S(1)} %constant_dynamic-update-slice_fusion.refs_0_), channel_id=1, source_target_pairs={{0,1},{1,0},{2,3},{3,2},{4,5},{5,4},{6,7},{7,6},{8,9},{9,8},{10,11... | collective-permute-start | bytes 3145736 | tf_op jit(solution)/shard_map/ppermute | solution.py:280
  141.6 10.6 %collective-permute-start.8 = (bf16[2,128,512]{2,1,0:T(8,128)(2,1)S(1)}, bf16[2,128,512]{2,1,0:T(8,128)(2,1)S(1)}, u32[]{:S(2)}, u32[]{:S(2)}) collective-permute-start(bf16[2,128,512]{2,1,0:T(8,128)(2,1)S(1)} %get-tuple-element.58), channel_id=1, source_target_pairs={{0,1},{1,0},{2,3},{3,2},{4,5},{5,4},{6,7},{7,6},{8,9},{9,8},{10,11... | collective-permute-start | bytes 786440 | tf_op jit(solution)/shard_map/ppermute | solution.py:19
  142.2 10.0 %collective-permute-start.9 = (bf16[2,128,512]{2,1,0:T(8,128)(2,1)S(1)}, bf16[2,128,512]{2,1,0:T(8,128)(2,1)S(1)}, u32[]{:S(2)}, u32[]{:S(2)}) collective-permute-start(bf16[2,128,512]{2,1,0:T(8,128)(2,1)S(1)} %get-tuple-element.59), channel_id=1, source_target_pairs={{0,2},{1,3},{2,0},{3,1},{4,6},{5,7},{6,4},{7,5},{8,10},{9,11},{10,... | collective-permute-start | bytes 786440 | tf_op jit(solution)/shard_map/ppermute | solution.py:19
  143.6 12.6 %collective-permute-start.10 = (bf16[2,128,512]{2,1,0:T(8,128)(2,1)S(1)}, bf16[2,128,512]{2,1,0:T(8,128)(2,1)S(1)}, u32[]{:S(2)}, u32[]{:S(2)}) collective-permute-start(bf16[2,128,512]{2,1,0:T(8,128)(2,1)S(1)} %get-tuple-element.60), channel_id=1, source_target_pairs={{0,4},{1,5},{2,6},{3,7},{4,0},{5,1},{6,2},{7,3},{8,12},{9,13},{10,... | collective-permute-start | bytes 786440 | tf_op jit(solution)/shard_map/ppermute | solution.py:19
  143.6 14.6 %collective-permute-start.11 = (bf16[2,128,512]{2,1,0:T(8,128)(2,1)S(1)}, bf16[2,128,512]{2,1,0:T(8,128)(2,1)S(1)}, u32[]{:S(2)}, u32[]{:S(2)}) collective-permute-start(bf16[2,128,512]{2,1,0:T(8,128)(2,1)S(1)} %get-tuple-element.61), channel_id=1, source_target_pairs={{0,8},{1,9},{2,10},{3,11},{4,12},{5,13},{6,14},{7,15},{8,0},{9,1},... | collective-permute-start | bytes 786440 | tf_op jit(solution)/shard_map/ppermute | solution.py:19
  (24 other events, 274.4 us)

commit v2 on v1

--- a/solution.py
+++ b/solution.py
@@ -8,8 +8,8 @@
 from jax.sharding import PartitionSpec as P
 
 SUB = 128
-GROUPS = 1
-VMEM = 48 * 1024 * 1024
+CHUNKS = ((0, 1), (2, 3))
+VMEM = 24 * 1024 * 1024
 F32 = jnp.float32
 BF16 = jnp.bfloat16
 OFF = 1e30
@@ -37,6 +37,14 @@
 
 def params(*semantics):
     return pltpu.CompilerParams(vmem_limit_bytes=VMEM, dimension_semantics=semantics or None)
+
+
+def cost(us):
+    return pl.CostEstimate(flops=int(us * 1.1e9), bytes_accessed=int(us * 1e5), transcendentals=0)
+
+
+def far(*arrays):
+    return [pltpu.with_memory_space_constraint(x, pltpu.HBM) for x in arrays]
 
 
 def head_rows(pair_rows, which, head_width):
@@ -45,8 +53,9 @@
     return jnp.where(keep, pair_rows, jnp.zeros_like(pair_rows))
 
 
-def project_kernel(scale, x_ref, c_ref, wq_ref, wk_ref, wv_ref, wo_ref, qt_ref, k_ref, v_ref, kt_ref, vt_ref, dot_ref):
+def project_kernel(scale, x_ref, c_ref, wq_ref, wk_ref, wv_ref, wo_ref, qt_ref, k_ref, v_ref, kt_ref, vt_ref, dot_ref, xt_ref):
     x = x_ref[0]
+    xt_ref[0] = x.T
     qt_ref[0] = (tt(wq_ref[...], x).astype(BF16).astype(F32) * scale).astype(BF16)
     k = nn(x, wk_ref[...])
     v = nn(x, wv_ref[...])
@@ -62,20 +71,24 @@
     row_block = pl.BlockSpec((1, rows, width), lambda s: (s, 0, 0))
     col_block = pl.BlockSpec((1, width, rows), lambda s: (s, 0, 0))
     whole = pl.BlockSpec((width, width), lambda s: (0, 0))
-    by_row = jax.ShapeDtypeStruct((samples, rows, width), BF16)
-    by_col = jax.ShapeDtypeStruct((samples, width, rows), BF16)
+    by_row = pltpu.VMEM((samples, rows, width), BF16)
+    by_col = pltpu.VMEM((samples, width, rows), BF16)
+    far_row = pltpu.HBM((samples, rows, width), BF16)
+    far_col = pltpu.HBM((samples, width, rows), BF16)
     return pl.pallas_call(
         functools.partial(project_kernel, scale),
         grid=(samples,),
         in_specs=[row_block, row_block] + [whole] * 4,
-        out_specs=[col_block, row_block, row_block, col_block, col_block, col_block],
-        out_shape=[by_col, by_row, by_row, by_col, by_col, by_col],
+        out_specs=[col_block, row_block, row_block, col_block, col_block, col_block, col_block],
+        out_shape=[by_col, by_row, far_row, far_col, by_col, far_col, far_col],
+        cost_estimate=cost(5),
         compiler_params=params("arbitrary"),
-    )(tokens, cotangent, w_query, w_key, w_value, w_out)
-
-
-def project_partner_kernel(x0, x1, x2, x3, wk_ref, wv_ref, k_ref, v_ref, kt_ref, vt_ref):
+    )(*far(tokens, cotangent, w_query, w_key, w_value, w_out))
+
+
+def project_partner_kernel(x0, x1, x2, x3, wk_ref, wv_ref, k_ref, v_ref, kt_ref, vt_ref, xt_ref):
     x = jnp.concatenate([x0[0], x1[0], x2[0], x3[0]], 0)
+    xt_ref[0] = x.T
     k = nn(x, wk_ref[...])
     v = nn(x, wv_ref[...])
     k_ref[0] = k.astype(BF16)
@@ -91,14 +104,15 @@
     row_block = pl.BlockSpec((1, rows, width), lambda s: (s, 0, 0))
     col_block = pl.BlockSpec((1, width, rows), lambda s: (s, 0, 0))
     whole = pl.BlockSpec((width, width), lambda s: (0, 0))
-    by_row = jax.ShapeDtypeStruct((samples, rows, width), BF16)
-    by_col = jax.ShapeDtypeStruct((samples, width, rows), BF16)
+    by_row = pltpu.VMEM((samples, rows, width), BF16)
+    by_col = pltpu.VMEM((samples, width, rows), BF16)
     return pl.pallas_call(
         project_partner_kernel,
         grid=(samples,),
         in_specs=[part] * 4 + [whole] * 2,
-        out_specs=[row_block, row_block, col_block, col_block],
-        out_shape=[by_row, by_row, by_col, by_col],
+        out_specs=[row_block, row_block, col_block, col_block, col_block],
+        out_shape=[by_row, by_row, by_col, by_col, by_col],
+        cost_estimate=cost(2.5),
         compiler_params=params("arbitrary"),
     )(*arrived, w_key, w_value)
 
@@ -131,19 +145,20 @@
         in_specs=[col_pair, row_pair, col_pair],
         out_specs=[per_head(rows), per_head(head_width), per_head(8)],
         out_shape=[
-            jax.ShapeDtypeStruct((samples, head_count, rows, rows), BF16),
-            jax.ShapeDtypeStruct((samples, head_count, head_width, rows), F32),
-            jax.ShapeDtypeStruct((samples, head_count, 8, rows), F32),
+            pltpu.HBM((samples, head_count, rows, rows), BF16),
+            pltpu.HBM((samples, head_count, head_width, rows), F32),
+            pltpu.HBM((samples, head_count, 8, rows), F32),
         ],
+        cost_estimate=cost(10),
         compiler_params=params("arbitrary", "arbitrary"),
     )(qt, k, vt)
 
 
 def attend_kernel(
-    first_pair, head_width, scale, mask_ref, e_ref, o_ref, st_ref, qt_ref, dot_ref, ko_ref, vo_ref, kto_ref, kp_ref, vp_ref, ktp_ref,
-    vtp_ref, ctx_ref, dqt_ref, dko_ref, dvo_ref, dkp_ref, dvp_ref,
+    pair, head_width, scale, mask_ref, e_ref, o_ref, st_ref, qt_ref, dot_ref, ko_ref, vo_ref, kto_ref, kp_ref, vp_ref, ktp_ref,
+    vtp_ref, *refs,
 ):
-    pair = first_pair + pl.program_id(0)
+    ctx_ref, dqt_ref, dko_ref, dvo_ref, dkp_ref, dvp_ref = refs[-6:]
     sections = mask_ref.shape[0]
     sub = kp_ref.shape[1] // sections
     ko, vo, kp, vp = ko_ref[0], vo_ref[0], kp_ref[0], vp_ref[0]
@@ -190,37 +205,39 @@
     dvp_ref[0] = dvp.astype(BF16)
 
 
-def attend(group, groups, head_masks, own, qt, dot, ko, vo, kto, partner_rows, head_count, scale):
+def attend(pair, head_masks, own, qt, dot, ko, vo, kto, partner_rows, head_count, scale, after):
     e, o, st = own
     kp, vp, ktp, vtp = partner_rows
     samples, width, rows = qt.shape
     head_width = width // head_count
-    pairs = head_count // 2 // groups
-    first = group * pairs
-    col_in = pl.BlockSpec((1, 2 * head_width, rows), lambda p, s: (s, first + p, 0))
-    row_in = pl.BlockSpec((1, rows, 2 * head_width), lambda p, s: (s, 0, first + p))
-    col_out = pl.BlockSpec((1, 2 * head_width, rows), lambda p, s: (s, p, 0))
-    row_out = pl.BlockSpec((1, rows, 2 * head_width), lambda p, s: (s, 0, p))
+    col_in = pl.BlockSpec((1, 2 * head_width, rows), lambda s: (s, pair, 0))
+    row_in = pl.BlockSpec((1, rows, 2 * head_width), lambda s: (s, 0, pair))
+    col_out = pl.BlockSpec((1, 2 * head_width, rows), lambda s: (s, 0, 0))
+    row_out = pl.BlockSpec((1, rows, 2 * head_width), lambda s: (s, 0, 0))
 
     def per_head(n):
-        return pl.BlockSpec((1, 2, n, rows), lambda p, s: (s, first + p, 0, 0))
-
-    by_col = jax.ShapeDtypeStruct((samples, width // groups, rows), BF16)
-    by_row = jax.ShapeDtypeStruct((samples, rows, width // groups), BF16)
-    return pl.pallas_call(
-        functools.partial(attend_kernel, first, head_width, scale),
-        grid=(pairs, samples),
+        return pl.BlockSpec((1, 2, n, rows), lambda s: (s, pair, 0, 0))
+
+    by_col = pltpu.VMEM((samples, 2 * head_width, rows), BF16)
+    by_row = pltpu.VMEM((samples, rows, 2 * head_width), BF16)
+    return pl.pallas_call(
+        functools.partial(attend_kernel, pair, head_width, scale),
+        grid=(samples,),
         in_specs=[pl.BlockSpec(memory_space=pltpu.SMEM), per_head(rows), per_head(head_width), per_head(8)]
-        + [col_in, col_in, row_in, row_in, col_in, row_in, row_in, col_in, col_in],
+        + [col_in, col_in, row_in, row_in, col_in, row_in, row_in, col_in, col_in]
+        + [pl.BlockSpec(memory_space=pl.ANY)] * len(after),
         out_specs=[col_out, col_out] + [row_out] * 4,
         out_shape=[by_col, by_col] + [by_row] * 4,
-        compiler_params=params("arbitrary", "arbitrary"),
-    )(head_masks, e, o, st, qt, dot, ko, vo, kto, kp, vp, ktp, vtp)
-
-
-def weights_kernel(place_ref, x_ref, x0, x1, x2, x3, c_ref, ctx_ref, dqt_ref, dko_ref, dvo_ref, dkp_ref, dvp_ref, keep_ref, send_ref, all_ref):
-    samples, rows, width = x_ref.shape
-    cols = dko_ref.shape[2]
+        cost_estimate=cost(7),
+        compiler_params=params("arbitrary"),
+    )(head_masks, *far(e, o, st), qt, *far(dot), ko, *far(vo, kto), kp, vp, ktp, vtp, *after)
+
+
+def weights_kernel(pairs, place_ref, xt_ref, xtp_ref, c_ref, *refs):
+    ctxs, dqts, dkos, dvos, dkps, dvps = (refs[i * pairs : (i + 1) * pairs] for i in range(6))
+    keep_ref, send_ref, all_ref = refs[-3:]
+    samples, width, rows = xt_ref.shape
+    cols = pairs * dkos[0].shape[2]
     chunk = keep_ref.shape[1]
     chunks = 2 * keep_ref.shape[0]
     per_type = chunks // 4
@@ -229,34 +246,38 @@
         for i in range(per_type):
             all_ref[(kind * per_type + i) ^ place_ref[0]] = value[i * chunk : (i + 1) * chunk].astype(BF16)
 
-    own = samples * rows
-    x_all = jnp.concatenate([x_ref[s] for s in range(samples)] + [x[s] for s in range(samples) for x in (x0, x1, x2, x3)], 0)
-    xt = x_all.T
-    ctx = jnp.concatenate([ctx_ref[s] for s in range(samples)], 1)
-    go = nn(ctx, c_ref[...].reshape(own, width))
+    xt = jnp.concatenate([xt_ref[s] for s in range(samples)], 1)
+    xt_all = jnp.concatenate([xt_ref[s] for s in range(samples)] + [xtp_ref[s] for s in range(samples)], 1)
+
+    def across(parts):
+        return jnp.concatenate([jnp.concatenate([r[s] for r in parts], 0) for s in range(samples)], 1)
+
+    def down(parts):
+        return [jnp.concatenate([r[s] for r in parts], 1) for s in range(samples)]
+
+    go = nn(across(ctxs), c_ref[...].reshape(samples * rows, width))
     put(3, jnp.concatenate([go[:, i : i + cols] for i in range(0, width, cols)], 0))
-    dqt = jnp.concatenate([dqt_ref[s] for s in range(samples)], 1)
-    put(0, nt(xt[:, :own], dqt))
-    dk = jnp.concatenate([dko_ref[s] for s in range(samples)] + [dkp_ref[s] for s in range(samples)], 0)
-    put(1, nn(xt, dk))
-    dv = jnp.concatenate([dvo_ref[s] for s in range(samples)] + [dvp_ref[s] for s in range(samples)], 0)
-    put(2, nn(xt, dv))
+    put(0, nt(xt, across(dqts)))
+    put(1, nn(xt_all, jnp.concatenate(down(dkos) + down(dkps), 0)))
+    put(2, nn(xt_all, jnp.concatenate(down(dvos) + down(dvps), 0)))
     keep_ref[...] = all_ref[: chunks // 2]
     send_ref[...] = all_ref[chunks // 2 :]
 
 
-def weight_grads(place, devices, tokens, arrived, cotangent, parts):
-    width = tokens.shape[2]
-    cols = parts[0].shape[1]
-    half = jax.ShapeDtypeStruct((devices // 2, 4 * width // devices, cols), BF16)
+def weight_grads(place, devices, xt, xtp, cotangent, parts, after):
+    samples, width, rows = xt.shape
+    pairs = len(parts[0])
+    cols = pairs * parts[0][0].shape[1]
+    half = pltpu.VMEM((devices // 2, 4 * width // devices, cols), BF16)
     whole = pl.BlockSpec(memory_space=pltpu.VMEM)
     return pl.pallas_call(
-        weights_kernel,
-        in_specs=[pl.BlockSpec(memory_space=pltpu.SMEM)] + [whole] * 12,
+        functools.partial(weights_kernel, pairs),
+        in_specs=[pl.BlockSpec(memory_space=pltpu.SMEM)] + [pl.BlockSpec(xt.shape, lambda: (0, 0, 0)), whole, pl.BlockSpec(cotangent.shape, lambda: (0, 0, 0))] + [whole] * (6 * pairs) + [pl.BlockSpec(memory_space=pl.ANY)] * len(after),
         out_shape=[half, half],
         scratch_shapes=[pltpu.VMEM((devices, 4 * width // devices, cols), BF16)],
+        cost_estimate=cost(3),
         compiler_params=params(),
-    )(place, tokens, *arrived, cotangent, *parts)
+    )(place, *far(xt), xtp, *far(cotangent), *[x for part in parts for x in part], *after)
 
 
 def plan_of(levels):
@@ -280,37 +301,35 @@
     return lax.ppermute(x, "tok", [(i, i ^ mask) for i in range(lax.axis_size("tok"))])
 
 
-def reduce_all(plan, keep, send):
-    sends = [send]
-    kept = keep
-    for number, bits in enumerate(plan):
-        came = [exchange(piece, spread(m + 1, bits)) for m, piece in enumerate(sends)]
-        total = kept.astype(F32)
-        for piece in came:
-            total = total + piece.astype(F32)
-        if number + 1 < len(plan):
-            share = total.shape[0] >> len(plan[number + 1])
-            parts = [total[i : i + share].astype(BF16) for i in range(0, total.shape[0], share)]
-            kept, sends = parts[0], parts[1:]
-        else:
-            kept = total.astype(BF16)
-    pieces = [kept]
-    for bits in reversed(plan):
-        mine = pieces[0] if len(pieces) == 1 else jnp.concatenate(pieces, 0)
-        pieces = [mine] + [exchange(mine, spread(m, bits)) for m in range(1, 1 << len(bits))]
-    return pieces
-
-
-def spread_kernel(groups, count, place_ref, *refs):
-    piece_refs, out_refs, all_ref = refs[: groups * count], refs[groups * count : -1], refs[-1]
-    kinds, per_type, chunk, width = 4, all_ref.shape[0] // 4, all_ref.shape[1], all_ref.shape[2]
+def fold(kept, came, share):
+    total = kept.astype(F32)
+    for piece in came:
+        total = total + piece.astype(F32)
+    parts = [total[i : i + share].astype(BF16) for i in range(0, total.shape[0], share)]
+    return parts[0], parts[1:]
+
+
+def send_all(pieces, bits):
+    return [exchange(piece, spread(m + 1, bits)) for m, piece in enumerate(pieces)]
+
+
+def gather_all(mine, bits):
+    return [mine] + [exchange(mine, spread(m, bits)) for m in range(1, 1 << len(bits))]
+
+
+def tie(*values):
+    return lax.optimization_barrier(values)
+
+
+def spread_kernel(groups, place_ref, *refs):
+    piece_refs, out_refs, all_ref = refs[:-5], refs[-5:-1], refs[-1]
+    per_type, width = all_ref.shape[0] // 4, all_ref.shape[2]
     cols = width // groups
-    for g in range(groups):
-        slot = 0
-        for ref in piece_refs[g * count : (g + 1) * count]:
-            for i in range(ref.shape[0]):
-                all_ref[slot ^ place_ref[0], :, g * cols : (g + 1) * cols] = ref[i].astype(F32)
-                slot += 1
+    slot = 0
+    for ref in piece_refs:
+        for i in range(ref.shape[0]):
+            all_ref[slot ^ place_ref[0]] = ref[i].astype(F32)
+            slot += 1
     for kind in range(3):
         out_refs[kind][...] = all_ref[kind * per_type : (kind + 1) * per_type].reshape(width, width)
     last = all_ref[3 * per_type :].reshape(groups, cols, width)
@@ -320,15 +339,14 @@
 
 
 def spread_grads(place, devices, width, pieces):
-    groups, count = len(pieces), len(pieces[0])
     whole = pl.BlockSpec(memory_space=pltpu.VMEM)
     return pl.pallas_call(
-        functools.partial(spread_kernel, groups, count),
-        in_specs=[pl.BlockSpec(memory_space=pltpu.SMEM)] + [whole] * (groups * count),
+        functools.partial(spread_kernel, len(CHUNKS)),
+        in_specs=[pl.BlockSpec(memory_space=pltpu.SMEM)] + [whole] * len(pieces),
         out_shape=[jax.ShapeDtypeStruct((width, width), F32)] * 4,
         scratch_shapes=[pltpu.VMEM((devices, 4 * width // devices, width), F32)],
         compiler_params=params(),
-    )(place, *[piece for group in pieces for piece in group])
+    )(place, *pieces)
 
 
 def back_kernel(groups, *refs):
@@ -353,7 +371,8 @@
         grid=(samples,),
         in_specs=[part] * (2 * groups) + [whole] * 2,
         out_specs=[pl.BlockSpec((1, rows // 4, width), lambda s: (s, 0, 0))] * 4,
-        out_shape=[jax.ShapeDtypeStruct((samples, rows // 4, width), BF16)] * 4,
+        out_shape=[pltpu.VMEM((samples, rows // 4, width), BF16)] * 4,
+        cost_estimate=cost(1.7),
         compiler_params=params("arbitrary"),
     )(*dkps, *dvps, w_key, w_value)
 
@@ -382,16 +401,17 @@
         grid=(samples,),
         in_specs=[part] * (2 * groups) + [row_part] * (2 * groups) + [whole] * 4,
         out_specs=[row_block, row_block],
-        out_shape=[jax.ShapeDtypeStruct((samples, rows, width), BF16), jax.ShapeDtypeStruct((samples, rows, width), F32)],
+        out_shape=[jax.ShapeDtypeStruct((samples, rows, width), BF16), pltpu.VMEM((samples, rows, width), F32)],
+        cost_estimate=cost(4),
         compiler_params=params("arbitrary"),
     )(*ctxs, *dqts, *dks, *dvs, w_out, w_query, w_key, w_value)
 
 
-def token_kernel(start_ref, gt_ref, b0, b1, b2, b3, out_ref, acc_ref):
+def token_kernel(i0, i1, i2, i3, gt_ref, b0, b1, b2, b3, out_ref, acc_ref):
     sub = b0.shape[1]
     acc_ref[...] = gt_ref[0]
-    for section, came in enumerate((b0, b1, b2, b3)):
-        acc_ref[pl.ds(pl.multiple_of(start_ref[section] * sub, sub), sub), :] += came[0].astype(F32)
+    for section, (index, came) in enumerate(((i0, b0), (i1, b1), (i2, b2), (i3, b3))):
+        acc_ref[pl.ds(pl.multiple_of(index[0, section] * sub, sub), sub), :] += came[0].astype(F32)
     out_ref[0] = acc_ref[...].astype(BF16)
 
 
@@ -402,12 +422,29 @@
     return pl.pallas_call(
         token_kernel,
         grid=(samples,),
-        in_specs=[pl.BlockSpec(memory_space=pltpu.SMEM), row_block] + [came] * 4,
+        in_specs=[pl.BlockSpec(memory_space=pltpu.SMEM)] * 4 + [row_block] + [came] * 4,
         out_specs=row_block,
         out_shape=jax.ShapeDtypeStruct((samples, rows, width), BF16),
         scratch_shapes=[pltpu.VMEM((rows, width), F32)],
         compiler_params=params("arbitrary"),
-    )(starts, partial, *backs)
+    )(*starts, partial, *backs)
+
+
+def pick_kernel(i0, i1, i2, i3, x_ref, o0, o1, o2, o3):
+    sub = o0.shape[1]
+    for section, (index, out) in enumerate(((i0, o0), (i1, o1), (i2, o2), (i3, o3))):
+        out[...] = x_ref[:, pl.ds(pl.multiple_of(index[0, section] * sub, sub), sub), :]
+
+
+def pick(starts, tokens):
+    samples, _, width = tokens.shape
+    return pl.pallas_call(
+        pick_kernel,
+        in_specs=[pl.BlockSpec(memory_space=pltpu.SMEM)] * 4 + [pl.BlockSpec(tokens.shape, lambda: (0, 0, 0))],
+        out_shape=[pltpu.VMEM((samples, SUB, width), BF16)] * 4,
+        cost_estimate=cost(1),
+        compiler_params=params(),
+    )(*starts, *far(tokens))
 
 
 def per_device(tokens, w_query, w_key, w_value, w_out, partner_block, head_masks, cotangent):
@@ -418,23 +455,51 @@
     plan = plan_of(levels)
     place = place_of(plan)
     scale = (width // head_count) ** -0.5
-    theirs = [partner(partner_block, levels - 4 + section)[0, section] for section in range(4)]
-    qt, ko, vo, kto, vto, dot = project(tokens, cotangent, w_query, w_key, w_value, w_out, scale)
-    arrived = [
-        partner(lax.dynamic_slice_in_dim(tokens, theirs[section] * SUB, SUB, 1), levels - 4 + section) for section in range(4)
-    ]
+    theirs = [partner(partner_block, levels - 4 + section) for section in range(4)]
+    qt, ko, vo, kto, vto, dot, xt = project(tokens, cotangent, w_query, w_key, w_value, w_out, scale)
+    arrived = [partner(piece, levels - 4 + section) for section, piece in enumerate(pick(theirs, tokens))]
     own = own_part(qt, ko, vto, head_count)
-    partner_rows = project_partner(arrived, w_key, w_value)
-    done, sums = [], []
-    for group in range(GROUPS):
-        parts = attend(group, GROUPS, head_masks[0], own, qt, dot, ko, vo, kto, partner_rows, head_count, scale)
-        done.append(parts)
-        sums.append(reduce_all(plan, *weight_grads(place, devices, tokens, arrived, cotangent, parts)))
-    ctxs, dqts, dkos, dvos, dkps, dvps = zip(*done)
-    backs = [partner(piece, levels - 4 + i) for i, piece in enumerate(back(dkps, dvps, w_key, w_value))]
+    *partner_rows, xtp = project_partner(arrived, w_key, w_value)
+    def run(pair, after=()):
+        return attend(pair, head_masks[0], own, qt, dot, ko, vo, kto, partner_rows, head_count, scale, after)
+
+    def weigh(parts, after=()):
+        return weight_grads(place, devices, xt, xtp, cotangent, list(zip(*parts)), after)
+
+    first = [run(pair) for pair in CHUNKS[0]]
+    kept0, sends0 = weigh(first)
+    came = send_all([sends0], plan[0])
+    second = [run(CHUNKS[1][0], (sends0,))]
+    kept0, sends0 = fold(kept0, came, devices // 4)
+    came = send_all(sends0, plan[1])
+    second.append(run(CHUNKS[1][1], sends0))
+    kept0, _ = fold(kept0, came, devices // 4)
+    kept, sends = weigh(second, (kept0,))
+    ctxs, dqts, dkos, dvos, dkps, dvps = zip(*(first + second))
+    came = send_all([sends], plan[0])
+    backs = back(dkps, dvps, w_key, w_value)
+    kept, sends = fold(kept, came, devices // 4)
+    came, *backs = tie(*send_all(sends, plan[1]), *backs)
+    backs = [partner(piece, levels - 4 + i) for i, piece in enumerate(backs)]
     output, partial = finish(ctxs, dqts, dkos, dvos, w_out, w_query, w_key, w_value)
-    grad_tokens = token_grads(jnp.stack(theirs), partial, backs)
-    return (output, grad_tokens, *spread_grads(place, devices, width, sums))
+    kept, _ = fold(kept, [came], devices // 4)
+    kept = jnp.concatenate([kept0, kept], 2)
+    left = devices // 4
+    for number in range(2, len(plan)):
+        left >>= len(plan[number])
+        sends = [kept[i : i + left] for i in range(0, kept.shape[0], left)]
+        came = send_all(sends[1:], plan[number])
+        if number == 2:
+            *came, partial = tie(*came, partial)
+        kept, _ = fold(sends[0], came, left)
+    grad_tokens = token_grads(theirs, partial, backs)
+    pieces = [kept]
+    for number in reversed(range(len(plan))):
+        mine = pieces[0] if len(pieces) == 1 else jnp.concatenate(pieces, 0)
+        if number == 0:
+            mine, grad_tokens = tie(mine, grad_tokens)
+        pieces = gather_all(mine, plan[number])
+    return (output, grad_tokens, *spread_grads(place, devices, width, pieces))
 
 
 def solution(mesh):

time: 164 us -> 129 us (0.79)
  waiting for transfers between devices: 51.9 us -> 33.7 us
  local copies, waits for them, and re-layouts: 16.8 us -> 0.15 us
  Pallas kernels: 63.2 us -> 67 us
  other arithmetic: 2.42 us -> 0.6 us
  between operations: 2.76 us -> 0.97 us
    ppermute x10 -> x12, waiting for transfers between devices: 45.9 us -> 18.4 us  [exchange(): lax.ppermute(x, 'tok', [(i, i ^ mask) for i in range(lax.axis_size('tok'))])]
    unnamed x55 -> x21, local copies, waits for them, and re-layouts: 12.8 us -> 0.08 us
    ppermute x12, waiting for transfers between devices: 6.04 us -> 15.3 us  [partner(): lax.ppermute(x, 'tok', [(i, i ^ 1 << stride) for i in range(lax.axis_size...]
    pallas_call x3 -> x8, Pallas kernels: 37.1 us -> 42.2 us  [the longest x4 31 us: attend(): pl.pallas_call(functools.partial(attend_kernel, pair, head_width, scale),...]
    dynamic_slice x1 -> x0, local copies, waits for them, and re-layouts: 2.1 us -> none  [per_device(): lax.dynamic_slice_in_dim(tokens, theirs[section] * SUB, SUB, 1)]
    another operation x3 -> x2, other arithmetic: 2.29 us -> 0.29 us  [the longest x1 1.82 us: per_device(): grad_tokens = token_grads(jnp.stack(theirs), partial, backs)]
    ppermute x12, starting transfers between devices: 15.1 us -> 13.2 us  [partner(): lax.ppermute(x, 'tok', [(i, i ^ 1 << stride) for i in range(lax.axis_size...]
    slice x5 -> x2, local copies, waits for them, and re-layouts: 1.8 us -> 0.04 us  [fold(): total[i:i + share].astype(BF16)]
  transfers between devices with their start and end apart: 22 -> 24, of which waited for: 10 -> 12; matrix products, arithmetic and copies ran while one was open for 2% -> 0% of each run, Pallas kernels for 14% -> 30%
where the time goes in v2:
time: 129 us
  Pallas kernels  67 us (52%)
  waiting for transfers between devices  33.7 us (26%)
  starting transfers between devices  26.2 us (20%)
    pallas_call x4, Pallas kernels, attend(): pl.pallas_call(functools.partial(attend_kernel, pair, head_width, scale),...  31 us
    ppermute x12, waiting for transfers between devices, exchange(): lax.ppermute(x, 'tok', [(i, i ^ mask) for i in range(lax.axis_size('tok'))])  18.4 us
    ppermute x12, waiting for transfers between devices, partner(): lax.ppermute(x, 'tok', [(i, i ^ 1 << stride) for i in range(lax.axis_size...  15.3 us
    ppermute x12, starting transfers between devices, partner(): lax.ppermute(x, 'tok', [(i, i ^ 1 << stride) for i in range(lax.axis_size...  13.2 us
    ppermute x12, starting transfers between devices, exchange(): lax.ppermute(x, 'tok', [(i, i ^ mask) for i in range(lax.axis_size('tok'))])  13 us
    pallas_call x1, Pallas kernels, own_part(): pl.pallas_call(functools.partial(own_kernel, head_width), grid=(head_coun...  11.2 us
    pallas_call x2, Pallas kernels, weight_grads(): pl.pallas_call(functools.partial(weights_kernel, pairs), in_specs=[pl.Blo...  6.88 us
    pallas_call x1, Pallas kernels, project(): pl.pallas_call(functools.partial(project_kernel, scale), grid=(samples,),...  5.38 us
  transfers between devices with their start and end apart: 24, of which 12 were waited for; matrix products, arithmetic and copies ran while one was open for 0% of the time, Pallas kernels for 30%

profile of v2, /device:TPU:0, one launch (start us, length us, event | category | flops | bytes accessed | tf_op | source)
XLA Modules:
  0.0 128.5 jit_solution(3505130558118936557)
XLA Ops:
  0.6 3.0 %collective-permute-start.1 = (s32[1,4]{1,0:T(1,128)}, s32[1,4]{1,0:T(1,128)S(1)}, u32[]{:S(2)}, u32[]{:S(2)}) collective-permute-start(s32[1,4]{1,0:T(1,128)} %param.13), channel_id=1, source_target_pairs={{0,2},{1,3},{2,0},{3,1},{4,6},{5,7},{6,4},{7,5},{8,10},{9,11},{10,... | collective-permute-start | bytes 56 | tf_op jit(solution)/shard_map/ppermute | solution.py:19
  3.7 2.6 %collective-permute-start.3 = (s32[1,4]{1,0:T(1,128)}, s32[1,4]{1,0:T(1,128)S(1)}, u32[]{:S(2)}, u32[]{:S(2)}) collective-permute-start(s32[1,4]{1,0:T(1,128)} %param.13), channel_id=1, source_target_pairs={{0,8},{1,9},{2,10},{3,11},{4,12},{5,13},{6,14},{7,15},{8,0},{9,1},... | collective-permute-start | bytes 56 | tf_op jit(solution)/shard_map/ppermute | solution.py:19
  7.8 5.4 %shard_map.127 = (bf16[2,512,512]{2,1,0:T(8,128)(2,1)S(1)}, bf16[2,512,512]{2,1,0:T(8,128)(2,1)S(1)}, bf16[2,512,512]{2,1,0:T(8,128)(2,1)}, bf16[2,512,512]{2,1,...) custom-call(bf16[2,512,512]{2,1,0:T(8,128)(2,1)} %x_ref.3, ...), custom_call_target="tpu_custom_call" | custom-call | flops 5500000256 | bytes 500000 | tf_op jit(solution)/shard_map/pallas_call | solution.py:78
  13.3 2.0 %shard_map.129 = (bf16[2,128,512]{2,1,0:T(8,128)(2,1)S(1)}, bf16[2,128,512]{2,1,0:T(8,128)(2,1)S(1)}, bf16[2,128,512]{2,1,0:T(8,128)(2,1)S(1)}, bf16[2,128,512]{2,1,0:T(8,128)(2,1)S(1)}) custom-call(s32[1,4]{1,0:T(1,128)S(1)} %collective-permute-done.i0, s32[1,4]{1,0:T(1,128)S(1)} %collective-permute-done.1.i1, s32[1,4]{1,0:T(1,128)S(1)} %collective-permute-done.2.i2, ...), custom_call_target="tpu_custom_call" | custom-call | flops 1100000000 | bytes 100000 | tf_op jit(solution)/shard_map/pallas_call | solution.py:441
  16.6 11.2 %shard_map.128 = (bf16[2,8,512,512]{3,2,1,0:T(8,128)(2,1)}, f32[2,8,64,512]{3,2,1,0:T(8,128)}, f32[2,8,8,512]{3,2,1,0:T(8,128)}) custom-call(bf16[2,512,512]{2,1,0:T(8,128)(2,1)S(1)} %get-tuple-element.74.qt_ref, bf16[2,512,512]{2,1,0:T(8,128)(2,1)S(1)} %get-tuple-element.75.k_ref.ko_ref, bf16[2,512,512]{2,1,0:T(8,128)(2,1)S(1)} %get-tuple-element.76.vt_ref), custom_call_target="tpu_custom_call" | custom-call | flops 11000000512 | bytes 1000000 | tf_op jit(solution)/shard_map/pallas_call | solution.py:142
  28.7 2.4 %collective-permute-done.7.x3 = bf16[2,128,512]{2,1,0:T(8,128)(2,1)S(1)} collective-permute-done((bf16[2,128,512]{2,1,0:T(8,128)(2,1)S(1)}, bf16[2,128,512]{2,1,0:T(8,128)(2,1)S(1)}, u32[]{:S(2)}, u32[]{:S(2)}) %collective-permute-start.7) | collective-permute-done | bytes 262176 | tf_op jit(solution)/shard_map/ppermute | solution.py:19
  32.7 7.8 %shard_map.132 = (bf16[2,128,512]{2,1,0:T(8,128)(2,1)S(1)}, bf16[2,128,512]{2,1,0:T(8,128)(2,1)S(1)}, bf16[2,512,128]{2,1,0:T(8,128)(2,1)S(1)}, bf16[2,512,128]{...) custom-call(s32[4,8]{1,0:T(4,128)S(1)} %bitcast.2, ...), custom_call_target="tpu_custom_call" | custom-call | flops 7699999744 | bytes 700000 | tf_op jit(solution)/shard_map/pallas_call | solution.py:223
  40.5 7.8 %shard_map.131 = (bf16[2,128,512]{2,1,0:T(8,128)(2,1)S(1)}, bf16[2,128,512]{2,1,0:T(8,128)(2,1)S(1)}, bf16[2,512,128]{2,1,0:T(8,128)(2,1)S(1)}, bf16[2,512,128]{...) custom-call(s32[4,8]{1,0:T(4,128)S(1)} %bitcast.3, ...), custom_call_target="tpu_custom_call" | custom-call | flops 7699999744 | bytes 700000 | tf_op jit(solution)/shard_map/pallas_call | solution.py:223
  48.2 3.4 %shard_map.133 = (bf16[8,128,256]{2,1,0:T(8,128)(2,1)S(1)}, bf16[8,128,256]{2,1,0:T(8,128)(2,1)S(1)}) custom-call(s32[1]{0:T(128)} %bitcast.1.place_ref, bf16[2,512,512]{2,1,0:T(8,128)(2,1)} %get-tuple-element.93.xt_ref, bf16[2,512,512]{2,1,0:T(8,128)(2,1)S(1)} %get-tuple-element.94.xtp_ref, bf16[2,512,512]{2,1,0:T(8,128)(2,1)} %c_ref.5, ...), custom_call_target="tpu_custom_call" | custom-call | flops 3300000000 | bytes 300000 | tf_op jit(solution)/shard_map/pallas_call | solution.py:273
  51.7 7.8 %shard_map.134 = (bf16[2,128,512]{2,1,0:T(8,128)(2,1)S(1)}, bf16[2,128,512]{2,1,0:T(8,128)(2,1)S(1)}, bf16[2,512,128]{2,1,0:T(8,128)(2,1)S(1)}, bf16[2,512,128]{...) custom-call(s32[4,8]{1,0:T(4,128)S(1)} %bitcast.4, ...), custom_call_target="tpu_custom_call" | custom-call | flops 7699999744 | bytes 700000 | tf_op jit(solution)/shard_map/pallas_call | solution.py:223
  61.3 7.7 %shard_map.135 = (bf16[2,128,512]{2,1,0:T(8,128)(2,1)S(1)}, bf16[2,128,512]{2,1,0:T(8,128)(2,1)S(1)}, bf16[2,512,128]{2,1,0:T(8,128)(2,1)S(1)}, bf16[2,512,128]{...) custom-call(s32[4,8]{1,0:T(4,128)S(1)} %bitcast.5, ...), custom_call_target="tpu_custom_call" | custom-call | flops 7699999744 | bytes 700000 | tf_op jit(solution)/shard_map/pallas_call | solution.py:223
  69.1 3.4 %shard_map.137 = (bf16[8,128,256]{2,1,0:T(8,128)(2,1)S(1)}, bf16[8,128,256]{2,1,0:T(8,128)(2,1)S(1)}) custom-call(s32[1]{0:T(128)} %bitcast.1.place_ref, bf16[2,512,512]{2,1,0:T(8,128)(2,1)} %get-tuple-element.93.xt_ref, bf16[2,512,512]{2,1,0:T(8,128)(2,1)S(1)} %get-tuple-element.94.xtp_ref, bf16[2,512,512]{2,1,0:T(8,128)(2,1)} %c_ref.5, ...), custom_call_target="tpu_custom_call" | custom-call | flops 3300000000 | bytes 300000 | tf_op jit(solution)/shard_map/pallas_call | solution.py:273
  77.2 6.0 %collective-permute-done.11 = bf16[4,128,256]{2,1,0:T(8,128)(2,1)S(1)} collective-permute-done((bf16[4,128,256]{2,1,0:T(8,128)(2,1)S(1)}, bf16[4,128,256]{2,1,0:T(8,128)(2,1)S(1)}, u32[]{:S(2)}, u32[]{:S(2)}) %collective-permute-start.11) | collective-permute-done | bytes 262176 | tf_op jit(solution)/shard_map/ppermute | solution.py:301
  84.7 3.0 %collective-permute-start.13 = (bf16[1,128,512]{2,1,0:T(8,128)(2,1)S(1)}, bf16[1,128,512]{2,1,0:T(8,128)(2,1)S(1)}, u32[]{:S(2)}, u32[]{:S(2)}) collective-permute-start(bf16[1,128,512]{2,1,0:T(8,128)(2,1)S(1)} %get-tuple-element.146), channel_id=1, source_target_pairs={{0,8},{1,9},{2,10},{3,11},{4,12},{5,13},{6,14},{7,15},{8,0},{9,1},... | collective-permute-start | bytes 393224 | tf_op jit(solution)/shard_map/ppermute | solution.py:301
  87.8 3.2 %shard_map.136 = (bf16[2,512,512]{2,1,0:T(8,128)(2,1)}, f32[2,512,512]{2,1,0:T(8,128)S(1)}) custom-call(bf16[2,128,512]{2,1,0:T(8,128)(2,1)S(1)} %get-tuple-element.91.refs_0_, bf16[2,128,512]{2,1,0:T(8,128)(2,1)S(1)} %get-tuple-element.92.refs_1_, bf16[2,128,512]{2,1,0:T(8,128)(2,1)S(1)} %get-tuple-element.106.refs_2_.refs_0_, ...), custom_call_target="tpu_custom_call" | custom-call | flops 4400000000 | bytes 400000 | tf_op jit(solution)/shard_map/pallas_call | solution.py:399
  91.6 3.2 %collective-permute-done.12 = bf16[1,128,512]{2,1,0:T(8,128)(2,1)S(1)} collective-permute-done((bf16[1,128,512]{2,1,0:T(8,128)(2,1)S(1)}, bf16[1,128,512]{2,1,0:T(8,128)(2,1)S(1)}, u32[]{:S(2)}, u32[]{:S(2)}) %collective-permute-start.12) | collective-permute-done | bytes 131104 | tf_op jit(solution)/shard_map/ppermute | solution.py:301
  95.7 2.5 %collective-permute-start.17 = (bf16[1,128,512]{2,1,0:T(8,128)(2,1)S(1)}, bf16[1,128,512]{2,1,0:T(8,128)(2,1)S(1)}, u32[]{:S(2)}, u32[]{:S(2)}) collective-permute-start(bf16[1,128,512]{2,1,0:T(8,128)(2,1)S(1)} %get-tuple-element.143), channel_id=1, source_target_pairs={{0,12},{1,13},{2,14},{3,15},{4,8},{5,9},{6,10},{7,11},{8,4},{9,5},... | collective-permute-start | bytes 393224 | tf_op jit(solution)/shard_map/ppermute | solution.py:301
  98.2 2.0 %collective-permute-start.15 = (bf16[1,128,512]{2,1,0:T(8,128)(2,1)S(1)}, bf16[1,128,512]{2,1,0:T(8,128)(2,1)S(1)}, u32[]{:S(2)}, u32[]{:S(2)}) collective-permute-start(bf16[1,128,512]{2,1,0:T(8,128)(2,1)S(1)} %get-tuple-element.143), channel_id=1, source_target_pairs={{0,4},{1,5},{2,6},{3,7},{4,0},{5,1},{6,2},{7,3},{8,12},{9,13},{10,... | collective-permute-start | bytes 393224 | tf_op jit(solution)/shard_map/ppermute | solution.py:301
  101.0 2.4 %collective-permute-done.17 = bf16[1,128,512]{2,1,0:T(8,128)(2,1)S(1)} collective-permute-done((bf16[1,128,512]{2,1,0:T(8,128)(2,1)S(1)}, bf16[1,128,512]{2,1,0:T(8,128)(2,1)S(1)}, u32[]{:S(2)}, u32[]{:S(2)}) %collective-permute-start.17) | collective-permute-done | bytes 131104 | tf_op jit(solution)/shard_map/ppermute | solution.py:301
  103.4 3.7 %collective-permute-start.21 = (bf16[2,128,512]{2,1,0:T(8,128)(2,1)S(1)}, bf16[2,128,512]{2,1,0:T(8,128)(2,1)S(1)}, u32[]{:S(2)}, u32[]{:S(2)}) collective-permute-start(bf16[2,128,512]{2,1,0:T(8,128)(2,1)S(1)} %get-tuple-element.134), channel_id=1, source_target_pairs={{0,4},{1,5},{2,6},{3,7},{4,0},{5,1},{6,2},{7,3},{8,12},{9,13},{10,... | collective-permute-start | bytes 786440 | tf_op jit(solution)/shard_map/ppermute | solution.py:19
  109.5 4.6 %collective-permute-done.21.b2 = bf16[2,128,512]{2,1,0:T(8,128)(2,1)S(1)} collective-permute-done((bf16[2,128,512]{2,1,0:T(8,128)(2,1)S(1)}, bf16[2,128,512]{2,1,0:T(8,128)(2,1)S(1)}, u32[]{:S(2)}, u32[]{:S(2)}) %collective-permute-start.21) | collective-permute-done | bytes 262176 | tf_op jit(solution)/shard_map/ppermute | solution.py:19
  114.1 7.5 %collective-permute-done.22.b3 = bf16[2,128,512]{2,1,0:T(8,128)(2,1)S(1)} collective-permute-done((bf16[2,128,512]{2,1,0:T(8,128)(2,1)S(1)}, bf16[2,128,512]{2,1,0:T(8,128)(2,1)S(1)}, u32[]{:S(2)}, u32[]{:S(2)}) %collective-permute-start.22) | collective-permute-done | bytes 262176 | tf_op jit(solution)/shard_map/ppermute | solution.py:19
  123.6 2.6 %collective-permute-done.23.refs_1_ = bf16[8,128,512]{2,1,0:T(8,128)(2,1)S(1)} collective-permute-done((bf16[8,128,512]{2,1,0:T(8,128)(2,1)S(1)}, bf16[8,128,512]{2,1,0:T(8,128)(2,1)S(1)}, u32[]{:S(2)}, u32[]{:S(2)}) %collective-permute-start.23) | collective-permute-done | bytes 1048608 | tf_op jit(solution)/shard_map/ppermute | solution.py:301
  126.2 2.3 %shard_map.140 = (f32[512,512]{1,0:T(8,128)}, f32[512,512]{1,0:T(8,128)}, f32[512,512]{1,0:T(8,128)}, f32[512,512]{1,0:T(8,128)}) custom-call(s32[1]{0:T(128)} %bitcast.1.place_ref, bf16[8,128,512]{2,1,0:T(8,128)(2,1)S(1)} %constant_dynamic-update-slice_fusion.refs_0_, bf16[8,128,512]{2,1,0:T(8,128)(2,1)S(1)} %collective-permute-done.23.refs_1_), custom_call_target="tpu_custom_call" | custom-call | tf_op jit(solution)/shard_map/pallas_call | solution.py:343
  (69 shorter events, 20.1 us)
Async XLA Ops:
  0.6 12.6 %collective-permute-start.1 = (s32[1,4]{1,0:T(1,128)}, s32[1,4]{1,0:T(1,128)S(1)}, u32[]{:S(2)}, u32[]{:S(2)}) collective-permute-start(s32[1,4]{1,0:T(1,128)} %param.13), channel_id=1, source_target_pairs={{0,2},{1,3},{2,0},{3,1},{4,6},{5,7},{6,4},{7,5},{8,10},{9,11},{10,... | collective-permute-start | bytes 56 | tf_op jit(solution)/shard_map/ppermute | solution.py:19
  3.7 9.6 %collective-permute-start = (s32[1,4]{1,0:T(1,128)}, s32[1,4]{1,0:T(1,128)S(1)}, u32[]{:S(2)}, u32[]{:S(2)}) collective-permute-start(s32[1,4]{1,0:T(1,128)} %param.13), channel_id=1, source_target_pairs={{0,1},{1,0},{2,3},{3,2},{4,5},{5,4},{6,7},{7,6},{8,9},{9,8},{10,11... | collective-permute-start | bytes 56 | tf_op jit(solution)/shard_map/ppermute | solution.py:19
  3.7 9.6 %collective-permute-start.3 = (s32[1,4]{1,0:T(1,128)}, s32[1,4]{1,0:T(1,128)S(1)}, u32[]{:S(2)}, u32[]{:S(2)}) collective-permute-start(s32[1,4]{1,0:T(1,128)} %param.13), channel_id=1, source_target_pairs={{0,8},{1,9},{2,10},{3,11},{4,12},{5,13},{6,14},{7,15},{8,0},{9,1},... | collective-permute-start | bytes 56 | tf_op jit(solution)/shard_map/ppermute | solution.py:19
  6.3 7.0 %collective-permute-start.2 = (s32[1,4]{1,0:T(1,128)}, s32[1,4]{1,0:T(1,128)S(1)}, u32[]{:S(2)}, u32[]{:S(2)}) collective-permute-start(s32[1,4]{1,0:T(1,128)} %param.13), channel_id=1, source_target_pairs={{0,4},{1,5},{2,6},{3,7},{4,0},{5,1},{6,2},{7,3},{8,12},{9,13},{10,... | collective-permute-start | bytes 56 | tf_op jit(solution)/shard_map/ppermute | solution.py:19
  15.3 12.5 %collective-permute-start.4 = (bf16[2,128,512]{2,1,0:T(8,128)(2,1)S(1)}, bf16[2,128,512]{2,1,0:T(8,128)(2,1)S(1)}, u32[]{:S(2)}, u32[]{:S(2)}) collective-permute-start(bf16[2,128,512]{2,1,0:T(8,128)(2,1)S(1)} %get-tuple-element.83), channel_id=1, source_target_pairs={{0,1},{1,0},{2,3},{3,2},{4,5},{5,4},{6,7},{7,6},{8,9},{9,8},{10,11... | collective-permute-start | bytes 786440 | tf_op jit(solution)/shard_map/ppermute | solution.py:19
  15.4 12.4 %collective-permute-start.5 = (bf16[2,128,512]{2,1,0:T(8,128)(2,1)S(1)}, bf16[2,128,512]{2,1,0:T(8,128)(2,1)S(1)}, u32[]{:S(2)}, u32[]{:S(2)}) collective-permute-start(bf16[2,128,512]{2,1,0:T(8,128)(2,1)S(1)} %get-tuple-element.84), channel_id=1, source_target_pairs={{0,2},{1,3},{2,0},{3,1},{4,6},{5,7},{6,4},{7,5},{8,10},{9,11},{10,... | collective-permute-start | bytes 786440 | tf_op jit(solution)/shard_map/ppermute | solution.py:19
  16.0 12.8 %collective-permute-start.6 = (bf16[2,128,512]{2,1,0:T(8,128)(2,1)S(1)}, bf16[2,128,512]{2,1,0:T(8,128)(2,1)S(1)}, u32[]{:S(2)}, u32[]{:S(2)}) collective-permute-start(bf16[2,128,512]{2,1,0:T(8,128)(2,1)S(1)} %get-tuple-element.85), channel_id=1, source_target_pairs={{0,4},{1,5},{2,6},{3,7},{4,0},{5,1},{6,2},{7,3},{8,12},{9,13},{10,... | collective-permute-start | bytes 786440 | tf_op jit(solution)/shard_map/ppermute | solution.py:19
  16.4 14.7 %collective-permute-start.7 = (bf16[2,128,512]{2,1,0:T(8,128)(2,1)S(1)}, bf16[2,128,512]{2,1,0:T(8,128)(2,1)S(1)}, u32[]{:S(2)}, u32[]{:S(2)}) collective-permute-start(bf16[2,128,512]{2,1,0:T(8,128)(2,1)S(1)} %get-tuple-element.86), channel_id=1, source_target_pairs={{0,8},{1,9},{2,10},{3,11},{4,12},{5,13},{6,14},{7,15},{8,0},{9,1},... | collective-permute-start | bytes 786440 | tf_op jit(solution)/shard_map/ppermute | solution.py:19
  51.7 7.8 %collective-permute-start.8 = (bf16[8,128,256]{2,1,0:T(8,128)(2,1)S(1)}, bf16[8,128,256]{2,1,0:T(8,128)(2,1)S(1)}, u32[]{:S(2)}, u32[]{:S(2)}) collective-permute-start(bf16[8,128,256]{2,1,0:T(8,128)(2,1)S(1)} %get-tuple-element.105.refs_0_), channel_id=1, source_target_pairs={{0,1},{1,0},{2,3},{3,2},{4,5},{5,4},{6,7},{7,6},{8,9},{9,8},{10,11... | collective-permute-start | bytes 1572872 | tf_op jit(solution)/shard_map/ppermute | solution.py:301
  59.7 9.3 %collective-permute-start.9 = (bf16[4,128,256]{2,1,0:T(8,128)(2,1)S(1)}, bf16[4,128,256]{2,1,0:T(8,128)(2,1)S(1)}, u32[]{:S(2)}, u32[]{:S(2)}) collective-permute-start(bf16[4,128,256]{2,1,0:T(8,128)(2,1)S(1)} %slice.36.refs_0_), channel_id=1, source_target_pairs={{0,2},{1,3},{2,0},{3,1},{4,6},{5,7},{6,4},{7,5},{8,10},{9,11},{10,... | collective-permute-start | bytes 786440 | tf_op jit(solution)/shard_map/ppermute | solution.py:301
  72.6 2.0 %collective-permute-start.10 = (bf16[8,128,256]{2,1,0:T(8,128)(2,1)S(1)}, bf16[8,128,256]{2,1,0:T(8,128)(2,1)S(1)}, u32[]{:S(2)}, u32[]{:S(2)}) collective-permute-start(bf16[8,128,256]{2,1,0:T(8,128)(2,1)S(1)} %get-tuple-element.121), channel_id=1, source_target_pairs={{0,1},{1,0},{2,3},{3,2},{4,5},{5,4},{6,7},{7,6},{8,9},{9,8},{10,11... | collective-permute-start | bytes 1572872 | tf_op jit(solution)/shard_map/ppermute | solution.py:301
  74.7 8.5 %collective-permute-start.11 = (bf16[4,128,256]{2,1,0:T(8,128)(2,1)S(1)}, bf16[4,128,256]{2,1,0:T(8,128)(2,1)S(1)}, u32[]{:S(2)}, u32[]{:S(2)}) collective-permute-start(bf16[4,128,256]{2,1,0:T(8,128)(2,1)S(1)} %slice.39), channel_id=1, source_target_pairs={{0,2},{1,3},{2,0},{3,1},{4,6},{5,7},{6,4},{7,5},{8,10},{9,11},{10,... | collective-permute-start | bytes 786440 | tf_op jit(solution)/shard_map/ppermute | solution.py:301
  83.3 8.3 %collective-permute-start.14 = (bf16[1,128,512]{2,1,0:T(8,128)(2,1)S(1)}, bf16[1,128,512]{2,1,0:T(8,128)(2,1)S(1)}, u32[]{:S(2)}, u32[]{:S(2)}) collective-permute-start(bf16[1,128,512]{2,1,0:T(8,128)(2,1)S(1)} %get-tuple-element.144), channel_id=1, source_target_pairs={{0,12},{1,13},{2,14},{3,15},{4,8},{5,9},{6,10},{7,11},{8,4},{9,5},... | collective-permute-start | bytes 393224 | tf_op jit(solution)/shard_map/ppermute | solution.py:301
  84.7 10.1 %collective-permute-start.12 = (bf16[1,128,512]{2,1,0:T(8,128)(2,1)S(1)}, bf16[1,128,512]{2,1,0:T(8,128)(2,1)S(1)}, u32[]{:S(2)}, u32[]{:S(2)}) collective-permute-start(bf16[1,128,512]{2,1,0:T(8,128)(2,1)S(1)} %get-tuple-element.145), channel_id=1, source_target_pairs={{0,4},{1,5},{2,6},{3,7},{4,0},{5,1},{6,2},{7,3},{8,12},{9,13},{10,... | collective-permute-start | bytes 393224 | tf_op jit(solution)/shard_map/ppermute | solution.py:301
  84.7 10.9 %collective-permute-start.13 = (bf16[1,128,512]{2,1,0:T(8,128)(2,1)S(1)}, bf16[1,128,512]{2,1,0:T(8,128)(2,1)S(1)}, u32[]{:S(2)}, u32[]{:S(2)}) collective-permute-start(bf16[1,128,512]{2,1,0:T(8,128)(2,1)S(1)} %get-tuple-element.146), channel_id=1, source_target_pairs={{0,8},{1,9},{2,10},{3,11},{4,12},{5,13},{6,14},{7,15},{8,0},{9,1},... | collective-permute-start | bytes 393224 | tf_op jit(solution)/shard_map/ppermute | solution.py:301
  95.7 7.7 %collective-permute-start.17 = (bf16[1,128,512]{2,1,0:T(8,128)(2,1)S(1)}, bf16[1,128,512]{2,1,0:T(8,128)(2,1)S(1)}, u32[]{:S(2)}, u32[]{:S(2)}) collective-permute-start(bf16[1,128,512]{2,1,0:T(8,128)(2,1)S(1)} %get-tuple-element.143), channel_id=1, source_target_pairs={{0,12},{1,13},{2,14},{3,15},{4,8},{5,9},{6,10},{7,11},{8,4},{9,5},... | collective-permute-start | bytes 393224 | tf_op jit(solution)/shard_map/ppermute | solution.py:301
  98.2 9.9 %collective-permute-start.16 = (bf16[1,128,512]{2,1,0:T(8,128)(2,1)S(1)}, bf16[1,128,512]{2,1,0:T(8,128)(2,1)S(1)}, u32[]{:S(2)}, u32[]{:S(2)}) collective-permute-start(bf16[1,128,512]{2,1,0:T(8,128)(2,1)S(1)} %get-tuple-element.143), channel_id=1, source_target_pairs={{0,8},{1,9},{2,10},{3,11},{4,12},{5,13},{6,14},{7,15},{8,0},{9,1},... | collective-permute-start | bytes 393224 | tf_op jit(solution)/shard_map/ppermute | solution.py:301
  98.2 10.1 %collective-permute-start.15 = (bf16[1,128,512]{2,1,0:T(8,128)(2,1)S(1)}, bf16[1,128,512]{2,1,0:T(8,128)(2,1)S(1)}, u32[]{:S(2)}, u32[]{:S(2)}) collective-permute-start(bf16[1,128,512]{2,1,0:T(8,128)(2,1)S(1)} %get-tuple-element.143), channel_id=1, source_target_pairs={{0,4},{1,5},{2,6},{3,7},{4,0},{5,1},{6,2},{7,3},{8,12},{9,13},{10,... | collective-permute-start | bytes 393224 | tf_op jit(solution)/shard_map/ppermute | solution.py:301
  100.2 9.3 %collective-permute-start.19 = (bf16[2,128,512]{2,1,0:T(8,128)(2,1)S(1)}, bf16[2,128,512]{2,1,0:T(8,128)(2,1)S(1)}, u32[]{:S(2)}, u32[]{:S(2)}) collective-permute-start(bf16[2,128,512]{2,1,0:T(8,128)(2,1)S(1)} %get-tuple-element.132), channel_id=1, source_target_pairs={{0,1},{1,0},{2,3},{3,2},{4,5},{5,4},{6,7},{7,6},{8,9},{9,8},{10,11... | collective-permute-start | bytes 786440 | tf_op jit(solution)/shard_map/ppermute | solution.py:19
  100.2 9.3 %collective-permute-start.20 = (bf16[2,128,512]{2,1,0:T(8,128)(2,1)S(1)}, bf16[2,128,512]{2,1,0:T(8,128)(2,1)S(1)}, u32[]{:S(2)}, u32[]{:S(2)}) collective-permute-start(bf16[2,128,512]{2,1,0:T(8,128)(2,1)S(1)} %get-tuple-element.133), channel_id=1, source_target_pairs={{0,2},{1,3},{2,0},{3,1},{4,6},{5,7},{6,4},{7,5},{8,10},{9,11},{10,... | collective-permute-start | bytes 786440 | tf_op jit(solution)/shard_map/ppermute | solution.py:19
  103.4 10.7 %collective-permute-start.21 = (bf16[2,128,512]{2,1,0:T(8,128)(2,1)S(1)}, bf16[2,128,512]{2,1,0:T(8,128)(2,1)S(1)}, u32[]{:S(2)}, u32[]{:S(2)}) collective-permute-start(bf16[2,128,512]{2,1,0:T(8,128)(2,1)S(1)} %get-tuple-element.134), channel_id=1, source_target_pairs={{0,4},{1,5},{2,6},{3,7},{4,0},{5,1},{6,2},{7,3},{8,12},{9,13},{10,... | collective-permute-start | bytes 786440 | tf_op jit(solution)/shard_map/ppermute | solution.py:19
  108.1 13.5 %collective-permute-start.22 = (bf16[2,128,512]{2,1,0:T(8,128)(2,1)S(1)}, bf16[2,128,512]{2,1,0:T(8,128)(2,1)S(1)}, u32[]{:S(2)}, u32[]{:S(2)}) collective-permute-start(bf16[2,128,512]{2,1,0:T(8,128)(2,1)S(1)} %get-tuple-element.135), channel_id=1, source_target_pairs={{0,8},{1,9},{2,10},{3,11},{4,12},{5,13},{6,14},{7,15},{8,0},{9,1},... | collective-permute-start | bytes 786440 | tf_op jit(solution)/shard_map/ppermute | solution.py:19
  108.4 15.0 %collective-permute-start.18 = (bf16[4,128,512]{2,1,0:T(8,128)(2,1)S(1)}, bf16[4,128,512]{2,1,0:T(8,128)(2,1)S(1)}, u32[]{:S(2)}, u32[]{:S(2)}) collective-permute-start(bf16[4,128,512]{2,1,0:T(8,128)(2,1)S(1)} %pad_maximum_fusion), channel_id=1, source_target_pairs={{0,2},{1,3},{2,0},{3,1},{4,6},{5,7},{6,4},{7,5},{8,10},{9,11},{10,... | collective-permute-start | bytes 1572872 | tf_op jit(solution)/shard_map/ppermute | solution.py:301
  123.5 2.7 %collective-permute-start.23 = (bf16[8,128,512]{2,1,0:T(8,128)(2,1)S(1)}, bf16[8,128,512]{2,1,0:T(8,128)(2,1)S(1)}, u32[]{:S(2)}, u32[]{:S(2)}) collective-permute-start(bf16[8,128,512]{2,1,0:T(8,128)(2,1)S(1)} %constant_dynamic-update-slice_fusion.refs_0_), channel_id=1, source_target_pairs={{0,1},{1,0},{2,3},{3,2},{4,5},{5,4},{6,7},{7,6},{8,9},{9,8},{10,11... | collective-permute-start | bytes 3145736 | tf_op jit(solution)/shard_map/ppermute | solution.py:301
  (9 other events, 99.0 us)

commit v3 on v2

--- a/solution.py
+++ b/solution.py
@@ -9,10 +9,12 @@
 
 SUB = 128
 CHUNKS = ((0, 1), (2, 3))
-VMEM = 24 * 1024 * 1024
+VMEM = 14 * 1024 * 1024
 F32 = jnp.float32
 BF16 = jnp.bfloat16
 OFF = 1e30
+TILE = 128
+DONE = object()
 
 
 def partner(x, stride):
@@ -45,6 +47,10 @@
 
 def far(*arrays):
     return [pltpu.with_memory_space_constraint(x, pltpu.HBM) for x in arrays]
+
+
+def near(*arrays):
+    return [pltpu.with_memory_space_constraint(x, pltpu.VMEM) for x in arrays]
 
 
 def head_rows(pair_rows, which, head_width):
@@ -86,151 +92,295 @@
     )(*far(tokens, cotangent, w_query, w_key, w_value, w_out))
 
 
-def project_partner_kernel(x0, x1, x2, x3, wk_ref, wv_ref, k_ref, v_ref, kt_ref, vt_ref, xt_ref):
-    x = jnp.concatenate([x0[0], x1[0], x2[0], x3[0]], 0)
-    xt_ref[0] = x.T
-    k = nn(x, wk_ref[...])
-    v = nn(x, wv_ref[...])
-    k_ref[0] = k.astype(BF16)
-    v_ref[0] = v.astype(BF16)
-    kt_ref[0] = k.T.astype(BF16)
-    vt_ref[0] = v.T.astype(BF16)
-
-
-def project_partner(arrived, w_key, w_value):
+def bring(sources, targets, sem):
+    copies = [pltpu.make_async_copy(src, dst, sem.at[i]) for i, (src, dst) in enumerate(zip(sources, targets))]
+    for copy in copies:
+        copy.start()
+    return copies
+
+
+def project_partner_kernel(loads, x0, x1, x2, x3, wk_ref, wv_ref, *refs):
+    k_ref, v_ref, kt_ref, vt_ref, xt_ref, *targets, sem = refs[-6 - loads :]
+    sources = refs[:loads]
+    copies = bring([sources[0].at[0], *sources[1:]], targets, sem)
+    for s in range(x0.shape[0]):
+        x = jnp.concatenate([x0[s], x1[s], x2[s], x3[s]], 0)
+        xt_ref[s] = x.T
+        k = nn(x, wk_ref[...])
+        v = nn(x, wv_ref[...])
+        k_ref[s] = k.astype(BF16)
+        v_ref[s] = v.astype(BF16)
+        kt_ref[s] = k.T.astype(BF16)
+        vt_ref[s] = v.T.astype(BF16)
+    for copy in copies:
+        copy.wait()
+
+
+def project_partner(arrived, w_key, w_value, loads, held):
     samples, sub_rows, width = arrived[0].shape
     rows = sub_rows * len(arrived)
-    part = pl.BlockSpec((1, sub_rows, width), lambda s: (s, 0, 0))
-    row_block = pl.BlockSpec((1, rows, width), lambda s: (s, 0, 0))
-    col_block = pl.BlockSpec((1, width, rows), lambda s: (s, 0, 0))
-    whole = pl.BlockSpec((width, width), lambda s: (0, 0))
+    whole = pl.BlockSpec(memory_space=pltpu.VMEM)
+    weight = pl.BlockSpec((width, width), lambda: (0, 0))
+    anywhere = pl.BlockSpec(memory_space=pl.ANY)
     by_row = pltpu.VMEM((samples, rows, width), BF16)
     by_col = pltpu.VMEM((samples, width, rows), BF16)
     return pl.pallas_call(
-        project_partner_kernel,
-        grid=(samples,),
-        in_specs=[part] * 4 + [whole] * 2,
-        out_specs=[row_block, row_block, col_block, col_block, col_block],
-        out_shape=[by_row, by_row, by_col, by_col, by_col],
+        functools.partial(project_partner_kernel, len(loads)),
+        in_specs=[whole] * 4 + [weight] * 2 + [anywhere] * len(loads) + [whole] * len(held),
+        out_specs=[whole] * (5 + len(loads)),
+        out_shape=[by_row, by_row, by_col, by_col, by_col, pltpu.VMEM(loads[0].shape[1:], BF16)]
+        + [pltpu.VMEM(x.shape, x.dtype) for x in loads[1:]],
+        scratch_shapes=[pltpu.SemaphoreType.DMA((len(loads),))],
         cost_estimate=cost(2.5),
-        compiler_params=params("arbitrary"),
-    )(*arrived, w_key, w_value)
-
-
-def own_kernel(head_width, qt_ref, k_ref, vt_ref, e_ref, o_ref, st_ref):
-    k = k_ref[0]
-    for which in range(2):
-        s = nn(k, head_rows(qt_ref[0], which, head_width))
-        top = jnp.max(s, axis=0, keepdims=True)
-        e = jnp.exp(s - top)
-        total = jnp.sum(e, axis=0, keepdims=True)
-        e = e.astype(BF16)
-        e_ref[0, which] = e
-        o_ref[0, which] = nn(vt_ref[0, which * head_width : (which + 1) * head_width, :], e)
-        st_ref[0, which] = jnp.concatenate([top, total, jnp.zeros((6, top.shape[1]), F32)], 0)
-
-
-def own_part(qt, k, vt, head_count):
+        compiler_params=params(),
+    )(*near(*arrived), *far(w_key, w_value, *loads), *near(*held))
+
+
+def weave(*streams):
+    streams = [iter(x) for x in streams]
+    while streams:
+        streams = [x for x in streams if next(x, DONE) is not DONE]
+
+
+def down8(x, op):
+    return op(x.reshape(x.shape[0] // 8, 8, x.shape[1]), axis=0)
+
+
+def own_kernel(head_width, qt_ref, k_ref, vt_ref, *refs):
+    loads = (len(refs) - 5) // 2
+    e_ref, o_ref, st_ref, *targets, s_ref, sem = refs[loads:]
+    copies = [pltpu.make_async_copy(src, dst, sem.at[i]) for i, (src, dst) in enumerate(zip(refs[:loads], targets))]
+
+    @pl.when(pl.program_id(0) == 0)
+    def _():
+        for copy in copies:
+            copy.start()
+
+    samples, width, rows = qt_ref.shape
+    units = [(sample, which) for sample in range(samples) for which in range(2)]
+
+    def one_pair(pair):
+        first = pl.multiple_of(pair * 2 * head_width, 2 * head_width)
+        tops = {}
+
+        def score(unit):
+            sample, which = unit
+            half = head_rows(qt_ref[sample, pl.ds(first, 2 * head_width), :], which, head_width)
+            top = None
+            for at in range(0, rows, TILE):
+                s = nn(k_ref[sample, at : at + TILE, pl.ds(first, 2 * head_width)], half)
+                s_ref[which, at : at + TILE, :] = s
+                part = down8(s, jnp.max)
+                top = part if top is None else jnp.maximum(top, part)
+                yield
+            tops[unit] = jnp.max(top, axis=0, keepdims=True)
+
+        def expo(unit):
+            sample, which = unit
+            cols = slice(which * rows, (which + 1) * rows)
+            total = None
+            for at in range(0, rows, TILE):
+                e = jnp.exp(s_ref[which, at : at + TILE, :] - tops[unit])
+                part = down8(e, jnp.sum)
+                total = part if total is None else total + part
+                e_ref[0, sample, at : at + TILE, cols] = e.astype(BF16)
+                yield
+            total = jnp.sum(total, axis=0, keepdims=True)
+            st_ref[sample, 2 * pair + which] = jnp.concatenate([tops[unit], total, jnp.zeros((6, rows), F32)], 0)
+
+        def out(unit):
+            sample, which = unit
+            cols = slice(which * rows, (which + 1) * rows)
+            span = pl.ds(first + which * head_width, head_width)
+            o_ref[sample, 2 * pair + which] = nn(vt_ref[sample, span, :], e_ref[0, sample, :, cols])
+            yield
+
+        count = len(units)
+        for i in range(count + 2):
+            streams = []
+            if i < count:
+                streams.append(score(units[i]))
+            if 1 <= i <= count:
+                streams.append(expo(units[i - 1]))
+            if i >= 2:
+                streams.append(out(units[i - 2]))
+            weave(*streams)
+
+    one_pair(pl.program_id(0))
+
+    @pl.when(pl.program_id(0) == pl.num_programs(0) - 1)
+    def _():
+        for copy in copies:
+            copy.wait()
+
+
+def own_part(qt, k, vt, head_count, loads):
     samples, width, rows = qt.shape
     head_width = width // head_count
-    col_pair = pl.BlockSpec((1, 2 * head_width, rows), lambda p, s: (s, p, 0))
-    row_pair = pl.BlockSpec((1, rows, 2 * head_width), lambda p, s: (s, 0, p))
-
-    def per_head(n):
-        return pl.BlockSpec((1, 2, n, rows), lambda p, s: (s, p, 0, 0))
-
+    whole = pl.BlockSpec(memory_space=pltpu.VMEM)
     return pl.pallas_call(
         functools.partial(own_kernel, head_width),
-        grid=(head_count // 2, samples),
-        in_specs=[col_pair, row_pair, col_pair],
-        out_specs=[per_head(rows), per_head(head_width), per_head(8)],
+        grid=(head_count // 2,),
+        in_specs=[whole] * 3 + [pl.BlockSpec(memory_space=pl.ANY)] * len(loads),
+        out_specs=[pl.BlockSpec((1, samples, rows, 2 * rows), lambda p: (p, 0, 0, 0))] + [whole] * (2 + len(loads)),
         out_shape=[
-            pltpu.HBM((samples, head_count, rows, rows), BF16),
-            pltpu.HBM((samples, head_count, head_width, rows), F32),
-            pltpu.HBM((samples, head_count, 8, rows), F32),
-        ],
+            pltpu.HBM((head_count // 2, samples, rows, 2 * rows), BF16),
+            pltpu.VMEM((samples, head_count, head_width, rows), F32),
+            pltpu.VMEM((samples, head_count, 8, rows), F32),
+        ]
+        + [pltpu.VMEM(x.shape, x.dtype) for x in loads],
+        scratch_shapes=[pltpu.VMEM((2, rows, rows), F32), pltpu.SemaphoreType.DMA((len(loads),))],
         cost_estimate=cost(10),
-        compiler_params=params("arbitrary", "arbitrary"),
-    )(qt, k, vt)
+        compiler_params=params("arbitrary"),
+    )(*near(qt, k, vt), *far(*loads))
 
 
 def attend_kernel(
-    pair, head_width, scale, mask_ref, e_ref, o_ref, st_ref, qt_ref, dot_ref, ko_ref, vo_ref, kto_ref, kp_ref, vp_ref, ktp_ref,
+    pair, head_width, scale, mask_ref, e_ref, o_ref, st_ref, qt_ref, dot_ref, vo_ref, kto_ref, kp_ref, vp_ref, ktp_ref,
     vtp_ref, *refs,
 ):
-    ctx_ref, dqt_ref, dko_ref, dvo_ref, dkp_ref, dvp_ref = refs[-6:]
+    s_ref, ep_ref, dsp_ref, dso_ref, ops_ref, sem = refs[-6:]
+    loads = sem.shape[0]
+    targets = refs[-6 - loads : -6]
+    ctx_ref, dqt_ref, dko_ref, dvo_ref, dkp_ref, dvp_ref = refs[-12 - loads : -6 - loads]
+    sources = [x.at[pair + 1] if len(x.shape) == 4 else x for x in refs[:loads]]
+    copies = bring(sources, targets, sem)
     sections = mask_ref.shape[0]
+    samples, _, rows = qt_ref.shape
     sub = kp_ref.shape[1] // sections
-    ko, vo, kp, vp = ko_ref[0], vo_ref[0], kp_ref[0], vp_ref[0]
-    dko = dvo = dkp = dvp = None
-    for which in range(2):
-        rows = slice(which * head_width, (which + 1) * head_width)
-        q_half = head_rows(qt_ref[0], which, head_width)
-        s = nn(kp, q_half)
-        top_own = st_ref[0, which, 0:1, :]
-        total_own = st_ref[0, which, 1:2, :]
-        offs = [jnp.where(mask_ref[i, 2 * pair + which] > 0, 0.0, OFF).astype(F32) for i in range(sections)]
-        top = top_own
+    both = slice(pair * 2 * head_width, (pair + 1) * 2 * head_width)
+    stats = {}
+
+    def span(which):
+        return slice((2 * pair + which) * head_width, (2 * pair + which + 1) * head_width)
+
+    def cols(which):
+        return slice(which * rows, (which + 1) * rows)
+
+    def score(unit):
+        sample, which = unit
+        kept = stats[unit] = {}
+        kept["q"] = head_rows(qt_ref[sample, both, :], which, head_width)
+        kept["g"] = head_rows(dot_ref[sample, both, :], which, head_width)
+        kept["off"] = [jnp.where(mask_ref[i, 2 * pair + which] > 0, 0.0, OFF).astype(F32) for i in range(sections)]
+        top = None
         for i in range(sections):
-            top = jnp.maximum(top, jnp.max(s[i * sub : (i + 1) * sub], axis=0, keepdims=True) - offs[i])
-        e_part = jnp.concatenate([jnp.exp(s[i * sub : (i + 1) * sub] - (top + offs[i])) for i in range(sections)], 0)
-        fade = jnp.exp(top_own - top)
-        total = fade * total_own + jnp.sum(e_part, axis=0, keepdims=True)
-        e_part = e_part.astype(BF16)
-        e_own = e_ref[0, which]
-        inverse = 1.0 / total
-        o = fade * o_ref[0, which] + nn(vtp_ref[0, rows, :], e_part)
+            at = slice(i * sub, (i + 1) * sub)
+            s = nn(kp_ref[sample, at, both], kept["q"])
+            s_ref[which, at, :] = s
+            part = down8(s, jnp.max) - kept["off"][i]
+            top = part if top is None else jnp.maximum(top, part)
+            yield
+        top_own = st_ref[sample, 2 * pair + which, 0:1, :]
+        kept["top"] = jnp.maximum(top_own, jnp.max(top, axis=0, keepdims=True))
+        kept["fade"] = jnp.exp(top_own - kept["top"])
+
+    def expo(unit):
+        sample, which = unit
+        kept = stats[unit]
+        total = None
+        for i in range(sections):
+            at = slice(i * sub, (i + 1) * sub)
+            e = jnp.exp(s_ref[which, at, :] - (kept["top"] + kept["off"][i]))
+            part = down8(e, jnp.sum)
+            total = part if total is None else total + part
+            ep_ref[sample, at, cols(which)] = e.astype(BF16)
+            yield
+        total = jnp.sum(total, axis=0, keepdims=True) + kept["fade"] * st_ref[sample, 2 * pair + which, 1:2, :]
+        kept["inverse"] = 1.0 / total
+
+    def blend(unit):
+        sample, which = unit
+        kept = stats[unit]
+        inverse, fade = kept["inverse"], kept["fade"]
+        here = slice(which * head_width, (which + 1) * head_width)
+        o = fade * o_ref[sample, 2 * pair + which] + nn(vtp_ref[sample, span(which), :], ep_ref[sample, :, cols(which)])
         ctx = (o * inverse).astype(BF16)
-        ctx_ref[0, rows, :] = ctx
-        ctx = ctx.astype(F32)
-        g = dot_ref[0, rows, :].astype(F32)
-        g_part = (g * inverse).astype(BF16)
-        g_own = (g * (inverse * fade)).astype(BF16)
-        r_part = jnp.sum(g_part.astype(F32) * ctx, axis=0, keepdims=True)
-        r_own = jnp.sum(g_own.astype(F32) * ctx, axis=0, keepdims=True)
-        blank = jnp.zeros_like(g_part)
-        g_part = jnp.concatenate([g_part, blank] if which == 0 else [blank, g_part], 0)
-        g_own = jnp.concatenate([g_own, blank] if which == 0 else [blank, g_own], 0)
-        ds_part = ((nn(vp, g_part) - r_part).astype(BF16) * e_part)
-        ds_own = ((nn(vo, g_own) - r_own).astype(BF16) * e_own)
-        dqt_ref[0, rows, :] = ((nn(kto_ref[0, rows, :], ds_own) + nn(ktp_ref[0, rows, :], ds_part)) * scale).astype(BF16)
-        terms = (nt(ds_own, q_half), nt(e_own, g_own), nt(ds_part, q_half), nt(e_part, g_part))
-        if which == 0:
-            dko, dvo, dkp, dvp = terms
-        else:
-            dko, dvo, dkp, dvp = dko + terms[0], dvo + terms[1], dkp + terms[2], dvp + terms[3]
-    dko_ref[0] = dko.astype(BF16)
-    dvo_ref[0] = dvo.astype(BF16)
-    dkp_ref[0] = dkp.astype(BF16)
-    dvp_ref[0] = dvp.astype(BF16)
-
-
-def attend(pair, head_masks, own, qt, dot, ko, vo, kto, partner_rows, head_count, scale, after):
-    e, o, st = own
+        ctx_ref[sample, here, :] = ctx
+        g = dot_ref[sample, span(which), :].astype(F32)
+        kept["r"] = jnp.sum(g * ctx.astype(F32), axis=0, keepdims=True)
+        q32, g32 = kept["q"].astype(F32), kept["g"].astype(F32)
+        ops_ref[sample, 0, :, cols(which)] = (q32 * inverse).astype(BF16)
+        ops_ref[sample, 1, :, cols(which)] = (g32 * inverse).astype(BF16)
+        ops_ref[sample, 2, :, cols(which)] = (q32 * (inverse * fade)).astype(BF16)
+        ops_ref[sample, 3, :, cols(which)] = (g32 * (inverse * fade)).astype(BF16)
+        yield
+
+    def slope(unit):
+        sample, which = unit
+        kept = stats[unit]
+        for v_ref, get, put_ref in ((vp_ref, ep_ref.at[sample], dsp_ref), (vo_ref, e_ref.at[sample], dso_ref)):
+            for lo in range(0, rows, TILE):
+                at = slice(lo, lo + TILE)
+                dp = nn(v_ref[sample, at, both], kept["g"]) - kept["r"]
+                put_ref[sample, at, cols(which)] = dp.astype(BF16) * get[at, cols(which)]
+                yield
+
+    def query(unit):
+        sample, which = unit
+        kept = stats[unit]
+        dq = nn(ktp_ref[sample, span(which), :], dsp_ref[sample, :, cols(which)])
+        yield
+        dq = dq + kept["fade"] * nn(kto_ref[sample, span(which), :], dso_ref[sample, :, cols(which)])
+        here = slice(which * head_width, (which + 1) * head_width)
+        dqt_ref[sample, here, :] = (dq * (kept["inverse"] * scale)).astype(BF16)
+
+    def keys(sample):
+        jobs = (
+            (dvp_ref, ep_ref.at[sample], 1),
+            (dvo_ref, e_ref.at[sample], 3),
+            (dkp_ref, dsp_ref.at[sample], 0),
+            (dko_ref, dso_ref.at[sample], 2),
+        )
+        for out_ref, left, number in jobs:
+            for lo in range(0, rows, TILE):
+                at = slice(lo, lo + TILE)
+                out_ref[sample, at, :] = nt(left[at, :], ops_ref[sample, number]).astype(BF16)
+                yield
+
+    def chain(*streams):
+        for stream in streams:
+            yield from stream
+
+    for sample in range(samples):
+        one, two = (sample, 0), (sample, 1)
+        before = keys(sample - 1) if sample else iter(())
+        weave(score(one), before)
+        weave(score(two), expo(one), before)
+        weave(blend(one))
+        weave(slope(one), expo(two), before)
+        weave(blend(two), before)
+        weave(slope(two), query(one), before)
+        weave(query(two), before)
+    weave(keys(samples - 1))
+    for copy in copies:
+        copy.wait()
+
+
+def attend(pair, head_masks, e, stats, qt, dot, vo, kto, partner_rows, head_count, scale, loads, held, after):
     kp, vp, ktp, vtp = partner_rows
     samples, width, rows = qt.shape
     head_width = width // head_count
-    col_in = pl.BlockSpec((1, 2 * head_width, rows), lambda s: (s, pair, 0))
-    row_in = pl.BlockSpec((1, rows, 2 * head_width), lambda s: (s, 0, pair))
-    col_out = pl.BlockSpec((1, 2 * head_width, rows), lambda s: (s, 0, 0))
-    row_out = pl.BlockSpec((1, rows, 2 * head_width), lambda s: (s, 0, 0))
-
-    def per_head(n):
-        return pl.BlockSpec((1, 2, n, rows), lambda s: (s, pair, 0, 0))
-
+    whole = pl.BlockSpec(memory_space=pltpu.VMEM)
+    anywhere = pl.BlockSpec(memory_space=pl.ANY)
     by_col = pltpu.VMEM((samples, 2 * head_width, rows), BF16)
     by_row = pltpu.VMEM((samples, rows, 2 * head_width), BF16)
     return pl.pallas_call(
         functools.partial(attend_kernel, pair, head_width, scale),
-        grid=(samples,),
-        in_specs=[pl.BlockSpec(memory_space=pltpu.SMEM), per_head(rows), per_head(head_width), per_head(8)]
-        + [col_in, col_in, row_in, row_in, col_in, row_in, row_in, col_in, col_in]
-        + [pl.BlockSpec(memory_space=pl.ANY)] * len(after),
-        out_specs=[col_out, col_out] + [row_out] * 4,
-        out_shape=[by_col, by_col] + [by_row] * 4,
-        cost_estimate=cost(7),
-        compiler_params=params("arbitrary"),
-    )(head_masks, *far(e, o, st), qt, *far(dot), ko, *far(vo, kto), kp, vp, ktp, vtp, *after)
+        in_specs=[pl.BlockSpec(memory_space=pltpu.SMEM)] + [whole] * 11 + [anywhere] * len(loads) + [whole] * len(held) + [anywhere] * len(after),
+        out_specs=[whole] * (6 + len(loads)),
+        out_shape=[by_col, by_col] + [by_row] * 4 + [pltpu.VMEM(x.shape[-4 + (x.ndim == 4) :], x.dtype) for x in loads],
+        scratch_shapes=[
+            pltpu.VMEM((2, rows, rows), F32),
+            pltpu.VMEM((samples, rows, 2 * rows), BF16),
+            pltpu.VMEM((samples, rows, 2 * rows), BF16),
+            pltpu.VMEM((samples, rows, 2 * rows), BF16),
+            pltpu.VMEM((samples, 4, 2 * head_width, 2 * rows), BF16),
+            pltpu.SemaphoreType.DMA((max(len(loads), 1),)) if loads else pltpu.SemaphoreType.DMA((0,)),
+        ],
+        cost_estimate=cost(6),
+        compiler_params=params(),
+    )(head_masks, *near(e, *stats, qt, dot, vo, kto, kp, vp, ktp, vtp), *far(*loads), *near(*held), *after)
 
 
 def weights_kernel(pairs, place_ref, xt_ref, xtp_ref, c_ref, *refs):
@@ -272,12 +422,12 @@
     whole = pl.BlockSpec(memory_space=pltpu.VMEM)
     return pl.pallas_call(
         functools.partial(weights_kernel, pairs),
-        in_specs=[pl.BlockSpec(memory_space=pltpu.SMEM)] + [pl.BlockSpec(xt.shape, lambda: (0, 0, 0)), whole, pl.BlockSpec(cotangent.shape, lambda: (0, 0, 0))] + [whole] * (6 * pairs) + [pl.BlockSpec(memory_space=pl.ANY)] * len(after),
+        in_specs=[pl.BlockSpec(memory_space=pltpu.SMEM)] + [whole] * 3 + [whole] * (6 * pairs) + [pl.BlockSpec(memory_space=pl.ANY)] * len(after),
         out_shape=[half, half],
         scratch_shapes=[pltpu.VMEM((devices, 4 * width // devices, cols), BF16)],
         cost_estimate=cost(3),
         compiler_params=params(),
-    )(place, *far(xt), xtp, *far(cotangent), *[x for part in parts for x in part], *after)
+    )(place, *near(xt, xtp, cotangent), *[x for part in parts for x in part], *after)
 
 
 def plan_of(levels):
@@ -321,15 +471,16 @@
     return lax.optimization_barrier(values)
 
 
-def spread_kernel(groups, place_ref, *refs):
+def spread_kernel(groups, count, place_ref, *refs):
     piece_refs, out_refs, all_ref = refs[:-5], refs[-5:-1], refs[-1]
     per_type, width = all_ref.shape[0] // 4, all_ref.shape[2]
     cols = width // groups
-    slot = 0
-    for ref in piece_refs:
-        for i in range(ref.shape[0]):
-            all_ref[slot ^ place_ref[0]] = ref[i].astype(F32)
-            slot += 1
+    for g in range(groups):
+        slot = 0
+        for ref in piece_refs[g * count : (g + 1) * count]:
+            for i in range(ref.shape[0]):
+                all_ref[slot ^ place_ref[0], :, g * cols : (g + 1) * cols] = ref[i].astype(F32)
+                slot += 1
     for kind in range(3):
         out_refs[kind][...] = all_ref[kind * per_type : (kind + 1) * per_type].reshape(width, width)
     last = all_ref[3 * per_type :].reshape(groups, cols, width)
@@ -340,13 +491,14 @@
 
 def spread_grads(place, devices, width, pieces):
     whole = pl.BlockSpec(memory_space=pltpu.VMEM)
-    return pl.pallas_call(
-        functools.partial(spread_kernel, len(CHUNKS)),
-        in_specs=[pl.BlockSpec(memory_space=pltpu.SMEM)] + [whole] * len(pieces),
+    groups, count = len(pieces), len(pieces[0])
+    return pl.pallas_call(
+        functools.partial(spread_kernel, groups, count),
+        in_specs=[pl.BlockSpec(memory_space=pltpu.SMEM)] + [whole] * (groups * count),
         out_shape=[jax.ShapeDtypeStruct((width, width), F32)] * 4,
         scratch_shapes=[pltpu.VMEM((devices, 4 * width // devices, width), F32)],
         compiler_params=params(),
-    )(place, *pieces)
+    )(place, *[piece for group in pieces for piece in group])
 
 
 def back_kernel(groups, *refs):
@@ -456,50 +608,76 @@
     place = place_of(plan)
     scale = (width // head_count) ** -0.5
     theirs = [partner(partner_block, levels - 4 + section) for section in range(4)]
-    qt, ko, vo, kto, vto, dot, xt = project(tokens, cotangent, w_query, w_key, w_value, w_out, scale)
-    arrived = [partner(piece, levels - 4 + section) for section, piece in enumerate(pick(theirs, tokens))]
-    own = own_part(qt, ko, vto, head_count)
-    *partner_rows, xtp = project_partner(arrived, w_key, w_value)
-    def run(pair, after=()):
-        return attend(pair, head_masks[0], own, qt, dot, ko, vo, kto, partner_rows, head_count, scale, after)
+    picked = pick(theirs, tokens)
+    first_tokens, *picked = tie(tokens, *picked)
+    arrived = [partner(piece, levels - 4 + section) for section, piece in enumerate(picked)]
+    qt, ko, vo, kto, vto, dot, xt = project(first_tokens, cotangent, w_query, w_key, w_value, w_out, scale)
+    e_all, *stats, vo, kto, dot = own_part(qt, ko, vto, head_count, [vo, kto, dot])
+    kp, vp, ktp, vtp, xtp, e = project_partner(arrived, w_key, w_value, [e_all], [*stats, qt, vo, kto, dot])
+
+    def run(pair, e, loads, held, after=()):
+        out = attend(
+            pair, head_masks[0], e, stats, qt, dot, vo, kto, (kp, vp, ktp, vtp), head_count, scale, loads, held, after
+        )
+        return out[:6], *out[6:]
 
     def weigh(parts, after=()):
-        return weight_grads(place, devices, xt, xtp, cotangent, list(zip(*parts)), after)
-
-    first = [run(pair) for pair in CHUNKS[0]]
+        return weight_grads(place, devices, xt, xtp, cot, list(zip(*parts)), after)
+
+    p0, e, xt = run(0, e, [e_all, xt], [xtp])
+    p1, e, cot = run(1, e, [e_all, cotangent], [xtp, xt])
+    first, second = [p0, p1], []
     kept0, sends0 = weigh(first)
     came = send_all([sends0], plan[0])
-    second = [run(CHUNKS[1][0], (sends0,))]
+    p2, e = run(2, e, [e_all], [xtp, xt, cot], (sends0,))
     kept0, sends0 = fold(kept0, came, devices // 4)
     came = send_all(sends0, plan[1])
-    second.append(run(CHUNKS[1][1], sends0))
+    (p3,) = run(3, e, [], [xtp, xt, cot], tuple(sends0))
+    second = [p2, p3]
     kept0, _ = fold(kept0, came, devices // 4)
-    kept, sends = weigh(second, (kept0,))
+    kept1, sends1 = weigh(second, (kept0,))
     ctxs, dqts, dkos, dvos, dkps, dvps = zip(*(first + second))
-    came = send_all([sends], plan[0])
+
+    def scatter(kept, number):
+        left = kept.shape[0] >> len(plan[number])
+        sends = [kept[i : i + left] for i in range(0, kept.shape[0], left)]
+        return sends[0], send_all(sends[1:], plan[number]), left
+
+    def finish_scatter(kept):
+        for number in range(3, len(plan)):
+            mine, came, left = scatter(kept, number)
+            kept, _ = fold(mine, came, left)
+        for number in reversed(range(3, len(plan))):
+            kept = jnp.concatenate(gather_all(kept, plan[number]), 0)
+        return kept
+
+    came1 = send_all([sends1], plan[0])
+    mine0, came0, left = scatter(kept0, 2)
     backs = back(dkps, dvps, w_key, w_value)
-    kept, sends = fold(kept, came, devices // 4)
-    came, *backs = tie(*send_all(sends, plan[1]), *backs)
+    kept1, sends1 = fold(kept1, came1, devices // 4)
+    came1, *backs = tie(*send_all(sends1, plan[1]), *backs)
     backs = [partner(piece, levels - 4 + i) for i, piece in enumerate(backs)]
+    kept1, _ = fold(kept1, [came1], devices // 4)
+    kept0, _ = fold(mine0, came0, left)
+    kept0 = finish_scatter(kept0)
+    mine1, *sends1 = [kept1[i : i + left] for i in range(0, kept1.shape[0], left)]
+    came = send_all([jnp.concatenate([kept0, piece], 0) for piece in sends1], plan[2])
     output, partial = finish(ctxs, dqts, dkos, dvos, w_out, w_query, w_key, w_value)
-    kept, _ = fold(kept, [came], devices // 4)
-    kept = jnp.concatenate([kept0, kept], 2)
-    left = devices // 4
-    for number in range(2, len(plan)):
-        left >>= len(plan[number])
-        sends = [kept[i : i + left] for i in range(0, kept.shape[0], left)]
-        came = send_all(sends[1:], plan[number])
-        if number == 2:
-            *came, partial = tie(*came, partial)
-        kept, _ = fold(sends[0], came, left)
+    *came, partial = tie(*came, partial)
+    kept1, _ = fold(mine1, [piece[left:] for piece in came], left)
+    pieces0 = gather_all(jnp.concatenate([kept0] + [piece[:left] for piece in came], 0), plan[1])
+    kept1 = finish_scatter(kept1)
+    kept1, *backs[1:2] = tie(kept1, *backs[1:2])
+    pieces1 = gather_all(kept1, plan[2])
+    mine0 = jnp.concatenate(pieces0, 0)
+    mine0, *backs[2:] = tie(mine0, *backs[2:])
+    pieces0 = gather_all(mine0, plan[0])
+    pieces1 = gather_all(jnp.concatenate(pieces1, 0), plan[1])
+    mine1, *backs = tie(jnp.concatenate(pieces1, 0), *backs)
     grad_tokens = token_grads(theirs, partial, backs)
-    pieces = [kept]
-    for number in reversed(range(len(plan))):
-        mine = pieces[0] if len(pieces) == 1 else jnp.concatenate(pieces, 0)
-        if number == 0:
-            mine, grad_tokens = tie(mine, grad_tokens)
-        pieces = gather_all(mine, plan[number])
-    return (output, grad_tokens, *spread_grads(place, devices, width, pieces))
+    mine1, grad_tokens = tie(mine1, grad_tokens)
+    pieces1 = gather_all(mine1, plan[0])
+    return (output, grad_tokens, *spread_grads(place, devices, width, [pieces0, pieces1]))
 
 
 def solution(mesh):

time: 129 us -> 117 us (0.907)
  Pallas kernels: 67 us -> 56.8 us
  waiting for transfers between devices: 33.7 us -> 24.8 us
  starting transfers between devices: 26.2 us -> 33.8 us
    ppermute x12, waiting for transfers between devices: 15.3 us -> 5.42 us  [partner(): lax.ppermute(x, 'tok', [(i, i ^ 1 << stride) for i in range(lax.axis_size...]
    pallas_call x4, Pallas kernels: 31 us -> 25 us  [attend(): pl.pallas_call(functools.partial(attend_kernel, pair, head_width, scale),...]
    ppermute x12 -> x17, starting transfers between devices: 13 us -> 18.3 us  [exchange(): lax.ppermute(x, 'tok', [(i, i ^ mask) for i in range(lax.axis_size('tok'))])]
    pallas_call x2, Pallas kernels: 6.88 us -> 4.3 us  [weight_grads(): pl.pallas_call(functools.partial(weights_kernel, pairs), in_specs=[pl.Blo...]
    ppermute x12, starting transfers between devices: 13.2 us -> 15.4 us  [partner(): lax.ppermute(x, 'tok', [(i, i ^ 1 << stride) for i in range(lax.axis_size...]
    pallas_call x1, Pallas kernels: 11.2 us -> 9.06 us  [own_part(): pl.pallas_call(functools.partial(own_kernel, head_width), grid=(head_coun...]
    ppermute x12 -> x17, waiting for transfers between devices: 18.4 us -> 19.4 us  [exchange(): lax.ppermute(x, 'tok', [(i, i ^ mask) for i in range(lax.axis_size('tok'))])]
  transfers between devices with their start and end apart: 24 -> 29, of which waited for: 12 -> 13; matrix products, arithmetic and copies ran while one was open for 0% -> 0% of each run, Pallas kernels for 30% -> 29%
where the time goes in v3:
time: 117 us
  Pallas kernels  56.8 us (49%)
  starting transfers between devices  33.8 us (29%)
  waiting for transfers between devices  24.8 us (21%)
    pallas_call x4, Pallas kernels, attend(): pl.pallas_call(functools.partial(attend_kernel, pair, head_width, scale),...  25 us
    ppermute x17, waiting for transfers between devices, exchange(): lax.ppermute(x, 'tok', [(i, i ^ mask) for i in range(lax.axis_size('tok'))])  19.4 us
    ppermute x17, starting transfers between devices, exchange(): lax.ppermute(x, 'tok', [(i, i ^ mask) for i in range(lax.axis_size('tok'))])  18.3 us
    ppermute x12, starting transfers between devices, partner(): lax.ppermute(x, 'tok', [(i, i ^ 1 << stride) for i in range(lax.axis_size...  15.4 us
    pallas_call x1, Pallas kernels, own_part(): pl.pallas_call(functools.partial(own_kernel, head_width), grid=(head_coun...  9.06 us
    ppermute x12, waiting for transfers between devices, partner(): lax.ppermute(x, 'tok', [(i, i ^ 1 << stride) for i in range(lax.axis_size...  5.42 us
    pallas_call x1, Pallas kernels, project(): pl.pallas_call(functools.partial(project_kernel, scale), grid=(samples,),...  5.38 us
    pallas_call x2, Pallas kernels, weight_grads(): pl.pallas_call(functools.partial(weights_kernel, pairs), in_specs=[pl.Blo...  4.3 us
  transfers between devices with their start and end apart: 29, of which 13 were waited for; matrix products, arithmetic and copies ran while one was open for 0% of the time, Pallas kernels for 29%

profile of v3, /device:TPU:0, one launch (start us, length us, event | category | flops | bytes accessed | tf_op | source)
XLA Modules:
  0.0 117.2 jit_solution(806877129908140522)
XLA Ops:
  0.6 3.0 %collective-permute-start.1 = (s32[1,4]{1,0:T(1,128)}, s32[1,4]{1,0:T(1,128)S(1)}, u32[]{:S(2)}, u32[]{:S(2)}) collective-permute-start(s32[1,4]{1,0:T(1,128)} %param.13), channel_id=1, source_target_pairs={{0,2},{1,3},{2,0},{3,1},{4,6},{5,7},{6,4},{7,5},{8,10},{9,11},{10,... | collective-permute-start | bytes 56 | tf_op jit(solution)/shard_map/ppermute | solution.py:21
  3.7 2.6 %collective-permute-start.3 = (s32[1,4]{1,0:T(1,128)}, s32[1,4]{1,0:T(1,128)S(1)}, u32[]{:S(2)}, u32[]{:S(2)}) collective-permute-start(s32[1,4]{1,0:T(1,128)} %param.13), channel_id=1, source_target_pairs={{0,8},{1,9},{2,10},{3,11},{4,12},{5,13},{6,14},{7,15},{8,0},{9,1},... | collective-permute-start | bytes 56 | tf_op jit(solution)/shard_map/ppermute | solution.py:21
  8.2 1.7 %collective-permute-done.2.i2 = s32[1,4]{1,0:T(1,128)S(1)} collective-permute-done((s32[1,4]{1,0:T(1,128)}, s32[1,4]{1,0:T(1,128)S(1)}, u32[]{:S(2)}, u32[]{:S(2)}) %collective-permute-start.2) | collective-permute-done | bytes 48 | tf_op jit(solution)/shard_map/ppermute | solution.py:21
  14.4 5.4 %shard_map.128 = (bf16[2,512,512]{2,1,0:T(8,128)(2,1)S(1)}, bf16[2,512,512]{2,1,0:T(8,128)(2,1)S(1)}, bf16[2,512,512]{2,1,0:T(8,128)(2,1)}, bf16[2,512,512]{2,1,...) custom-call(bf16[2,512,512]{2,1,0:T(8,128)(2,1)} %x_ref.2, ...), custom_call_target="tpu_custom_call" | custom-call | flops 5500000256 | bytes 500000 | tf_op jit(solution)/shard_map/pallas_call | solution.py:84
  19.8 9.1 %shard_map.129 = (bf16[4,2,512,1024]{3,2,1,0:T(8,128)(2,1)}, f32[2,8,64,512]{3,2,1,0:T(8,128)S(1)}, f32[2,8,8,512]{3,2,1,0:T(8,128)S(1)}, bf16[2,512,512]{2,1,0:...) custom-call(bf16[2,512,512]{2,1,0:T(8,128)(2,1)S(1)} %get-tuple-element.107.qt_ref.refs_3_, ...), custom_call_target="tpu_custom_call" | custom-call | flops 11000000512 | bytes 1000000 | tf_op jit(solution)/shard_map/pallas_call | solution.py:221
  28.9 2.8 %shard_map.130 = (bf16[2,512,512]{2,1,0:T(8,128)(2,1)S(1)}, bf16[2,512,512]{2,1,0:T(8,128)(2,1)S(1)}, bf16[2,512,512]{2,1,0:T(8,128)(2,1)S(1)}, bf16[2,512,512]{...) custom-call(bf16[2,128,512]{2,1,0:T(8,128)(2,1)S(1)} %collective-permute-done.4.x0, ...), custom_call_target="tpu_custom_call" | custom-call | flops 2750000128 | bytes 250000 | tf_op jit(solution)/shard_map/pallas_call | solution.py:127
  31.7 6.3 %shard_map.131 = (bf16[2,128,512]{2,1,0:T(8,128)(2,1)S(1)}, bf16[2,128,512]{2,1,0:T(8,128)(2,1)S(1)}, bf16[2,512,128]{2,1,0:T(8,128)(2,1)S(1)}, bf16[2,512,128]{...) custom-call(s32[4,8]{1,0:T(4,128)S(1)} %bitcast.2, ...), custom_call_target="tpu_custom_call" | custom-call | flops 6600000000 | bytes 600000 | tf_op jit(solution)/shard_map/pallas_call | solution.py:368
  38.0 6.2 %shard_map.132 = (bf16[2,128,512]{2,1,0:T(8,128)(2,1)S(1)}, bf16[2,128,512]{2,1,0:T(8,128)(2,1)S(1)}, bf16[2,512,128]{2,1,0:T(8,128)(2,1)S(1)}, bf16[2,512,128]{...) custom-call(s32[4,8]{1,0:T(4,128)S(1)} %bitcast.3, ...), custom_call_target="tpu_custom_call" | custom-call | flops 6600000000 | bytes 600000 | tf_op jit(solution)/shard_map/pallas_call | solution.py:368
  44.2 2.1 %shard_map.133 = (bf16[8,128,256]{2,1,0:T(8,128)(2,1)S(1)}, bf16[8,128,256]{2,1,0:T(8,128)(2,1)S(1)}) custom-call(s32[1]{0:T(128)} %bitcast.1.place_ref, bf16[2,512,512]{2,1,0:T(8,128)(2,1)S(1)} %get-tuple-element.128.refs_3_.xt_ref.refs_2_.refs_1_, bf16[2,512,512]{2,1,0:T(8,128)(2,1)S(1)} %get-tuple-element.125.refs_2_.xtp_ref.refs_1_.refs_0_, ...), custom_call_target="tpu_custom_call" | custom-call | flops 3300000000 | bytes 300000 | tf_op jit(solution)/shard_map/pallas_call | solution.py:423
  46.5 6.3 %shard_map.134 = (bf16[2,128,512]{2,1,0:T(8,128)(2,1)S(1)}, bf16[2,128,512]{2,1,0:T(8,128)(2,1)S(1)}, bf16[2,512,128]{2,1,0:T(8,128)(2,1)S(1)}, bf16[2,512,128]{...) custom-call(s32[4,8]{1,0:T(4,128)S(1)} %bitcast.4, ...), custom_call_target="tpu_custom_call" | custom-call | flops 6600000000 | bytes 600000 | tf_op jit(solution)/shard_map/pallas_call | solution.py:368
  54.5 6.2 %shard_map.135 = (bf16[2,128,512]{2,1,0:T(8,128)(2,1)S(1)}, bf16[2,128,512]{2,1,0:T(8,128)(2,1)S(1)}, bf16[2,512,128]{2,1,0:T(8,128)(2,1)S(1)}, bf16[2,512,128]{...) custom-call(s32[4,8]{1,0:T(4,128)S(1)} %bitcast.5, ...), custom_call_target="tpu_custom_call" | custom-call | flops 6600000000 | bytes 600000 | tf_op jit(solution)/shard_map/pallas_call | solution.py:368
  61.7 2.2 %shard_map.137 = (bf16[8,128,256]{2,1,0:T(8,128)(2,1)S(1)}, bf16[8,128,256]{2,1,0:T(8,128)(2,1)S(1)}) custom-call(s32[1]{0:T(128)} %bitcast.1.place_ref, bf16[2,512,512]{2,1,0:T(8,128)(2,1)S(1)} %get-tuple-element.128.refs_3_.xt_ref.refs_2_.refs_1_, bf16[2,512,512]{2,1,0:T(8,128)(2,1)S(1)} %get-tuple-element.125.refs_2_.xtp_ref.refs_1_.refs_0_, ...), custom_call_target="tpu_custom_call" | custom-call | flops 3300000000 | bytes 300000 | tf_op jit(solution)/shard_map/pallas_call | solution.py:423
  64.6 3.0 %collective-permute-start.14 = (bf16[1,128,256]{2,1,0:T(8,128)(2,1)S(1)}, bf16[1,128,256]{2,1,0:T(8,128)(2,1)S(1)}, u32[]{:S(2)}, u32[]{:S(2)}) collective-permute-start(bf16[1,128,256]{2,1,0:T(8,128)(2,1)S(1)} %get-tuple-element.196), channel_id=1, source_target_pairs={{0,12},{1,13},{2,14},{3,15},{4,8},{5,9},{6,10},{7,11},{8,4},{9,5},... | collective-permute-start | bytes 196616 | tf_op jit(solution)/shard_map/ppermute | solution.py:451
  71.9 2.3 %collective-permute-done.13 = bf16[1,128,256]{2,1,0:T(8,128)(2,1)S(1)} collective-permute-done((bf16[1,128,256]{2,1,0:T(8,128)(2,1)S(1)}, bf16[1,128,256]{2,1,0:T(8,128)(2,1)S(1)}, u32[]{:S(2)}, u32[]{:S(2)}) %collective-permute-start.13) | collective-permute-done | bytes 65568 | tf_op jit(solution)/shard_map/ppermute | solution.py:451
  76.1 1.7 %collective-permute-start.17 = (bf16[2,128,256]{2,1,0:T(8,128)(2,1)S(1)}, bf16[2,128,256]{2,1,0:T(8,128)(2,1)S(1)}, u32[]{:S(2)}, u32[]{:S(2)}) collective-permute-start(bf16[2,128,256]{2,1,0:T(8,128)(2,1)S(1)} %get-tuple-element.204), channel_id=1, source_target_pairs={{0,12},{1,13},{2,14},{3,15},{4,8},{5,9},{6,10},{7,11},{8,4},{9,5},... | collective-permute-start | bytes 393224 | tf_op jit(solution)/shard_map/ppermute | solution.py:451
  80.6 3.2 %shard_map.136 = (bf16[2,512,512]{2,1,0:T(8,128)(2,1)}, f32[2,512,512]{2,1,0:T(8,128)S(1)}) custom-call(bf16[2,128,512]{2,1,0:T(8,128)(2,1)S(1)} %get-tuple-element.126.refs_0_, bf16[2,128,512]{2,1,0:T(8,128)(2,1)S(1)} %get-tuple-element.129.refs_1_, bf16[2,128,512]{2,1,0:T(8,128)(2,1)S(1)} %get-tuple-element.143.refs_2_.refs_0_, ...), custom_call_target="tpu_custom_call" | custom-call | flops 4400000000 | bytes 400000 | tf_op jit(solution)/shard_map/pallas_call | solution.py:551
  85.3 3.5 %collective-permute-start.25 = (bf16[2,128,512]{2,1,0:T(8,128)(2,1)S(1)}, bf16[2,128,512]{2,1,0:T(8,128)(2,1)S(1)}, u32[]{:S(2)}, u32[]{:S(2)}) collective-permute-start(bf16[2,128,512]{2,1,0:T(8,128)(2,1)S(1)} %get-tuple-element.173), channel_id=1, source_target_pairs={{0,4},{1,5},{2,6},{3,7},{4,0},{5,1},{6,2},{7,3},{8,12},{9,13},{10,... | collective-permute-start | bytes 786440 | tf_op jit(solution)/shard_map/ppermute | solution.py:21
  90.2 2.3 %collective-permute-start.21 = (bf16[1,128,256]{2,1,0:T(8,128)(2,1)S(1)}, bf16[1,128,256]{2,1,0:T(8,128)(2,1)S(1)}, u32[]{:S(2)}, u32[]{:S(2)}) collective-permute-start(bf16[1,128,256]{2,1,0:T(8,128)(2,1)S(1)} %add_convert_fusion.4), channel_id=1, source_target_pairs={{0,12},{1,13},{2,14},{3,15},{4,8},{5,9},{6,10},{7,11},{8,4},{9,5},... | collective-permute-start | bytes 196616 | tf_op jit(solution)/shard_map/ppermute | solution.py:451
  92.5 2.1 %collective-permute-start.19 = (bf16[1,128,256]{2,1,0:T(8,128)(2,1)S(1)}, bf16[1,128,256]{2,1,0:T(8,128)(2,1)S(1)}, u32[]{:S(2)}, u32[]{:S(2)}) collective-permute-start(bf16[1,128,256]{2,1,0:T(8,128)(2,1)S(1)} %add_convert_fusion.4), channel_id=1, source_target_pairs={{0,4},{1,5},{2,6},{3,7},{4,0},{5,1},{6,2},{7,3},{8,12},{9,13},{10,... | collective-permute-start | bytes 196616 | tf_op jit(solution)/shard_map/ppermute | solution.py:451
  94.6 4.0 %collective-permute-done.21 = bf16[1,128,256]{2,1,0:T(8,128)(2,1)S(1)} collective-permute-done((bf16[1,128,256]{2,1,0:T(8,128)(2,1)S(1)}, bf16[1,128,256]{2,1,0:T(8,128)(2,1)S(1)}, u32[]{:S(2)}, u32[]{:S(2)}) %collective-permute-start.21) | collective-permute-done | bytes 65568 | tf_op jit(solution)/shard_map/ppermute | solution.py:451
  101.3 6.6 %collective-permute-done.24 = bf16[4,128,256]{2,1,0:T(8,128)(2,1)S(1)} collective-permute-done((bf16[4,128,256]{2,1,0:T(8,128)(2,1)S(1)}, bf16[4,128,256]{2,1,0:T(8,128)(2,1)S(1)}, u32[]{:S(2)}, u32[]{:S(2)}) %collective-permute-start.24) | collective-permute-done | bytes 262176 | tf_op jit(solution)/shard_map/ppermute | solution.py:451
  107.9 3.0 %collective-permute-done.26.b3 = bf16[2,128,512]{2,1,0:T(8,128)(2,1)S(1)} collective-permute-done((bf16[2,128,512]{2,1,0:T(8,128)(2,1)S(1)}, bf16[2,128,512]{2,1,0:T(8,128)(2,1)S(1)}, u32[]{:S(2)}, u32[]{:S(2)}) %collective-permute-start.26) | collective-permute-done | bytes 262176 | tf_op jit(solution)/shard_map/ppermute | solution.py:21
  110.9 1.9 %shard_map.139 = bf16[2,512,512]{2,1,0:T(8,128)(2,1)} custom-call(s32[1,4]{1,0:T(1,128)S(1)} %collective-permute-done.i0, s32[1,4]{1,0:T(1,128)S(1)} %collective-permute-done.1.i1, s32[1,4]{1,0:T(1,128)S(1)} %collective-permute-done.2.i2, s32[1,4]{1,0:T(1,128)S(1)} %collective-permute-done.3.i3, f32[2,512,512]{2,1,0:T(8,128)S(1)} %get-tuple-element.178.gt_ref, ...), custom_call_target="tpu_custom_call" | custom-call | tf_op jit(solution)/shard_map/pallas_call | solution.py:574
  114.8 2.4 %shard_map.140 = (f32[512,512]{1,0:T(8,128)}, f32[512,512]{1,0:T(8,128)}, f32[512,512]{1,0:T(8,128)}, f32[512,512]{1,0:T(8,128)}) custom-call(s32[1]{0:T(128)} %bitcast.1.place_ref, bf16[8,128,256]{2,1,0:T(8,128)(2,1)S(1)} %constant_dynamic-update-slice_fusion.5.refs_0_, bf16[8,128,256]{2,1,0:T(8,128)(2,1)S(1)} %collective-permute-done.27.refs_1_, ...), custom_call_target="tpu_custom_call" | custom-call | tf_op jit(solution)/shard_map/pallas_call | solution.py:495
  (80 shorter events, 26.4 us)
Async XLA Ops:
  0.6 7.2 %collective-permute-start.1 = (s32[1,4]{1,0:T(1,128)}, s32[1,4]{1,0:T(1,128)S(1)}, u32[]{:S(2)}, u32[]{:S(2)}) collective-permute-start(s32[1,4]{1,0:T(1,128)} %param.13), channel_id=1, source_target_pairs={{0,2},{1,3},{2,0},{3,1},{4,6},{5,7},{6,4},{7,5},{8,10},{9,11},{10,... | collective-permute-start | bytes 56 | tf_op jit(solution)/shard_map/ppermute | solution.py:21
  3.7 4.6 %collective-permute-start.3 = (s32[1,4]{1,0:T(1,128)}, s32[1,4]{1,0:T(1,128)S(1)}, u32[]{:S(2)}, u32[]{:S(2)}) collective-permute-start(s32[1,4]{1,0:T(1,128)} %param.13), channel_id=1, source_target_pairs={{0,8},{1,9},{2,10},{3,11},{4,12},{5,13},{6,14},{7,15},{8,0},{9,1},... | collective-permute-start | bytes 56 | tf_op jit(solution)/shard_map/ppermute | solution.py:21
  11.2 17.6 %collective-permute-start.4 = (bf16[2,128,512]{2,1,0:T(8,128)(2,1)S(1)}, bf16[2,128,512]{2,1,0:T(8,128)(2,1)S(1)}, u32[]{:S(2)}, u32[]{:S(2)}) collective-permute-start(bf16[2,128,512]{2,1,0:T(8,128)(2,1)S(1)} %get-tuple-element.102), channel_id=1, source_target_pairs={{0,1},{1,0},{2,3},{3,2},{4,5},{5,4},{6,7},{7,6},{8,9},{9,8},{10,11... | collective-permute-start | bytes 786440 | tf_op jit(solution)/shard_map/ppermute | solution.py:21
  11.3 17.5 %collective-permute-start.5 = (bf16[2,128,512]{2,1,0:T(8,128)(2,1)S(1)}, bf16[2,128,512]{2,1,0:T(8,128)(2,1)S(1)}, u32[]{:S(2)}, u32[]{:S(2)}) collective-permute-start(bf16[2,128,512]{2,1,0:T(8,128)(2,1)S(1)} %get-tuple-element.103), channel_id=1, source_target_pairs={{0,2},{1,3},{2,0},{3,1},{4,6},{5,7},{6,4},{7,5},{8,10},{9,11},{10,... | collective-permute-start | bytes 786440 | tf_op jit(solution)/shard_map/ppermute | solution.py:21
  11.9 17.0 %collective-permute-start.6 = (bf16[2,128,512]{2,1,0:T(8,128)(2,1)S(1)}, bf16[2,128,512]{2,1,0:T(8,128)(2,1)S(1)}, u32[]{:S(2)}, u32[]{:S(2)}) collective-permute-start(bf16[2,128,512]{2,1,0:T(8,128)(2,1)S(1)} %get-tuple-element.104), channel_id=1, source_target_pairs={{0,4},{1,5},{2,6},{3,7},{4,0},{5,1},{6,2},{7,3},{8,12},{9,13},{10,... | collective-permute-start | bytes 786440 | tf_op jit(solution)/shard_map/ppermute | solution.py:21
  13.5 15.4 %collective-permute-start.7 = (bf16[2,128,512]{2,1,0:T(8,128)(2,1)S(1)}, bf16[2,128,512]{2,1,0:T(8,128)(2,1)S(1)}, u32[]{:S(2)}, u32[]{:S(2)}) collective-permute-start(bf16[2,128,512]{2,1,0:T(8,128)(2,1)S(1)} %get-tuple-element.105), channel_id=1, source_target_pairs={{0,8},{1,9},{2,10},{3,11},{4,12},{5,13},{6,14},{7,15},{8,0},{9,1},... | collective-permute-start | bytes 786440 | tf_op jit(solution)/shard_map/ppermute | solution.py:21
  46.4 6.3 %collective-permute-start.8 = (bf16[8,128,256]{2,1,0:T(8,128)(2,1)S(1)}, bf16[8,128,256]{2,1,0:T(8,128)(2,1)S(1)}, u32[]{:S(2)}, u32[]{:S(2)}) collective-permute-start(bf16[8,128,256]{2,1,0:T(8,128)(2,1)S(1)} %get-tuple-element.142.refs_4_), channel_id=1, source_target_pairs={{0,1},{1,0},{2,3},{3,2},{4,5},{5,4},{6,7},{7,6},{8,9},{9,8},{10,11... | collective-permute-start | bytes 1572872 | tf_op jit(solution)/shard_map/ppermute | solution.py:451
  52.9 8.8 %collective-permute-start.9 = (bf16[4,128,256]{2,1,0:T(8,128)(2,1)S(1)}, bf16[4,128,256]{2,1,0:T(8,128)(2,1)S(1)}, u32[]{:S(2)}, u32[]{:S(2)}) collective-permute-start(bf16[4,128,256]{2,1,0:T(8,128)(2,1)S(1)} %slice.76.refs_3_), channel_id=1, source_target_pairs={{0,2},{1,3},{2,0},{3,1},{4,6},{5,7},{6,4},{7,5},{8,10},{9,11},{10,... | collective-permute-start | bytes 786440 | tf_op jit(solution)/shard_map/ppermute | solution.py:451
  64.0 6.9 %collective-permute-start.12 = (bf16[1,128,256]{2,1,0:T(8,128)(2,1)S(1)}, bf16[1,128,256]{2,1,0:T(8,128)(2,1)S(1)}, u32[]{:S(2)}, u32[]{:S(2)}) collective-permute-start(bf16[1,128,256]{2,1,0:T(8,128)(2,1)S(1)} %get-tuple-element.195), channel_id=1, source_target_pairs={{0,4},{1,5},{2,6},{3,7},{4,0},{5,1},{6,2},{7,3},{8,12},{9,13},{10,... | collective-permute-start | bytes 196616 | tf_op jit(solution)/shard_map/ppermute | solution.py:451
  64.6 7.4 %collective-permute-start.14 = (bf16[1,128,256]{2,1,0:T(8,128)(2,1)S(1)}, bf16[1,128,256]{2,1,0:T(8,128)(2,1)S(1)}, u32[]{:S(2)}, u32[]{:S(2)}) collective-permute-start(bf16[1,128,256]{2,1,0:T(8,128)(2,1)S(1)} %get-tuple-element.196), channel_id=1, source_target_pairs={{0,12},{1,13},{2,14},{3,15},{4,8},{5,9},{6,10},{7,11},{8,4},{9,5},... | collective-permute-start | bytes 196616 | tf_op jit(solution)/shard_map/ppermute | solution.py:451
  67.6 6.7 %collective-permute-start.13 = (bf16[1,128,256]{2,1,0:T(8,128)(2,1)S(1)}, bf16[1,128,256]{2,1,0:T(8,128)(2,1)S(1)}, u32[]{:S(2)}, u32[]{:S(2)}) collective-permute-start(bf16[1,128,256]{2,1,0:T(8,128)(2,1)S(1)} %get-tuple-element.197), channel_id=1, source_target_pairs={{0,8},{1,9},{2,10},{3,11},{4,12},{5,13},{6,14},{7,15},{8,0},{9,1},... | collective-permute-start | bytes 196616 | tf_op jit(solution)/shard_map/ppermute | solution.py:451
  67.8 8.2 %collective-permute-start.11 = (bf16[4,128,256]{2,1,0:T(8,128)(2,1)S(1)}, bf16[4,128,256]{2,1,0:T(8,128)(2,1)S(1)}, u32[]{:S(2)}, u32[]{:S(2)}) collective-permute-start(bf16[4,128,256]{2,1,0:T(8,128)(2,1)S(1)} %slice.79), channel_id=1, source_target_pairs={{0,2},{1,3},{2,0},{3,1},{4,6},{5,7},{6,4},{7,5},{8,10},{9,11},{10,... | collective-permute-start | bytes 786440 | tf_op jit(solution)/shard_map/ppermute | solution.py:451
  76.1 9.2 %collective-permute-start.17 = (bf16[2,128,256]{2,1,0:T(8,128)(2,1)S(1)}, bf16[2,128,256]{2,1,0:T(8,128)(2,1)S(1)}, u32[]{:S(2)}, u32[]{:S(2)}) collective-permute-start(bf16[2,128,256]{2,1,0:T(8,128)(2,1)S(1)} %get-tuple-element.204), channel_id=1, source_target_pairs={{0,12},{1,13},{2,14},{3,15},{4,8},{5,9},{6,10},{7,11},{8,4},{9,5},... | collective-permute-start | bytes 393224 | tf_op jit(solution)/shard_map/ppermute | solution.py:451
  77.8 12.0 %collective-permute-start.16 = (bf16[2,128,256]{2,1,0:T(8,128)(2,1)S(1)}, bf16[2,128,256]{2,1,0:T(8,128)(2,1)S(1)}, u32[]{:S(2)}, u32[]{:S(2)}) collective-permute-start(bf16[2,128,256]{2,1,0:T(8,128)(2,1)S(1)} %get-tuple-element.205), channel_id=1, source_target_pairs={{0,8},{1,9},{2,10},{3,11},{4,12},{5,13},{6,14},{7,15},{8,0},{9,1},... | collective-permute-start | bytes 393224 | tf_op jit(solution)/shard_map/ppermute | solution.py:451
  78.9 10.9 %collective-permute-start.15 = (bf16[2,128,256]{2,1,0:T(8,128)(2,1)S(1)}, bf16[2,128,256]{2,1,0:T(8,128)(2,1)S(1)}, u32[]{:S(2)}, u32[]{:S(2)}) collective-permute-start(bf16[2,128,256]{2,1,0:T(8,128)(2,1)S(1)} %get-tuple-element.206), channel_id=1, source_target_pairs={{0,4},{1,5},{2,6},{3,7},{4,0},{5,1},{6,2},{7,3},{8,12},{9,13},{10,... | collective-permute-start | bytes 393224 | tf_op jit(solution)/shard_map/ppermute | solution.py:451
  83.8 6.4 %collective-permute-start.18 = (bf16[2,128,512]{2,1,0:T(8,128)(2,1)S(1)}, bf16[2,128,512]{2,1,0:T(8,128)(2,1)S(1)}, u32[]{:S(2)}, u32[]{:S(2)}) collective-permute-start(bf16[2,128,512]{2,1,0:T(8,128)(2,1)S(1)} %get-tuple-element.169), channel_id=1, source_target_pairs={{0,2},{1,3},{2,0},{3,1},{4,6},{5,7},{6,4},{7,5},{8,10},{9,11},{10,... | collective-permute-start | bytes 786440 | tf_op jit(solution)/shard_map/ppermute | solution.py:21
  85.3 25.6 %collective-permute-start.23 = (bf16[2,128,512]{2,1,0:T(8,128)(2,1)S(1)}, bf16[2,128,512]{2,1,0:T(8,128)(2,1)S(1)}, u32[]{:S(2)}, u32[]{:S(2)}) collective-permute-start(bf16[2,128,512]{2,1,0:T(8,128)(2,1)S(1)} %get-tuple-element.171), channel_id=1, source_target_pairs={{0,1},{1,0},{2,3},{3,2},{4,5},{5,4},{6,7},{7,6},{8,9},{9,8},{10,11... | collective-permute-start | bytes 786440 | tf_op jit(solution)/shard_map/ppermute | solution.py:21
  85.3 22.6 %collective-permute-start.25 = (bf16[2,128,512]{2,1,0:T(8,128)(2,1)S(1)}, bf16[2,128,512]{2,1,0:T(8,128)(2,1)S(1)}, u32[]{:S(2)}, u32[]{:S(2)}) collective-permute-start(bf16[2,128,512]{2,1,0:T(8,128)(2,1)S(1)} %get-tuple-element.173), channel_id=1, source_target_pairs={{0,4},{1,5},{2,6},{3,7},{4,0},{5,1},{6,2},{7,3},{8,12},{9,13},{10,... | collective-permute-start | bytes 786440 | tf_op jit(solution)/shard_map/ppermute | solution.py:21
  90.2 8.4 %collective-permute-start.21 = (bf16[1,128,256]{2,1,0:T(8,128)(2,1)S(1)}, bf16[1,128,256]{2,1,0:T(8,128)(2,1)S(1)}, u32[]{:S(2)}, u32[]{:S(2)}) collective-permute-start(bf16[1,128,256]{2,1,0:T(8,128)(2,1)S(1)} %add_convert_fusion.4), channel_id=1, source_target_pairs={{0,12},{1,13},{2,14},{3,15},{4,8},{5,9},{6,10},{7,11},{8,4},{9,5},... | collective-permute-start | bytes 196616 | tf_op jit(solution)/shard_map/ppermute | solution.py:451
  92.5 6.6 %collective-permute-start.20 = (bf16[1,128,256]{2,1,0:T(8,128)(2,1)S(1)}, bf16[1,128,256]{2,1,0:T(8,128)(2,1)S(1)}, u32[]{:S(2)}, u32[]{:S(2)}) collective-permute-start(bf16[1,128,256]{2,1,0:T(8,128)(2,1)S(1)} %add_convert_fusion.4), channel_id=1, source_target_pairs={{0,8},{1,9},{2,10},{3,11},{4,12},{5,13},{6,14},{7,15},{8,0},{9,1},... | collective-permute-start | bytes 196616 | tf_op jit(solution)/shard_map/ppermute | solution.py:451
  92.5 8.2 %collective-permute-start.19 = (bf16[1,128,256]{2,1,0:T(8,128)(2,1)S(1)}, bf16[1,128,256]{2,1,0:T(8,128)(2,1)S(1)}, u32[]{:S(2)}, u32[]{:S(2)}) collective-permute-start(bf16[1,128,256]{2,1,0:T(8,128)(2,1)S(1)} %add_convert_fusion.4), channel_id=1, source_target_pairs={{0,4},{1,5},{2,6},{3,7},{4,0},{5,1},{6,2},{7,3},{8,12},{9,13},{10,... | collective-permute-start | bytes 196616 | tf_op jit(solution)/shard_map/ppermute | solution.py:451
  98.6 12.2 %collective-permute-start.26 = (bf16[2,128,512]{2,1,0:T(8,128)(2,1)S(1)}, bf16[2,128,512]{2,1,0:T(8,128)(2,1)S(1)}, u32[]{:S(2)}, u32[]{:S(2)}) collective-permute-start(bf16[2,128,512]{2,1,0:T(8,128)(2,1)S(1)} %get-tuple-element.174), channel_id=1, source_target_pairs={{0,8},{1,9},{2,10},{3,11},{4,12},{5,13},{6,14},{7,15},{8,0},{9,1},... | collective-permute-start | bytes 786440 | tf_op jit(solution)/shard_map/ppermute | solution.py:21
  99.1 8.7 %collective-permute-start.24 = (bf16[4,128,256]{2,1,0:T(8,128)(2,1)S(1)}, bf16[4,128,256]{2,1,0:T(8,128)(2,1)S(1)}, u32[]{:S(2)}, u32[]{:S(2)}) collective-permute-start(bf16[4,128,256]{2,1,0:T(8,128)(2,1)S(1)} %pad_maximum_fusion.1), channel_id=1, source_target_pairs={{0,2},{1,3},{2,0},{3,1},{4,6},{5,7},{6,4},{7,5},{8,10},{9,11},{10,... | collective-permute-start | bytes 786440 | tf_op jit(solution)/shard_map/ppermute | solution.py:451
  100.7 10.2 %collective-permute-start.22 = (bf16[4,128,256]{2,1,0:T(8,128)(2,1)S(1)}, bf16[4,128,256]{2,1,0:T(8,128)(2,1)S(1)}, u32[]{:S(2)}, u32[]{:S(2)}) collective-permute-start(bf16[4,128,256]{2,1,0:T(8,128)(2,1)S(1)} %pad_maximum_fusion), channel_id=1, source_target_pairs={{0,2},{1,3},{2,0},{3,1},{4,6},{5,7},{6,4},{7,5},{8,10},{9,11},{10,... | collective-permute-start | bytes 786440 | tf_op jit(solution)/shard_map/ppermute | solution.py:451
  (10 other events, 49.1 us)

commit v4 on v3

--- a/solution.py
+++ b/solution.py
@@ -120,20 +120,19 @@
     samples, sub_rows, width = arrived[0].shape
     rows = sub_rows * len(arrived)
     whole = pl.BlockSpec(memory_space=pltpu.VMEM)
-    weight = pl.BlockSpec((width, width), lambda: (0, 0))
     anywhere = pl.BlockSpec(memory_space=pl.ANY)
     by_row = pltpu.VMEM((samples, rows, width), BF16)
     by_col = pltpu.VMEM((samples, width, rows), BF16)
     return pl.pallas_call(
         functools.partial(project_partner_kernel, len(loads)),
-        in_specs=[whole] * 4 + [weight] * 2 + [anywhere] * len(loads) + [whole] * len(held),
+        in_specs=[whole] * 6 + [anywhere] * len(loads) + [whole] * len(held),
         out_specs=[whole] * (5 + len(loads)),
         out_shape=[by_row, by_row, by_col, by_col, by_col, pltpu.VMEM(loads[0].shape[1:], BF16)]
         + [pltpu.VMEM(x.shape, x.dtype) for x in loads[1:]],
         scratch_shapes=[pltpu.SemaphoreType.DMA((len(loads),))],
         cost_estimate=cost(2.5),
         compiler_params=params(),
-    )(*near(*arrived), *far(w_key, w_value, *loads), *near(*held))
+    )(*near(*arrived, w_key, w_value), *far(*loads), *near(*held))
 
 
 def weave(*streams):
@@ -610,10 +609,10 @@
     theirs = [partner(partner_block, levels - 4 + section) for section in range(4)]
     picked = pick(theirs, tokens)
     first_tokens, *picked = tie(tokens, *picked)
-    arrived = [partner(piece, levels - 4 + section) for section, piece in enumerate(picked)]
+    arrived = [partner(picked[section], levels - 4 + section) for section in (3, 2, 1, 0)][::-1]
     qt, ko, vo, kto, vto, dot, xt = project(first_tokens, cotangent, w_query, w_key, w_value, w_out, scale)
-    e_all, *stats, vo, kto, dot = own_part(qt, ko, vto, head_count, [vo, kto, dot])
-    kp, vp, ktp, vtp, xtp, e = project_partner(arrived, w_key, w_value, [e_all], [*stats, qt, vo, kto, dot])
+    e_all, *stats, vo, kto, dot, near_key, near_value = own_part(qt, ko, vto, head_count, [vo, kto, dot, w_key, w_value])
+    kp, vp, ktp, vtp, xtp, e = project_partner(arrived, near_key, near_value, [e_all], [*stats, qt, vo, kto, dot])
 
     def run(pair, e, loads, held, after=()):
         out = attend(
@@ -675,8 +674,8 @@
     pieces1 = gather_all(jnp.concatenate(pieces1, 0), plan[1])
     mine1, *backs = tie(jnp.concatenate(pieces1, 0), *backs)
     grad_tokens = token_grads(theirs, partial, backs)
-    mine1, grad_tokens = tie(mine1, grad_tokens)
     pieces1 = gather_all(mine1, plan[0])
+    pieces1[-1], grad_tokens = tie(pieces1[-1], grad_tokens)
     return (output, grad_tokens, *spread_grads(place, devices, width, [pieces0, pieces1]))
 
 

time: 117 us -> 115 us (0.983)
  Pallas kernels: 56.8 us -> 55.6 us
    pallas_call x1, Pallas kernels: 2.82 us -> 1.61 us  [project_partner(): pl.pallas_call(functools.partial(project_partner_kernel, len(loads)), in_...]
where the time goes in v4:
time: 115 us
  Pallas kernels  55.6 us (48%)
  starting transfers between devices  33.8 us (29%)
  waiting for transfers between devices  23.7 us (21%)
    pallas_call x4, Pallas kernels, attend(): pl.pallas_call(functools.partial(attend_kernel, pair, head_width, scale),...  25 us
    ppermute x17, starting transfers between devices, exchange(): lax.ppermute(x, 'tok', [(i, i ^ mask) for i in range(lax.axis_size('tok'))])  18.3 us
    ppermute x17, waiting for transfers between devices, exchange(): lax.ppermute(x, 'tok', [(i, i ^ mask) for i in range(lax.axis_size('tok'))])  18.3 us
    ppermute x12, starting transfers between devices, partner(): lax.ppermute(x, 'tok', [(i, i ^ 1 << stride) for i in range(lax.axis_size...  15.4 us
    pallas_call x1, Pallas kernels, own_part(): pl.pallas_call(functools.partial(own_kernel, head_width), grid=(head_coun...  9.1 us
    ppermute x12, waiting for transfers between devices, partner(): lax.ppermute(x, 'tok', [(i, i ^ 1 << stride) for i in range(lax.axis_size...  5.42 us
    pallas_call x1, Pallas kernels, project(): pl.pallas_call(functools.partial(project_kernel, scale), grid=(samples,),...  5.38 us
    pallas_call x2, Pallas kernels, weight_grads(): pl.pallas_call(functools.partial(weights_kernel, pairs), in_specs=[pl.Blo...  4.3 us
  transfers between devices with their start and end apart: 29, of which 13 were waited for; matrix products, arithmetic and copies ran while one was open for 0% of the time, Pallas kernels for 29%

profile of v4, /device:TPU:0, one launch (start us, length us, event | category | flops | bytes accessed | tf_op | source)
XLA Modules:
  0.0 114.9 jit_solution(13658572610939986796)
XLA Ops:
  0.6 3.0 %collective-permute-start.1 = (s32[1,4]{1,0:T(1,128)}, s32[1,4]{1,0:T(1,128)S(1)}, u32[]{:S(2)}, u32[]{:S(2)}) collective-permute-start(s32[1,4]{1,0:T(1,128)} %param.13), channel_id=1, source_target_pairs={{0,2},{1,3},{2,0},{3,1},{4,6},{5,7},{6,4},{7,5},{8,10},{9,11},{10,... | collective-permute-start | bytes 56 | tf_op jit(solution)/shard_map/ppermute | solution.py:21
  3.7 2.6 %collective-permute-start.3 = (s32[1,4]{1,0:T(1,128)}, s32[1,4]{1,0:T(1,128)S(1)}, u32[]{:S(2)}, u32[]{:S(2)}) collective-permute-start(s32[1,4]{1,0:T(1,128)} %param.13), channel_id=1, source_target_pairs={{0,8},{1,9},{2,10},{3,11},{4,12},{5,13},{6,14},{7,15},{8,0},{9,1},... | collective-permute-start | bytes 56 | tf_op jit(solution)/shard_map/ppermute | solution.py:21
  8.2 1.7 %collective-permute-done.2.i2 = s32[1,4]{1,0:T(1,128)S(1)} collective-permute-done((s32[1,4]{1,0:T(1,128)}, s32[1,4]{1,0:T(1,128)S(1)}, u32[]{:S(2)}, u32[]{:S(2)}) %collective-permute-start.2) | collective-permute-done | bytes 48 | tf_op jit(solution)/shard_map/ppermute | solution.py:21
  14.4 5.4 %shard_map.128 = (bf16[2,512,512]{2,1,0:T(8,128)(2,1)S(1)}, bf16[2,512,512]{2,1,0:T(8,128)(2,1)S(1)}, bf16[2,512,512]{2,1,0:T(8,128)(2,1)}, bf16[2,512,512]{2,1,...) custom-call(bf16[2,512,512]{2,1,0:T(8,128)(2,1)} %x_ref.2, ...), custom_call_target="tpu_custom_call" | custom-call | flops 5500000256 | bytes 500000 | tf_op jit(solution)/shard_map/pallas_call | solution.py:84
  19.8 9.1 %shard_map.129 = (bf16[4,2,512,1024]{3,2,1,0:T(8,128)(2,1)}, f32[2,8,64,512]{3,2,1,0:T(8,128)S(1)}, f32[2,8,8,512]{3,2,1,0:T(8,128)S(1)}, bf16[2,512,512]{2,1,0:...) custom-call(bf16[2,512,512]{2,1,0:T(8,128)(2,1)S(1)} %get-tuple-elem, ...), custom_call_target="tpu_custom_call" | custom-call | flops 11000000512 | bytes 1000000 | tf_op jit(solution)/shard_map/pallas_call | solution.py:220
  30.5 6.3 %shard_map.131 = (bf16[2,128,512]{2,1,0:T(8,128)(2,1)S(1)}, bf16[2,128,512]{2,1,0:T(8,128)(2,1)S(1)}, bf16[2,512,128]{2,1,0:T(8,128)(2,1)S(1)}, bf16[2,512,128]{...) custom-call(s32[4,8]{1,0:T(4,128)S(1)} %bitcast.2, ...), custom_call_target="tpu_custom_call" | custom-call | flops 6600000000 | bytes 600000 | tf_op jit(solution)/shard_map/pallas_call | solution.py:367
  36.8 6.3 %shard_map.132 = (bf16[2,128,512]{2,1,0:T(8,128)(2,1)S(1)}, bf16[2,128,512]{2,1,0:T(8,128)(2,1)S(1)}, bf16[2,512,128]{2,1,0:T(8,128)(2,1)S(1)}, bf16[2,512,128]{...) custom-call(s32[4,8]{1,0:T(4,128)S(1)} %bitcast.3, ...), custom_call_target="tpu_custom_call" | custom-call | flops 6600000000 | bytes 600000 | tf_op jit(solution)/shard_map/pallas_call | solution.py:367
  43.1 2.1 %shard_map.133 = (bf16[8,128,256]{2,1,0:T(8,128)(2,1)S(1)}, bf16[8,128,256]{2,1,0:T(8,128)(2,1)S(1)}) custom-call(s32[1]{0:T(128)} %bitcast.1.place_ref, bf16[2,512,512]{2,1,0:T(8,128)(2,1)S(1)} %get-tuple-element.132.refs_3_.xt_ref.refs_2_.refs_1_, bf16[2,512,512]{2,1,0:T(8,128)(2,1)S(1)} %get-tuple-element.129.refs_2_.xtp_ref.refs_1_.refs_0_, ...), custom_call_target="tpu_custom_call" | custom-call | flops 3300000000 | bytes 300000 | tf_op jit(solution)/shard_map/pallas_call | solution.py:422
  45.3 6.3 %shard_map.134 = (bf16[2,128,512]{2,1,0:T(8,128)(2,1)S(1)}, bf16[2,128,512]{2,1,0:T(8,128)(2,1)S(1)}, bf16[2,512,128]{2,1,0:T(8,128)(2,1)S(1)}, bf16[2,512,128]{...) custom-call(s32[4,8]{1,0:T(4,128)S(1)} %bitcast.4, ...), custom_call_target="tpu_custom_call" | custom-call | flops 6600000000 | bytes 600000 | tf_op jit(solution)/shard_map/pallas_call | solution.py:367
  53.3 6.2 %shard_map.135 = (bf16[2,128,512]{2,1,0:T(8,128)(2,1)S(1)}, bf16[2,128,512]{2,1,0:T(8,128)(2,1)S(1)}, bf16[2,512,128]{2,1,0:T(8,128)(2,1)S(1)}, bf16[2,512,128]{...) custom-call(s32[4,8]{1,0:T(4,128)S(1)} %bitcast.5, ...), custom_call_target="tpu_custom_call" | custom-call | flops 6600000000 | bytes 600000 | tf_op jit(solution)/shard_map/pallas_call | solution.py:367
  60.6 2.2 %shard_map.137 = (bf16[8,128,256]{2,1,0:T(8,128)(2,1)S(1)}, bf16[8,128,256]{2,1,0:T(8,128)(2,1)S(1)}) custom-call(s32[1]{0:T(128)} %bitcast.1.place_ref, bf16[2,512,512]{2,1,0:T(8,128)(2,1)S(1)} %get-tuple-element.132.refs_3_.xt_ref.refs_2_.refs_1_, bf16[2,512,512]{2,1,0:T(8,128)(2,1)S(1)} %get-tuple-element.129.refs_2_.xtp_ref.refs_1_.refs_0_, ...), custom_call_target="tpu_custom_call" | custom-call | flops 3300000000 | bytes 300000 | tf_op jit(solution)/shard_map/pallas_call | solution.py:422
  63.4 3.0 %collective-permute-start.14 = (bf16[1,128,256]{2,1,0:T(8,128)(2,1)S(1)}, bf16[1,128,256]{2,1,0:T(8,128)(2,1)S(1)}, u32[]{:S(2)}, u32[]{:S(2)}) collective-permute-start(bf16[1,128,256]{2,1,0:T(8,128)(2,1)S(1)} %get-tuple-element.200), channel_id=1, source_target_pairs={{0,12},{1,13},{2,14},{3,15},{4,8},{5,9},{6,10},{7,11},{8,4},{9,5},... | collective-permute-start | bytes 196616 | tf_op jit(solution)/shard_map/ppermute | solution.py:450
  70.8 2.3 %collective-permute-done.13 = bf16[1,128,256]{2,1,0:T(8,128)(2,1)S(1)} collective-permute-done((bf16[1,128,256]{2,1,0:T(8,128)(2,1)S(1)}, bf16[1,128,256]{2,1,0:T(8,128)(2,1)S(1)}, u32[]{:S(2)}, u32[]{:S(2)}) %collective-permute-start.13) | collective-permute-done | bytes 65568 | tf_op jit(solution)/shard_map/ppermute | solution.py:450
  73.1 1.7 %collective-permute-done.11 = bf16[4,128,256]{2,1,0:T(8,128)(2,1)S(1)} collective-permute-done((bf16[4,128,256]{2,1,0:T(8,128)(2,1)S(1)}, bf16[4,128,256]{2,1,0:T(8,128)(2,1)S(1)}, u32[]{:S(2)}, u32[]{:S(2)}) %collective-permute-start.11) | collective-permute-done | bytes 262176 | tf_op jit(solution)/shard_map/ppermute | solution.py:450
  74.9 1.7 %collective-permute-start.17 = (bf16[2,128,256]{2,1,0:T(8,128)(2,1)S(1)}, bf16[2,128,256]{2,1,0:T(8,128)(2,1)S(1)}, u32[]{:S(2)}, u32[]{:S(2)}) collective-permute-start(bf16[2,128,256]{2,1,0:T(8,128)(2,1)S(1)} %get-tuple-element.208), channel_id=1, source_target_pairs={{0,12},{1,13},{2,14},{3,15},{4,8},{5,9},{6,10},{7,11},{8,4},{9,5},... | collective-permute-start | bytes 393224 | tf_op jit(solution)/shard_map/ppermute | solution.py:450
  79.4 3.2 %shard_map.136 = (bf16[2,512,512]{2,1,0:T(8,128)(2,1)}, f32[2,512,512]{2,1,0:T(8,128)S(1)}) custom-call(bf16[2,128,512]{2,1,0:T(8,128)(2,1)S(1)} %get-tuple-element.130.refs_0_, bf16[2,128,512]{2,1,0:T(8,128)(2,1)S(1)} %get-tuple-element.133.refs_1_, bf16[2,128,512]{2,1,0:T(8,128)(2,1)S(1)} %get-tuple-element.147.refs_2_.refs_0_, ...), custom_call_target="tpu_custom_call" | custom-call | flops 4400000000 | bytes 400000 | tf_op jit(solution)/shard_map/pallas_call | solution.py:550
  84.2 3.5 %collective-permute-start.25 = (bf16[2,128,512]{2,1,0:T(8,128)(2,1)S(1)}, bf16[2,128,512]{2,1,0:T(8,128)(2,1)S(1)}, u32[]{:S(2)}, u32[]{:S(2)}) collective-permute-start(bf16[2,128,512]{2,1,0:T(8,128)(2,1)S(1)} %get-tuple-element.177), channel_id=1, source_target_pairs={{0,4},{1,5},{2,6},{3,7},{4,0},{5,1},{6,2},{7,3},{8,12},{9,13},{10,... | collective-permute-start | bytes 786440 | tf_op jit(solution)/shard_map/ppermute | solution.py:21
  89.1 2.3 %collective-permute-start.21 = (bf16[1,128,256]{2,1,0:T(8,128)(2,1)S(1)}, bf16[1,128,256]{2,1,0:T(8,128)(2,1)S(1)}, u32[]{:S(2)}, u32[]{:S(2)}) collective-permute-start(bf16[1,128,256]{2,1,0:T(8,128)(2,1)S(1)} %add_convert_fusion.4), channel_id=1, source_target_pairs={{0,12},{1,13},{2,14},{3,15},{4,8},{5,9},{6,10},{7,11},{8,4},{9,5},... | collective-permute-start | bytes 196616 | tf_op jit(solution)/shard_map/ppermute | solution.py:450
  91.3 2.1 %collective-permute-start.19 = (bf16[1,128,256]{2,1,0:T(8,128)(2,1)S(1)}, bf16[1,128,256]{2,1,0:T(8,128)(2,1)S(1)}, u32[]{:S(2)}, u32[]{:S(2)}) collective-permute-start(bf16[1,128,256]{2,1,0:T(8,128)(2,1)S(1)} %add_convert_fusion.4), channel_id=1, source_target_pairs={{0,4},{1,5},{2,6},{3,7},{4,0},{5,1},{6,2},{7,3},{8,12},{9,13},{10,... | collective-permute-start | bytes 196616 | tf_op jit(solution)/shard_map/ppermute | solution.py:450
  93.5 4.0 %collective-permute-done.21 = bf16[1,128,256]{2,1,0:T(8,128)(2,1)S(1)} collective-permute-done((bf16[1,128,256]{2,1,0:T(8,128)(2,1)S(1)}, bf16[1,128,256]{2,1,0:T(8,128)(2,1)S(1)}, u32[]{:S(2)}, u32[]{:S(2)}) %collective-permute-start.21) | collective-permute-done | bytes 65568 | tf_op jit(solution)/shard_map/ppermute | solution.py:450
  100.1 6.6 %collective-permute-done.24 = bf16[4,128,256]{2,1,0:T(8,128)(2,1)S(1)} collective-permute-done((bf16[4,128,256]{2,1,0:T(8,128)(2,1)S(1)}, bf16[4,128,256]{2,1,0:T(8,128)(2,1)S(1)}, u32[]{:S(2)}, u32[]{:S(2)}) %collective-permute-start.24) | collective-permute-done | bytes 262176 | tf_op jit(solution)/shard_map/ppermute | solution.py:450
  106.7 3.0 %collective-permute-done.26.b3 = bf16[2,128,512]{2,1,0:T(8,128)(2,1)S(1)} collective-permute-done((bf16[2,128,512]{2,1,0:T(8,128)(2,1)S(1)}, bf16[2,128,512]{2,1,0:T(8,128)(2,1)S(1)}, u32[]{:S(2)}, u32[]{:S(2)}) %collective-permute-start.26) | collective-permute-done | bytes 262176 | tf_op jit(solution)/shard_map/ppermute | solution.py:21
  110.3 1.8 %shard_map.139 = bf16[2,512,512]{2,1,0:T(8,128)(2,1)} custom-call(s32[1,4]{1,0:T(1,128)S(1)} %collective-permute-done.i0, s32[1,4]{1,0:T(1,128)S(1)} %collective-permute-done.1.i1, s32[1,4]{1,0:T(1,128)S(1)} %collective-permute-done.2.i2, s32[1,4]{1,0:T(1,128)S(1)} %collective-permute-done.3.i3, f32[2,512,512]{2,1,0:T(8,128)S(1)} %get-tuple-element.182.gt_ref, ...), custom_call_target="tpu_custom_call" | custom-call | tf_op jit(solution)/shard_map/pallas_call | solution.py:573
  112.5 2.4 %shard_map.140 = (f32[512,512]{1,0:T(8,128)}, f32[512,512]{1,0:T(8,128)}, f32[512,512]{1,0:T(8,128)}, f32[512,512]{1,0:T(8,128)}) custom-call(s32[1]{0:T(128)} %bitcast.1.place_ref, bf16[8,128,256]{2,1,0:T(8,128)(2,1)S(1)} %constant_dynamic-update-slice_fusion.5.refs_0_, bf16[8,128,256]{2,1,0:T(8,128)(2,1)S(1)} %collective-permute-done.28.refs_1_, ...), custom_call_target="tpu_custom_call" | custom-call | tf_op jit(solution)/shard_map/pallas_call | solution.py:494
  (80 shorter events, 25.2 us)
Async XLA Ops:
  0.6 7.2 %collective-permute-start.1 = (s32[1,4]{1,0:T(1,128)}, s32[1,4]{1,0:T(1,128)S(1)}, u32[]{:S(2)}, u32[]{:S(2)}) collective-permute-start(s32[1,4]{1,0:T(1,128)} %param.13), channel_id=1, source_target_pairs={{0,2},{1,3},{2,0},{3,1},{4,6},{5,7},{6,4},{7,5},{8,10},{9,11},{10,... | collective-permute-start | bytes 56 | tf_op jit(solution)/shard_map/ppermute | solution.py:21
  3.7 4.6 %collective-permute-start.3 = (s32[1,4]{1,0:T(1,128)}, s32[1,4]{1,0:T(1,128)S(1)}, u32[]{:S(2)}, u32[]{:S(2)}) collective-permute-start(s32[1,4]{1,0:T(1,128)} %param.13), channel_id=1, source_target_pairs={{0,8},{1,9},{2,10},{3,11},{4,12},{5,13},{6,14},{7,15},{8,0},{9,1},... | collective-permute-start | bytes 56 | tf_op jit(solution)/shard_map/ppermute | solution.py:21
  11.2 17.6 %collective-permute-start.4 = (bf16[2,128,512]{2,1,0:T(8,128)(2,1)S(1)}, bf16[2,128,512]{2,1,0:T(8,128)(2,1)S(1)}, u32[]{:S(2)}, u32[]{:S(2)}) collective-permute-start(bf16[2,128,512]{2,1,0:T(8,128)(2,1)S(1)} %get-tuple-element.104), channel_id=1, source_target_pairs={{0,1},{1,0},{2,3},{3,2},{4,5},{5,4},{6,7},{7,6},{8,9},{9,8},{10,11... | collective-permute-start | bytes 786440 | tf_op jit(solution)/shard_map/ppermute | solution.py:21
  11.3 17.6 %collective-permute-start.5 = (bf16[2,128,512]{2,1,0:T(8,128)(2,1)S(1)}, bf16[2,128,512]{2,1,0:T(8,128)(2,1)S(1)}, u32[]{:S(2)}, u32[]{:S(2)}) collective-permute-start(bf16[2,128,512]{2,1,0:T(8,128)(2,1)S(1)} %get-tuple-element.105), channel_id=1, source_target_pairs={{0,2},{1,3},{2,0},{3,1},{4,6},{5,7},{6,4},{7,5},{8,10},{9,11},{10,... | collective-permute-start | bytes 786440 | tf_op jit(solution)/shard_map/ppermute | solution.py:21
  11.9 17.0 %collective-permute-start.6 = (bf16[2,128,512]{2,1,0:T(8,128)(2,1)S(1)}, bf16[2,128,512]{2,1,0:T(8,128)(2,1)S(1)}, u32[]{:S(2)}, u32[]{:S(2)}) collective-permute-start(bf16[2,128,512]{2,1,0:T(8,128)(2,1)S(1)} %get-tuple-element.106), channel_id=1, source_target_pairs={{0,4},{1,5},{2,6},{3,7},{4,0},{5,1},{6,2},{7,3},{8,12},{9,13},{10,... | collective-permute-start | bytes 786440 | tf_op jit(solution)/shard_map/ppermute | solution.py:21
  13.5 15.4 %collective-permute-start.7 = (bf16[2,128,512]{2,1,0:T(8,128)(2,1)S(1)}, bf16[2,128,512]{2,1,0:T(8,128)(2,1)S(1)}, u32[]{:S(2)}, u32[]{:S(2)}) collective-permute-start(bf16[2,128,512]{2,1,0:T(8,128)(2,1)S(1)} %get-tuple-element.107), channel_id=1, source_target_pairs={{0,8},{1,9},{2,10},{3,11},{4,12},{5,13},{6,14},{7,15},{8,0},{9,1},... | collective-permute-start | bytes 786440 | tf_op jit(solution)/shard_map/ppermute | solution.py:21
  45.2 6.3 %collective-permute-start.8 = (bf16[8,128,256]{2,1,0:T(8,128)(2,1)S(1)}, bf16[8,128,256]{2,1,0:T(8,128)(2,1)S(1)}, u32[]{:S(2)}, u32[]{:S(2)}) collective-permute-start(bf16[8,128,256]{2,1,0:T(8,128)(2,1)S(1)} %get-tuple-element.146.refs_4_), channel_id=1, source_target_pairs={{0,1},{1,0},{2,3},{3,2},{4,5},{5,4},{6,7},{7,6},{8,9},{9,8},{10,11... | collective-permute-start | bytes 1572872 | tf_op jit(solution)/shard_map/ppermute | solution.py:450
  51.7 8.8 %collective-permute-start.9 = (bf16[4,128,256]{2,1,0:T(8,128)(2,1)S(1)}, bf16[4,128,256]{2,1,0:T(8,128)(2,1)S(1)}, u32[]{:S(2)}, u32[]{:S(2)}) collective-permute-start(bf16[4,128,256]{2,1,0:T(8,128)(2,1)S(1)} %slice.76.refs_3_), channel_id=1, source_target_pairs={{0,2},{1,3},{2,0},{3,1},{4,6},{5,7},{6,4},{7,5},{8,10},{9,11},{10,... | collective-permute-start | bytes 786440 | tf_op jit(solution)/shard_map/ppermute | solution.py:450
  62.9 6.9 %collective-permute-start.12 = (bf16[1,128,256]{2,1,0:T(8,128)(2,1)S(1)}, bf16[1,128,256]{2,1,0:T(8,128)(2,1)S(1)}, u32[]{:S(2)}, u32[]{:S(2)}) collective-permute-start(bf16[1,128,256]{2,1,0:T(8,128)(2,1)S(1)} %get-tuple-element.199), channel_id=1, source_target_pairs={{0,4},{1,5},{2,6},{3,7},{4,0},{5,1},{6,2},{7,3},{8,12},{9,13},{10,... | collective-permute-start | bytes 196616 | tf_op jit(solution)/shard_map/ppermute | solution.py:450
  63.4 7.4 %collective-permute-start.14 = (bf16[1,128,256]{2,1,0:T(8,128)(2,1)S(1)}, bf16[1,128,256]{2,1,0:T(8,128)(2,1)S(1)}, u32[]{:S(2)}, u32[]{:S(2)}) collective-permute-start(bf16[1,128,256]{2,1,0:T(8,128)(2,1)S(1)} %get-tuple-element.200), channel_id=1, source_target_pairs={{0,12},{1,13},{2,14},{3,15},{4,8},{5,9},{6,10},{7,11},{8,4},{9,5},... | collective-permute-start | bytes 196616 | tf_op jit(solution)/shard_map/ppermute | solution.py:450
  66.4 6.7 %collective-permute-start.13 = (bf16[1,128,256]{2,1,0:T(8,128)(2,1)S(1)}, bf16[1,128,256]{2,1,0:T(8,128)(2,1)S(1)}, u32[]{:S(2)}, u32[]{:S(2)}) collective-permute-start(bf16[1,128,256]{2,1,0:T(8,128)(2,1)S(1)} %get-tuple-element.201), channel_id=1, source_target_pairs={{0,8},{1,9},{2,10},{3,11},{4,12},{5,13},{6,14},{7,15},{8,0},{9,1},... | collective-permute-start | bytes 196616 | tf_op jit(solution)/shard_map/ppermute | solution.py:450
  66.6 8.2 %collective-permute-start.11 = (bf16[4,128,256]{2,1,0:T(8,128)(2,1)S(1)}, bf16[4,128,256]{2,1,0:T(8,128)(2,1)S(1)}, u32[]{:S(2)}, u32[]{:S(2)}) collective-permute-start(bf16[4,128,256]{2,1,0:T(8,128)(2,1)S(1)} %slice.79), channel_id=1, source_target_pairs={{0,2},{1,3},{2,0},{3,1},{4,6},{5,7},{6,4},{7,5},{8,10},{9,11},{10,... | collective-permute-start | bytes 786440 | tf_op jit(solution)/shard_map/ppermute | solution.py:450
  74.9 9.2 %collective-permute-start.17 = (bf16[2,128,256]{2,1,0:T(8,128)(2,1)S(1)}, bf16[2,128,256]{2,1,0:T(8,128)(2,1)S(1)}, u32[]{:S(2)}, u32[]{:S(2)}) collective-permute-start(bf16[2,128,256]{2,1,0:T(8,128)(2,1)S(1)} %get-tuple-element.208), channel_id=1, source_target_pairs={{0,12},{1,13},{2,14},{3,15},{4,8},{5,9},{6,10},{7,11},{8,4},{9,5},... | collective-permute-start | bytes 393224 | tf_op jit(solution)/shard_map/ppermute | solution.py:450
  76.6 12.0 %collective-permute-start.16 = (bf16[2,128,256]{2,1,0:T(8,128)(2,1)S(1)}, bf16[2,128,256]{2,1,0:T(8,128)(2,1)S(1)}, u32[]{:S(2)}, u32[]{:S(2)}) collective-permute-start(bf16[2,128,256]{2,1,0:T(8,128)(2,1)S(1)} %get-tuple-element.209), channel_id=1, source_target_pairs={{0,8},{1,9},{2,10},{3,11},{4,12},{5,13},{6,14},{7,15},{8,0},{9,1},... | collective-permute-start | bytes 393224 | tf_op jit(solution)/shard_map/ppermute | solution.py:450
  77.7 10.9 %collective-permute-start.15 = (bf16[2,128,256]{2,1,0:T(8,128)(2,1)S(1)}, bf16[2,128,256]{2,1,0:T(8,128)(2,1)S(1)}, u32[]{:S(2)}, u32[]{:S(2)}) collective-permute-start(bf16[2,128,256]{2,1,0:T(8,128)(2,1)S(1)} %get-tuple-element.210), channel_id=1, source_target_pairs={{0,4},{1,5},{2,6},{3,7},{4,0},{5,1},{6,2},{7,3},{8,12},{9,13},{10,... | collective-permute-start | bytes 393224 | tf_op jit(solution)/shard_map/ppermute | solution.py:450
  82.6 6.4 %collective-permute-start.18 = (bf16[2,128,512]{2,1,0:T(8,128)(2,1)S(1)}, bf16[2,128,512]{2,1,0:T(8,128)(2,1)S(1)}, u32[]{:S(2)}, u32[]{:S(2)}) collective-permute-start(bf16[2,128,512]{2,1,0:T(8,128)(2,1)S(1)} %get-tuple-element.173), channel_id=1, source_target_pairs={{0,2},{1,3},{2,0},{3,1},{4,6},{5,7},{6,4},{7,5},{8,10},{9,11},{10,... | collective-permute-start | bytes 786440 | tf_op jit(solution)/shard_map/ppermute | solution.py:21
  84.2 25.6 %collective-permute-start.23 = (bf16[2,128,512]{2,1,0:T(8,128)(2,1)S(1)}, bf16[2,128,512]{2,1,0:T(8,128)(2,1)S(1)}, u32[]{:S(2)}, u32[]{:S(2)}) collective-permute-start(bf16[2,128,512]{2,1,0:T(8,128)(2,1)S(1)} %get-tuple-element.175), channel_id=1, source_target_pairs={{0,1},{1,0},{2,3},{3,2},{4,5},{5,4},{6,7},{7,6},{8,9},{9,8},{10,11... | collective-permute-start | bytes 786440 | tf_op jit(solution)/shard_map/ppermute | solution.py:21
  84.2 22.6 %collective-permute-start.25 = (bf16[2,128,512]{2,1,0:T(8,128)(2,1)S(1)}, bf16[2,128,512]{2,1,0:T(8,128)(2,1)S(1)}, u32[]{:S(2)}, u32[]{:S(2)}) collective-permute-start(bf16[2,128,512]{2,1,0:T(8,128)(2,1)S(1)} %get-tuple-element.177), channel_id=1, source_target_pairs={{0,4},{1,5},{2,6},{3,7},{4,0},{5,1},{6,2},{7,3},{8,12},{9,13},{10,... | collective-permute-start | bytes 786440 | tf_op jit(solution)/shard_map/ppermute | solution.py:21
  89.1 8.4 %collective-permute-start.21 = (bf16[1,128,256]{2,1,0:T(8,128)(2,1)S(1)}, bf16[1,128,256]{2,1,0:T(8,128)(2,1)S(1)}, u32[]{:S(2)}, u32[]{:S(2)}) collective-permute-start(bf16[1,128,256]{2,1,0:T(8,128)(2,1)S(1)} %add_convert_fusion.4), channel_id=1, source_target_pairs={{0,12},{1,13},{2,14},{3,15},{4,8},{5,9},{6,10},{7,11},{8,4},{9,5},... | collective-permute-start | bytes 196616 | tf_op jit(solution)/shard_map/ppermute | solution.py:450
  91.3 6.6 %collective-permute-start.20 = (bf16[1,128,256]{2,1,0:T(8,128)(2,1)S(1)}, bf16[1,128,256]{2,1,0:T(8,128)(2,1)S(1)}, u32[]{:S(2)}, u32[]{:S(2)}) collective-permute-start(bf16[1,128,256]{2,1,0:T(8,128)(2,1)S(1)} %add_convert_fusion.4), channel_id=1, source_target_pairs={{0,8},{1,9},{2,10},{3,11},{4,12},{5,13},{6,14},{7,15},{8,0},{9,1},... | collective-permute-start | bytes 196616 | tf_op jit(solution)/shard_map/ppermute | solution.py:450
  91.3 8.2 %collective-permute-start.19 = (bf16[1,128,256]{2,1,0:T(8,128)(2,1)S(1)}, bf16[1,128,256]{2,1,0:T(8,128)(2,1)S(1)}, u32[]{:S(2)}, u32[]{:S(2)}) collective-permute-start(bf16[1,128,256]{2,1,0:T(8,128)(2,1)S(1)} %add_convert_fusion.4), channel_id=1, source_target_pairs={{0,4},{1,5},{2,6},{3,7},{4,0},{5,1},{6,2},{7,3},{8,12},{9,13},{10,... | collective-permute-start | bytes 196616 | tf_op jit(solution)/shard_map/ppermute | solution.py:450
  97.5 12.2 %collective-permute-start.26 = (bf16[2,128,512]{2,1,0:T(8,128)(2,1)S(1)}, bf16[2,128,512]{2,1,0:T(8,128)(2,1)S(1)}, u32[]{:S(2)}, u32[]{:S(2)}) collective-permute-start(bf16[2,128,512]{2,1,0:T(8,128)(2,1)S(1)} %get-tuple-element.178), channel_id=1, source_target_pairs={{0,8},{1,9},{2,10},{3,11},{4,12},{5,13},{6,14},{7,15},{8,0},{9,1},... | collective-permute-start | bytes 786440 | tf_op jit(solution)/shard_map/ppermute | solution.py:21
  98.0 8.7 %collective-permute-start.24 = (bf16[4,128,256]{2,1,0:T(8,128)(2,1)S(1)}, bf16[4,128,256]{2,1,0:T(8,128)(2,1)S(1)}, u32[]{:S(2)}, u32[]{:S(2)}) collective-permute-start(bf16[4,128,256]{2,1,0:T(8,128)(2,1)S(1)} %pad_maximum_fusion.1), channel_id=1, source_target_pairs={{0,2},{1,3},{2,0},{3,1},{4,6},{5,7},{6,4},{7,5},{8,10},{9,11},{10,... | collective-permute-start | bytes 786440 | tf_op jit(solution)/shard_map/ppermute | solution.py:450
  99.5 10.2 %collective-permute-start.22 = (bf16[4,128,256]{2,1,0:T(8,128)(2,1)S(1)}, bf16[4,128,256]{2,1,0:T(8,128)(2,1)S(1)}, u32[]{:S(2)}, u32[]{:S(2)}) collective-permute-start(bf16[4,128,256]{2,1,0:T(8,128)(2,1)S(1)} %pad_maximum_fusion), channel_id=1, source_target_pairs={{0,2},{1,3},{2,0},{3,1},{4,6},{5,7},{6,4},{7,5},{8,10},{9,11},{10,... | collective-permute-start | bytes 786440 | tf_op jit(solution)/shard_map/ppermute | solution.py:450
  (10 other events, 48.5 us)

commit v5 on v4

--- a/solution.py
+++ b/solution.py
@@ -99,10 +99,8 @@
     return copies
 
 
-def project_partner_kernel(loads, x0, x1, x2, x3, wk_ref, wv_ref, *refs):
-    k_ref, v_ref, kt_ref, vt_ref, xt_ref, *targets, sem = refs[-6 - loads :]
-    sources = refs[:loads]
-    copies = bring([sources[0].at[0], *sources[1:]], targets, sem)
+def project_partner_kernel(x0, x1, x2, x3, wk_ref, wv_ref, *refs):
+    k_ref, v_ref, kt_ref, vt_ref, xt_ref = refs[-5:]
     for s in range(x0.shape[0]):
         x = jnp.concatenate([x0[s], x1[s], x2[s], x3[s]], 0)
         xt_ref[s] = x.T
@@ -112,27 +110,22 @@
         v_ref[s] = v.astype(BF16)
         kt_ref[s] = k.T.astype(BF16)
         vt_ref[s] = v.T.astype(BF16)
-    for copy in copies:
-        copy.wait()
-
-
-def project_partner(arrived, w_key, w_value, loads, held):
+
+
+def project_partner(arrived, w_key, w_value, held):
     samples, sub_rows, width = arrived[0].shape
     rows = sub_rows * len(arrived)
     whole = pl.BlockSpec(memory_space=pltpu.VMEM)
-    anywhere = pl.BlockSpec(memory_space=pl.ANY)
     by_row = pltpu.VMEM((samples, rows, width), BF16)
     by_col = pltpu.VMEM((samples, width, rows), BF16)
     return pl.pallas_call(
-        functools.partial(project_partner_kernel, len(loads)),
-        in_specs=[whole] * 6 + [anywhere] * len(loads) + [whole] * len(held),
-        out_specs=[whole] * (5 + len(loads)),
-        out_shape=[by_row, by_row, by_col, by_col, by_col, pltpu.VMEM(loads[0].shape[1:], BF16)]
-        + [pltpu.VMEM(x.shape, x.dtype) for x in loads[1:]],
-        scratch_shapes=[pltpu.SemaphoreType.DMA((len(loads),))],
+        project_partner_kernel,
+        in_specs=[whole] * (6 + len(held)),
+        out_specs=[whole] * 5,
+        out_shape=[by_row, by_row, by_col, by_col, by_col],
         cost_estimate=cost(2.5),
         compiler_params=params(),
-    )(*near(*arrived, w_key, w_value), *far(*loads), *near(*held))
+    )(*near(*arrived, w_key, w_value), *near(*held))
 
 
 def weave(*streams):
@@ -146,8 +139,8 @@
 
 
 def own_kernel(head_width, qt_ref, k_ref, vt_ref, *refs):
-    loads = (len(refs) - 5) // 2
-    e_ref, o_ref, st_ref, *targets, s_ref, sem = refs[loads:]
+    loads = (len(refs) - 8) // 2
+    e_ref, e0_ref, o_ref, st_ref, *targets, s_ref, buf_ref, sem, e_sem = refs[loads:]
     copies = [pltpu.make_async_copy(src, dst, sem.at[i]) for i, (src, dst) in enumerate(zip(refs[:loads], targets))]
 
     @pl.when(pl.program_id(0) == 0)
@@ -158,7 +151,7 @@
     samples, width, rows = qt_ref.shape
     units = [(sample, which) for sample in range(samples) for which in range(2)]
 
-    def one_pair(pair):
+    def one_pair(pair, put_ref):
         first = pl.multiple_of(pair * 2 * head_width, 2 * head_width)
         tops = {}
 
@@ -182,7 +175,7 @@
                 e = jnp.exp(s_ref[which, at : at + TILE, :] - tops[unit])
                 part = down8(e, jnp.sum)
                 total = part if total is None else total + part
-                e_ref[0, sample, at : at + TILE, cols] = e.astype(BF16)
+                put_ref[sample, at : at + TILE, cols] = e.astype(BF16)
                 yield
             total = jnp.sum(total, axis=0, keepdims=True)
             st_ref[sample, 2 * pair + which] = jnp.concatenate([tops[unit], total, jnp.zeros((6, rows), F32)], 0)
@@ -191,7 +184,7 @@
             sample, which = unit
             cols = slice(which * rows, (which + 1) * rows)
             span = pl.ds(first + which * head_width, head_width)
-            o_ref[sample, 2 * pair + which] = nn(vt_ref[sample, span, :], e_ref[0, sample, :, cols])
+            o_ref[sample, 2 * pair + which] = nn(vt_ref[sample, span, :], put_ref[sample, :, cols])
             yield
 
         count = len(units)
@@ -205,10 +198,22 @@
                 streams.append(out(units[i - 2]))
             weave(*streams)
 
-    one_pair(pl.program_id(0))
-
-    @pl.when(pl.program_id(0) == pl.num_programs(0) - 1)
+    step = pl.program_id(0)
+    away = buf_ref.shape[0]
+
+    def move(number):
+        return pltpu.make_async_copy(buf_ref.at[number], e_ref.at[number], e_sem.at[number])
+
+    @pl.when(step < away)
     def _():
+        one_pair(step + 1, buf_ref.at[step])
+        move(step).start()
+
+    @pl.when(step == away)
+    def _():
+        one_pair(0, e0_ref)
+        for number in range(away):
+            move(number).wait()
         for copy in copies:
             copy.wait()
 
@@ -221,14 +226,20 @@
         functools.partial(own_kernel, head_width),
         grid=(head_count // 2,),
         in_specs=[whole] * 3 + [pl.BlockSpec(memory_space=pl.ANY)] * len(loads),
-        out_specs=[pl.BlockSpec((1, samples, rows, 2 * rows), lambda p: (p, 0, 0, 0))] + [whole] * (2 + len(loads)),
+        out_specs=[pl.BlockSpec(memory_space=pl.ANY)] + [whole] * (3 + len(loads)),
         out_shape=[
-            pltpu.HBM((head_count // 2, samples, rows, 2 * rows), BF16),
+            pltpu.HBM((head_count // 2 - 1, samples, rows, 2 * rows), BF16),
+            pltpu.VMEM((samples, rows, 2 * rows), BF16),
             pltpu.VMEM((samples, head_count, head_width, rows), F32),
             pltpu.VMEM((samples, head_count, 8, rows), F32),
         ]
         + [pltpu.VMEM(x.shape, x.dtype) for x in loads],
-        scratch_shapes=[pltpu.VMEM((2, rows, rows), F32), pltpu.SemaphoreType.DMA((len(loads),))],
+        scratch_shapes=[
+            pltpu.VMEM((2, rows, rows), F32),
+            pltpu.VMEM((head_count // 2 - 1, samples, rows, 2 * rows), BF16),
+            pltpu.SemaphoreType.DMA((len(loads),)),
+            pltpu.SemaphoreType.DMA((head_count // 2 - 1,)),
+        ],
         cost_estimate=cost(10),
         compiler_params=params("arbitrary"),
     )(*near(qt, k, vt), *far(*loads))
@@ -242,7 +253,7 @@
     loads = sem.shape[0]
     targets = refs[-6 - loads : -6]
     ctx_ref, dqt_ref, dko_ref, dvo_ref, dkp_ref, dvp_ref = refs[-12 - loads : -6 - loads]
-    sources = [x.at[pair + 1] if len(x.shape) == 4 else x for x in refs[:loads]]
+    sources = [x.at[pair] if len(x.shape) == 4 else x for x in refs[:loads]]
     copies = bring(sources, targets, sem)
     sections = mask_ref.shape[0]
     samples, _, rows = qt_ref.shape
@@ -611,8 +622,8 @@
     first_tokens, *picked = tie(tokens, *picked)
     arrived = [partner(picked[section], levels - 4 + section) for section in (3, 2, 1, 0)][::-1]
     qt, ko, vo, kto, vto, dot, xt = project(first_tokens, cotangent, w_query, w_key, w_value, w_out, scale)
-    e_all, *stats, vo, kto, dot, near_key, near_value = own_part(qt, ko, vto, head_count, [vo, kto, dot, w_key, w_value])
-    kp, vp, ktp, vtp, xtp, e = project_partner(arrived, near_key, near_value, [e_all], [*stats, qt, vo, kto, dot])
+    e_all, e, *stats, vo, kto, dot, near_key, near_value = own_part(qt, ko, vto, head_count, [vo, kto, dot, w_key, w_value])
+    kp, vp, ktp, vtp, xtp = project_partner(arrived, near_key, near_value, [e, *stats, qt, vo, kto, dot])
 
     def run(pair, e, loads, held, after=()):
         out = attend(
@@ -669,7 +680,6 @@
     kept1, *backs[1:2] = tie(kept1, *backs[1:2])
     pieces1 = gather_all(kept1, plan[2])
     mine0 = jnp.concatenate(pieces0, 0)
-    mine0, *backs[2:] = tie(mine0, *backs[2:])
     pieces0 = gather_all(mine0, plan[0])
     pieces1 = gather_all(jnp.concatenate(pieces1, 0), plan[1])
     mine1, *backs = tie(jnp.concatenate(pieces1, 0), *backs)

time: 115 us -> 116 us (level)
  starting transfers between devices: 33.8 us -> 37.9 us
  Pallas kernels: 55.6 us -> 53.6 us
    ppermute x17, starting transfers between devices: 18.3 us -> 23 us  [exchange(): lax.ppermute(x, 'tok', [(i, i ^ mask) for i in range(lax.axis_size('tok'))])]
    ppermute x12, waiting for transfers between devices: 5.42 us -> 3.4 us  [partner(): lax.ppermute(x, 'tok', [(i, i ^ 1 << stride) for i in range(lax.axis_size...]
    pallas_call x1, Pallas kernels: 9.1 us -> 7.22 us  [own_part(): pl.pallas_call(functools.partial(own_kernel, head_width), grid=(head_coun...]
  transfers between devices with their start and end apart: 29 -> 29, of which waited for: 13 -> 13; matrix products, arithmetic and copies ran while one was open for 0% -> 0% of each run, Pallas kernels for 29% -> 27%
where the time goes in v5:
time: 116 us
  Pallas kernels  53.6 us (46%)
  starting transfers between devices  37.9 us (33%)
  waiting for transfers between devices  22.6 us (19%)
    pallas_call x4, Pallas kernels, attend(): pl.pallas_call(functools.partial(attend_kernel, pair, head_width, scale),...  25 us
    ppermute x17, starting transfers between devices, exchange(): lax.ppermute(x, 'tok', [(i, i ^ mask) for i in range(lax.axis_size('tok'))])  23 us
    ppermute x17, waiting for transfers between devices, exchange(): lax.ppermute(x, 'tok', [(i, i ^ mask) for i in range(lax.axis_size('tok'))])  19.2 us
    ppermute x12, starting transfers between devices, partner(): lax.ppermute(x, 'tok', [(i, i ^ 1 << stride) for i in range(lax.axis_size...  15 us
    pallas_call x1, Pallas kernels, own_part(): pl.pallas_call(functools.partial(own_kernel, head_width), grid=(head_coun...  7.22 us
    pallas_call x1, Pallas kernels, project(): pl.pallas_call(functools.partial(project_kernel, scale), grid=(samples,),...  5.38 us
    pallas_call x2, Pallas kernels, weight_grads(): pl.pallas_call(functools.partial(weights_kernel, pairs), in_specs=[pl.Blo...  4.31 us
    ppermute x12, waiting for transfers between devices, partner(): lax.ppermute(x, 'tok', [(i, i ^ 1 << stride) for i in range(lax.axis_size...  3.4 us
  transfers between devices with their start and end apart: 29, of which 13 were waited for; matrix products, arithmetic and copies ran while one was open for 0% of the time, Pallas kernels for 27%

profile of v5, /device:TPU:0, one launch (start us, length us, event | category | flops | bytes accessed | tf_op | source)
XLA Modules:
  0.0 116.0 jit_solution(10567000270159291848)
XLA Ops:
  0.6 3.0 %collective-permute-start.1 = (s32[1,4]{1,0:T(1,128)}, s32[1,4]{1,0:T(1,128)S(1)}, u32[]{:S(2)}, u32[]{:S(2)}) collective-permute-start(s32[1,4]{1,0:T(1,128)} %param.13), channel_id=1, source_target_pairs={{0,2},{1,3},{2,0},{3,1},{4,6},{5,7},{6,4},{7,5},{8,10},{9,11},{10,... | collective-permute-start | bytes 56 | tf_op jit(solution)/shard_map/ppermute | solution.py:21
  3.7 2.6 %collective-permute-start.3 = (s32[1,4]{1,0:T(1,128)}, s32[1,4]{1,0:T(1,128)S(1)}, u32[]{:S(2)}, u32[]{:S(2)}) collective-permute-start(s32[1,4]{1,0:T(1,128)} %param.13), channel_id=1, source_target_pairs={{0,8},{1,9},{2,10},{3,11},{4,12},{5,13},{6,14},{7,15},{8,0},{9,1},... | collective-permute-start | bytes 56 | tf_op jit(solution)/shard_map/ppermute | solution.py:21
  8.2 1.7 %collective-permute-done.2.i2 = s32[1,4]{1,0:T(1,128)S(1)} collective-permute-done((s32[1,4]{1,0:T(1,128)}, s32[1,4]{1,0:T(1,128)S(1)}, u32[]{:S(2)}, u32[]{:S(2)}) %collective-permute-start.2) | collective-permute-done | bytes 48 | tf_op jit(solution)/shard_map/ppermute | solution.py:21
  14.4 5.4 %shard_map.128 = (bf16[2,512,512]{2,1,0:T(8,128)(2,1)S(1)}, bf16[2,512,512]{2,1,0:T(8,128)(2,1)S(1)}, bf16[2,512,512]{2,1,0:T(8,128)(2,1)}, bf16[2,512,512]{2,1,...) custom-call(bf16[2,512,512]{2,1,0:T(8,128)(2,1)} %x_ref.2, ...), custom_call_target="tpu_custom_call" | custom-call | flops 5500000256 | bytes 500000 | tf_op jit(solution)/shard_map/pallas_call | solution.py:84
  19.8 7.2 %shard_map.129 = (bf16[3,2,512,1024]{3,2,1,0:T(8,128)(2,1)}, bf16[2,512,1024]{2,1,0:T(8,128)(2,1)S(1)}, f32[2,8,64,512]{3,2,1,0:T(8,128)S(1)}, f32[2,8,8,512]{3,...) custom-call(bf16[2,512,512]{2,1,0:T(8,128)(2,1)S(1)} %get-tuple-elem, ...), custom_call_target="tpu_custom_call" | custom-call | flops 11000000512 | bytes 1000000 | tf_op jit(solution)/shard_map/pallas_call | solution.py:225
  29.5 6.3 %shard_map.131 = (bf16[2,128,512]{2,1,0:T(8,128)(2,1)S(1)}, bf16[2,128,512]{2,1,0:T(8,128)(2,1)S(1)}, bf16[2,512,128]{2,1,0:T(8,128)(2,1)S(1)}, bf16[2,512,128]{...) custom-call(s32[4,8]{1,0:T(4,128)S(1)} %bitcast.2, ...), custom_call_target="tpu_custom_call" | custom-call | flops 6600000000 | bytes 600000 | tf_op jit(solution)/shard_map/pallas_call | solution.py:378
  35.8 6.3 %shard_map.132 = (bf16[2,128,512]{2,1,0:T(8,128)(2,1)S(1)}, bf16[2,128,512]{2,1,0:T(8,128)(2,1)S(1)}, bf16[2,512,128]{2,1,0:T(8,128)(2,1)S(1)}, bf16[2,512,128]{...) custom-call(s32[4,8]{1,0:T(4,128)S(1)} %bitcast.3, ...), custom_call_target="tpu_custom_call" | custom-call | flops 6600000000 | bytes 600000 | tf_op jit(solution)/shard_map/pallas_call | solution.py:378
  42.1 2.1 %shard_map.133 = (bf16[8,128,256]{2,1,0:T(8,128)(2,1)S(1)}, bf16[8,128,256]{2,1,0:T(8,128)(2,1)S(1)}) custom-call(s32[1]{0:T(128)} %bitcast.1.place_ref, bf16[2,512,512]{2,1,0:T(8,128)(2,1)S(1)} %get-tuple-element.129.refs_3_.xt_ref.refs_2_.refs_1_, bf16[2,512,512]{2,1,0:T(8,128)(2,1)S(1)} %get-tuple-element.126.refs_2_.xtp_ref.refs_1_.refs_0_, ...), custom_call_target="tpu_custom_call" | custom-call | flops 3300000000 | bytes 300000 | tf_op jit(solution)/shard_map/pallas_call | solution.py:433
  44.3 6.3 %shard_map.134 = (bf16[2,128,512]{2,1,0:T(8,128)(2,1)S(1)}, bf16[2,128,512]{2,1,0:T(8,128)(2,1)S(1)}, bf16[2,512,128]{2,1,0:T(8,128)(2,1)S(1)}, bf16[2,512,128]{...) custom-call(s32[4,8]{1,0:T(4,128)S(1)} %bitcast.4, ...), custom_call_target="tpu_custom_call" | custom-call | flops 6600000000 | bytes 600000 | tf_op jit(solution)/shard_map/pallas_call | solution.py:378
  52.4 6.2 %shard_map.135 = (bf16[2,128,512]{2,1,0:T(8,128)(2,1)S(1)}, bf16[2,128,512]{2,1,0:T(8,128)(2,1)S(1)}, bf16[2,512,128]{2,1,0:T(8,128)(2,1)S(1)}, bf16[2,512,128]{...) custom-call(s32[4,8]{1,0:T(4,128)S(1)} %bitcast.5, ...), custom_call_target="tpu_custom_call" | custom-call | flops 6600000000 | bytes 600000 | tf_op jit(solution)/shard_map/pallas_call | solution.py:378
  59.6 2.2 %shard_map.137 = (bf16[8,128,256]{2,1,0:T(8,128)(2,1)S(1)}, bf16[8,128,256]{2,1,0:T(8,128)(2,1)S(1)}) custom-call(s32[1]{0:T(128)} %bitcast.1.place_ref, bf16[2,512,512]{2,1,0:T(8,128)(2,1)S(1)} %get-tuple-element.129.refs_3_.xt_ref.refs_2_.refs_1_, bf16[2,512,512]{2,1,0:T(8,128)(2,1)S(1)} %get-tuple-element.126.refs_2_.xtp_ref.refs_1_.refs_0_, ...), custom_call_target="tpu_custom_call" | custom-call | flops 3300000000 | bytes 300000 | tf_op jit(solution)/shard_map/pallas_call | solution.py:433
  62.0 2.4 %collective-permute-start.14 = (bf16[1,128,256]{2,1,0:T(8,128)(2,1)S(1)}, bf16[1,128,256]{2,1,0:T(8,128)(2,1)S(1)}, u32[]{:S(2)}, u32[]{:S(2)}) collective-permute-start(bf16[1,128,256]{2,1,0:T(8,128)(2,1)S(1)} %get-tuple-element.194), channel_id=1, source_target_pairs={{0,12},{1,13},{2,14},{3,15},{4,8},{5,9},{6,10},{7,11},{8,4},{9,5},... | collective-permute-start | bytes 196616 | tf_op jit(solution)/shard_map/ppermute | solution.py:461
  68.8 3.0 %collective-permute-done.13 = bf16[1,128,256]{2,1,0:T(8,128)(2,1)S(1)} collective-permute-done((bf16[1,128,256]{2,1,0:T(8,128)(2,1)S(1)}, bf16[1,128,256]{2,1,0:T(8,128)(2,1)S(1)}, u32[]{:S(2)}, u32[]{:S(2)}) %collective-permute-start.13) | collective-permute-done | bytes 65568 | tf_op jit(solution)/shard_map/ppermute | solution.py:461
  71.9 1.7 %collective-permute-done.11 = bf16[4,128,256]{2,1,0:T(8,128)(2,1)S(1)} collective-permute-done((bf16[4,128,256]{2,1,0:T(8,128)(2,1)S(1)}, bf16[4,128,256]{2,1,0:T(8,128)(2,1)S(1)}, u32[]{:S(2)}, u32[]{:S(2)}) %collective-permute-start.11) | collective-permute-done | bytes 262176 | tf_op jit(solution)/shard_map/ppermute | solution.py:461
  76.4 1.7 %collective-permute-start.15 = (bf16[2,128,256]{2,1,0:T(8,128)(2,1)S(1)}, bf16[2,128,256]{2,1,0:T(8,128)(2,1)S(1)}, u32[]{:S(2)}, u32[]{:S(2)}) collective-permute-start(bf16[2,128,256]{2,1,0:T(8,128)(2,1)S(1)} %get-tuple-element.204), channel_id=1, source_target_pairs={{0,4},{1,5},{2,6},{3,7},{4,0},{5,1},{6,2},{7,3},{8,12},{9,13},{10,... | collective-permute-start | bytes 393224 | tf_op jit(solution)/shard_map/ppermute | solution.py:461
  78.1 3.2 %shard_map.136 = (bf16[2,512,512]{2,1,0:T(8,128)(2,1)}, f32[2,512,512]{2,1,0:T(8,128)S(1)}) custom-call(bf16[2,128,512]{2,1,0:T(8,128)(2,1)S(1)} %get-tuple-element.127.refs_0_, bf16[2,128,512]{2,1,0:T(8,128)(2,1)S(1)} %get-tuple-element.130.refs_1_, bf16[2,128,512]{2,1,0:T(8,128)(2,1)S(1)} %get-tuple-element.144.refs_2_.refs_0_, ...), custom_call_target="tpu_custom_call" | custom-call | flops 4400000000 | bytes 400000 | tf_op jit(solution)/shard_map/pallas_call | solution.py:561
  82.9 3.1 %collective-permute-start.24 = (bf16[2,128,512]{2,1,0:T(8,128)(2,1)S(1)}, bf16[2,128,512]{2,1,0:T(8,128)(2,1)S(1)}, u32[]{:S(2)}, u32[]{:S(2)}) collective-permute-start(bf16[2,128,512]{2,1,0:T(8,128)(2,1)S(1)} %get-tuple-element.174), channel_id=1, source_target_pairs={{0,4},{1,5},{2,6},{3,7},{4,0},{5,1},{6,2},{7,3},{8,12},{9,13},{10,... | collective-permute-start | bytes 786440 | tf_op jit(solution)/shard_map/ppermute | solution.py:21
  89.6 2.5 %collective-permute-start.19 = (bf16[1,128,256]{2,1,0:T(8,128)(2,1)S(1)}, bf16[1,128,256]{2,1,0:T(8,128)(2,1)S(1)}, u32[]{:S(2)}, u32[]{:S(2)}) collective-permute-start(bf16[1,128,256]{2,1,0:T(8,128)(2,1)S(1)} %add_convert_fusion.4), channel_id=1, source_target_pairs={{0,4},{1,5},{2,6},{3,7},{4,0},{5,1},{6,2},{7,3},{8,12},{9,13},{10,... | collective-permute-start | bytes 196616 | tf_op jit(solution)/shard_map/ppermute | solution.py:461
  92.1 2.9 %collective-permute-done.21 = bf16[1,128,256]{2,1,0:T(8,128)(2,1)S(1)} collective-permute-done((bf16[1,128,256]{2,1,0:T(8,128)(2,1)S(1)}, bf16[1,128,256]{2,1,0:T(8,128)(2,1)S(1)}, u32[]{:S(2)}, u32[]{:S(2)}) %collective-permute-start.21) | collective-permute-done | bytes 65568 | tf_op jit(solution)/shard_map/ppermute | solution.py:461
  95.0 2.1 %collective-permute-done.20 = bf16[1,128,256]{2,1,0:T(8,128)(2,1)S(1)} collective-permute-done((bf16[1,128,256]{2,1,0:T(8,128)(2,1)S(1)}, bf16[1,128,256]{2,1,0:T(8,128)(2,1)S(1)}, u32[]{:S(2)}, u32[]{:S(2)}) %collective-permute-start.20) | collective-permute-done | bytes 65568 | tf_op jit(solution)/shard_map/ppermute | solution.py:461
  97.1 6.5 %collective-permute-start.27 = (bf16[4,128,256]{2,1,0:T(8,128)(2,1)S(1)}, bf16[4,128,256]{2,1,0:T(8,128)(2,1)S(1)}, u32[]{:S(2)}, u32[]{:S(2)}) collective-permute-start(bf16[4,128,256]{2,1,0:T(8,128)(2,1)S(1)} %pad_maximum_fusion.1), channel_id=1, source_target_pairs={{0,2},{1,3},{2,0},{3,1},{4,6},{5,7},{6,4},{7,5},{8,10},{9,11},{10,... | collective-permute-start | bytes 786440 | tf_op jit(solution)/shard_map/ppermute | solution.py:461
  103.8 7.0 %collective-permute-done.22 = bf16[4,128,256]{2,1,0:T(8,128)(2,1)S(1)} collective-permute-done((bf16[4,128,256]{2,1,0:T(8,128)(2,1)S(1)}, bf16[4,128,256]{2,1,0:T(8,128)(2,1)S(1)}, u32[]{:S(2)}, u32[]{:S(2)}) %collective-permute-start.22) | collective-permute-done | bytes 262176 | tf_op jit(solution)/shard_map/ppermute | solution.py:461
  111.5 1.8 %shard_map.139 = bf16[2,512,512]{2,1,0:T(8,128)(2,1)} custom-call(s32[1,4]{1,0:T(1,128)S(1)} %collective-permute-done.i0, s32[1,4]{1,0:T(1,128)S(1)} %collective-permute-done.1.i1, s32[1,4]{1,0:T(1,128)S(1)} %collective-permute-done.2.i2, s32[1,4]{1,0:T(1,128)S(1)} %collective-permute-done.3.i3, f32[2,512,512]{2,1,0:T(8,128)S(1)} %get-tuple-element.177.gt_ref, ...), custom_call_target="tpu_custom_call" | custom-call | tf_op jit(solution)/shard_map/pallas_call | solution.py:584
  113.6 2.4 %shard_map.140 = (f32[512,512]{1,0:T(8,128)}, f32[512,512]{1,0:T(8,128)}, f32[512,512]{1,0:T(8,128)}, f32[512,512]{1,0:T(8,128)}) custom-call(s32[1]{0:T(128)} %bitcast.1.place_ref, bf16[8,128,256]{2,1,0:T(8,128)(2,1)S(1)} %constant_dynamic-update-slice_fusion.5.refs_0_, bf16[8,128,256]{2,1,0:T(8,128)(2,1)S(1)} %collective-permute-done.28.refs_1_, ...), custom_call_target="tpu_custom_call" | custom-call | tf_op jit(solution)/shard_map/pallas_call | solution.py:505
  (80 shorter events, 25.4 us)
Async XLA Ops:
  0.6 7.2 %collective-permute-start.1 = (s32[1,4]{1,0:T(1,128)}, s32[1,4]{1,0:T(1,128)S(1)}, u32[]{:S(2)}, u32[]{:S(2)}) collective-permute-start(s32[1,4]{1,0:T(1,128)} %param.13), channel_id=1, source_target_pairs={{0,2},{1,3},{2,0},{3,1},{4,6},{5,7},{6,4},{7,5},{8,10},{9,11},{10,... | collective-permute-start | bytes 56 | tf_op jit(solution)/shard_map/ppermute | solution.py:21
  3.7 4.6 %collective-permute-start.3 = (s32[1,4]{1,0:T(1,128)}, s32[1,4]{1,0:T(1,128)S(1)}, u32[]{:S(2)}, u32[]{:S(2)}) collective-permute-start(s32[1,4]{1,0:T(1,128)} %param.13), channel_id=1, source_target_pairs={{0,8},{1,9},{2,10},{3,11},{4,12},{5,13},{6,14},{7,15},{8,0},{9,1},... | collective-permute-start | bytes 56 | tf_op jit(solution)/shard_map/ppermute | solution.py:21
  11.2 15.7 %collective-permute-start.4 = (bf16[2,128,512]{2,1,0:T(8,128)(2,1)S(1)}, bf16[2,128,512]{2,1,0:T(8,128)(2,1)S(1)}, u32[]{:S(2)}, u32[]{:S(2)}) collective-permute-start(bf16[2,128,512]{2,1,0:T(8,128)(2,1)S(1)} %get-tuple-element.114), channel_id=1, source_target_pairs={{0,1},{1,0},{2,3},{3,2},{4,5},{5,4},{6,7},{7,6},{8,9},{9,8},{10,11... | collective-permute-start | bytes 786440 | tf_op jit(solution)/shard_map/ppermute | solution.py:21
  11.3 15.7 %collective-permute-start.5 = (bf16[2,128,512]{2,1,0:T(8,128)(2,1)S(1)}, bf16[2,128,512]{2,1,0:T(8,128)(2,1)S(1)}, u32[]{:S(2)}, u32[]{:S(2)}) collective-permute-start(bf16[2,128,512]{2,1,0:T(8,128)(2,1)S(1)} %get-tuple-element.115), channel_id=1, source_target_pairs={{0,2},{1,3},{2,0},{3,1},{4,6},{5,7},{6,4},{7,5},{8,10},{9,11},{10,... | collective-permute-start | bytes 786440 | tf_op jit(solution)/shard_map/ppermute | solution.py:21
  11.9 15.1 %collective-permute-start.6 = (bf16[2,128,512]{2,1,0:T(8,128)(2,1)S(1)}, bf16[2,128,512]{2,1,0:T(8,128)(2,1)S(1)}, u32[]{:S(2)}, u32[]{:S(2)}) collective-permute-start(bf16[2,128,512]{2,1,0:T(8,128)(2,1)S(1)} %get-tuple-element.116), channel_id=1, source_target_pairs={{0,4},{1,5},{2,6},{3,7},{4,0},{5,1},{6,2},{7,3},{8,12},{9,13},{10,... | collective-permute-start | bytes 786440 | tf_op jit(solution)/shard_map/ppermute | solution.py:21
  13.5 14.7 %collective-permute-start.7 = (bf16[2,128,512]{2,1,0:T(8,128)(2,1)S(1)}, bf16[2,128,512]{2,1,0:T(8,128)(2,1)S(1)}, u32[]{:S(2)}, u32[]{:S(2)}) collective-permute-start(bf16[2,128,512]{2,1,0:T(8,128)(2,1)S(1)} %get-tuple-element.117), channel_id=1, source_target_pairs={{0,8},{1,9},{2,10},{3,11},{4,12},{5,13},{6,14},{7,15},{8,0},{9,1},... | collective-permute-start | bytes 786440 | tf_op jit(solution)/shard_map/ppermute | solution.py:21
  44.2 6.4 %collective-permute-start.8 = (bf16[8,128,256]{2,1,0:T(8,128)(2,1)S(1)}, bf16[8,128,256]{2,1,0:T(8,128)(2,1)S(1)}, u32[]{:S(2)}, u32[]{:S(2)}) collective-permute-start(bf16[8,128,256]{2,1,0:T(8,128)(2,1)S(1)} %get-tuple-element.143.refs_4_), channel_id=1, source_target_pairs={{0,1},{1,0},{2,3},{3,2},{4,5},{5,4},{6,7},{7,6},{8,9},{9,8},{10,11... | collective-permute-start | bytes 1572872 | tf_op jit(solution)/shard_map/ppermute | solution.py:461
  50.8 8.8 %collective-permute-start.9 = (bf16[4,128,256]{2,1,0:T(8,128)(2,1)S(1)}, bf16[4,128,256]{2,1,0:T(8,128)(2,1)S(1)}, u32[]{:S(2)}, u32[]{:S(2)}) collective-permute-start(bf16[4,128,256]{2,1,0:T(8,128)(2,1)S(1)} %slice.76.refs_3_), channel_id=1, source_target_pairs={{0,2},{1,3},{2,0},{3,1},{4,6},{5,7},{6,4},{7,5},{8,10},{9,11},{10,... | collective-permute-start | bytes 786440 | tf_op jit(solution)/shard_map/ppermute | solution.py:461
  61.9 6.9 %collective-permute-start.12 = (bf16[1,128,256]{2,1,0:T(8,128)(2,1)S(1)}, bf16[1,128,256]{2,1,0:T(8,128)(2,1)S(1)}, u32[]{:S(2)}, u32[]{:S(2)}) collective-permute-start(bf16[1,128,256]{2,1,0:T(8,128)(2,1)S(1)} %get-tuple-element.193), channel_id=1, source_target_pairs={{0,4},{1,5},{2,6},{3,7},{4,0},{5,1},{6,2},{7,3},{8,12},{9,13},{10,... | collective-permute-start | bytes 196616 | tf_op jit(solution)/shard_map/ppermute | solution.py:461
  62.0 6.9 %collective-permute-start.14 = (bf16[1,128,256]{2,1,0:T(8,128)(2,1)S(1)}, bf16[1,128,256]{2,1,0:T(8,128)(2,1)S(1)}, u32[]{:S(2)}, u32[]{:S(2)}) collective-permute-start(bf16[1,128,256]{2,1,0:T(8,128)(2,1)S(1)} %get-tuple-element.194), channel_id=1, source_target_pairs={{0,12},{1,13},{2,14},{3,15},{4,8},{5,9},{6,10},{7,11},{8,4},{9,5},... | collective-permute-start | bytes 196616 | tf_op jit(solution)/shard_map/ppermute | solution.py:461
  64.3 7.5 %collective-permute-start.13 = (bf16[1,128,256]{2,1,0:T(8,128)(2,1)S(1)}, bf16[1,128,256]{2,1,0:T(8,128)(2,1)S(1)}, u32[]{:S(2)}, u32[]{:S(2)}) collective-permute-start(bf16[1,128,256]{2,1,0:T(8,128)(2,1)S(1)} %get-tuple-element.195), channel_id=1, source_target_pairs={{0,8},{1,9},{2,10},{3,11},{4,12},{5,13},{6,14},{7,15},{8,0},{9,1},... | collective-permute-start | bytes 196616 | tf_op jit(solution)/shard_map/ppermute | solution.py:461
  65.6 7.9 %collective-permute-start.11 = (bf16[4,128,256]{2,1,0:T(8,128)(2,1)S(1)}, bf16[4,128,256]{2,1,0:T(8,128)(2,1)S(1)}, u32[]{:S(2)}, u32[]{:S(2)}) collective-permute-start(bf16[4,128,256]{2,1,0:T(8,128)(2,1)S(1)} %slice.79), channel_id=1, source_target_pairs={{0,2},{1,3},{2,0},{3,1},{4,6},{5,7},{6,4},{7,5},{8,10},{9,11},{10,... | collective-permute-start | bytes 786440 | tf_op jit(solution)/shard_map/ppermute | solution.py:461
  73.7 9.2 %collective-permute-start.17 = (bf16[2,128,256]{2,1,0:T(8,128)(2,1)S(1)}, bf16[2,128,256]{2,1,0:T(8,128)(2,1)S(1)}, u32[]{:S(2)}, u32[]{:S(2)}) collective-permute-start(bf16[2,128,256]{2,1,0:T(8,128)(2,1)S(1)} %get-tuple-element.202), channel_id=1, source_target_pairs={{0,12},{1,13},{2,14},{3,15},{4,8},{5,9},{6,10},{7,11},{8,4},{9,5},... | collective-permute-start | bytes 393224 | tf_op jit(solution)/shard_map/ppermute | solution.py:461
  74.9 12.5 %collective-permute-start.16 = (bf16[2,128,256]{2,1,0:T(8,128)(2,1)S(1)}, bf16[2,128,256]{2,1,0:T(8,128)(2,1)S(1)}, u32[]{:S(2)}, u32[]{:S(2)}) collective-permute-start(bf16[2,128,256]{2,1,0:T(8,128)(2,1)S(1)} %get-tuple-element.203), channel_id=1, source_target_pairs={{0,8},{1,9},{2,10},{3,11},{4,12},{5,13},{6,14},{7,15},{8,0},{9,1},... | collective-permute-start | bytes 393224 | tf_op jit(solution)/shard_map/ppermute | solution.py:461
  76.4 11.0 %collective-permute-start.15 = (bf16[2,128,256]{2,1,0:T(8,128)(2,1)S(1)}, bf16[2,128,256]{2,1,0:T(8,128)(2,1)S(1)}, u32[]{:S(2)}, u32[]{:S(2)}) collective-permute-start(bf16[2,128,256]{2,1,0:T(8,128)(2,1)S(1)} %get-tuple-element.204), channel_id=1, source_target_pairs={{0,4},{1,5},{2,6},{3,7},{4,0},{5,1},{6,2},{7,3},{8,12},{9,13},{10,... | collective-permute-start | bytes 393224 | tf_op jit(solution)/shard_map/ppermute | solution.py:461
  81.4 6.4 %collective-permute-start.18 = (bf16[2,128,512]{2,1,0:T(8,128)(2,1)S(1)}, bf16[2,128,512]{2,1,0:T(8,128)(2,1)S(1)}, u32[]{:S(2)}, u32[]{:S(2)}) collective-permute-start(bf16[2,128,512]{2,1,0:T(8,128)(2,1)S(1)} %get-tuple-element.170), channel_id=1, source_target_pairs={{0,2},{1,3},{2,0},{3,1},{4,6},{5,7},{6,4},{7,5},{8,10},{9,11},{10,... | collective-permute-start | bytes 786440 | tf_op jit(solution)/shard_map/ppermute | solution.py:21
  82.9 27.9 %collective-permute-start.23 = (bf16[2,128,512]{2,1,0:T(8,128)(2,1)S(1)}, bf16[2,128,512]{2,1,0:T(8,128)(2,1)S(1)}, u32[]{:S(2)}, u32[]{:S(2)}) collective-permute-start(bf16[2,128,512]{2,1,0:T(8,128)(2,1)S(1)} %get-tuple-element.172), channel_id=1, source_target_pairs={{0,1},{1,0},{2,3},{3,2},{4,5},{5,4},{6,7},{7,6},{8,9},{9,8},{10,11... | collective-permute-start | bytes 786440 | tf_op jit(solution)/shard_map/ppermute | solution.py:21
  82.9 27.9 %collective-permute-start.24 = (bf16[2,128,512]{2,1,0:T(8,128)(2,1)S(1)}, bf16[2,128,512]{2,1,0:T(8,128)(2,1)S(1)}, u32[]{:S(2)}, u32[]{:S(2)}) collective-permute-start(bf16[2,128,512]{2,1,0:T(8,128)(2,1)S(1)} %get-tuple-element.174), channel_id=1, source_target_pairs={{0,4},{1,5},{2,6},{3,7},{4,0},{5,1},{6,2},{7,3},{8,12},{9,13},{10,... | collective-permute-start | bytes 786440 | tf_op jit(solution)/shard_map/ppermute | solution.py:21
  87.7 7.3 %collective-permute-start.21 = (bf16[1,128,256]{2,1,0:T(8,128)(2,1)S(1)}, bf16[1,128,256]{2,1,0:T(8,128)(2,1)S(1)}, u32[]{:S(2)}, u32[]{:S(2)}) collective-permute-start(bf16[1,128,256]{2,1,0:T(8,128)(2,1)S(1)} %add_convert_fusion.4), channel_id=1, source_target_pairs={{0,12},{1,13},{2,14},{3,15},{4,8},{5,9},{6,10},{7,11},{8,4},{9,5},... | collective-permute-start | bytes 196616 | tf_op jit(solution)/shard_map/ppermute | solution.py:461
  89.4 7.7 %collective-permute-start.20 = (bf16[1,128,256]{2,1,0:T(8,128)(2,1)S(1)}, bf16[1,128,256]{2,1,0:T(8,128)(2,1)S(1)}, u32[]{:S(2)}, u32[]{:S(2)}) collective-permute-start(bf16[1,128,256]{2,1,0:T(8,128)(2,1)S(1)} %add_convert_fusion.4), channel_id=1, source_target_pairs={{0,8},{1,9},{2,10},{3,11},{4,12},{5,13},{6,14},{7,15},{8,0},{9,1},... | collective-permute-start | bytes 196616 | tf_op jit(solution)/shard_map/ppermute | solution.py:461
  89.6 14.0 %collective-permute-start.19 = (bf16[1,128,256]{2,1,0:T(8,128)(2,1)S(1)}, bf16[1,128,256]{2,1,0:T(8,128)(2,1)S(1)}, u32[]{:S(2)}, u32[]{:S(2)}) collective-permute-start(bf16[1,128,256]{2,1,0:T(8,128)(2,1)S(1)} %add_convert_fusion.4), channel_id=1, source_target_pairs={{0,4},{1,5},{2,6},{3,7},{4,0},{5,1},{6,2},{7,3},{8,12},{9,13},{10,... | collective-permute-start | bytes 196616 | tf_op jit(solution)/shard_map/ppermute | solution.py:461
  95.0 15.8 %collective-permute-start.25 = (bf16[2,128,512]{2,1,0:T(8,128)(2,1)S(1)}, bf16[2,128,512]{2,1,0:T(8,128)(2,1)S(1)}, u32[]{:S(2)}, u32[]{:S(2)}) collective-permute-start(bf16[2,128,512]{2,1,0:T(8,128)(2,1)S(1)} %get-tuple-element.175), channel_id=1, source_target_pairs={{0,8},{1,9},{2,10},{3,11},{4,12},{5,13},{6,14},{7,15},{8,0},{9,1},... | collective-permute-start | bytes 786440 | tf_op jit(solution)/shard_map/ppermute | solution.py:21
  97.1 13.8 %collective-permute-start.27 = (bf16[4,128,256]{2,1,0:T(8,128)(2,1)S(1)}, bf16[4,128,256]{2,1,0:T(8,128)(2,1)S(1)}, u32[]{:S(2)}, u32[]{:S(2)}) collective-permute-start(bf16[4,128,256]{2,1,0:T(8,128)(2,1)S(1)} %pad_maximum_fusion.1), channel_id=1, source_target_pairs={{0,2},{1,3},{2,0},{3,1},{4,6},{5,7},{6,4},{7,5},{8,10},{9,11},{10,... | collective-permute-start | bytes 786440 | tf_op jit(solution)/shard_map/ppermute | solution.py:461
  103.7 7.1 %collective-permute-start.22 = (bf16[4,128,256]{2,1,0:T(8,128)(2,1)S(1)}, bf16[4,128,256]{2,1,0:T(8,128)(2,1)S(1)}, u32[]{:S(2)}, u32[]{:S(2)}) collective-permute-start(bf16[4,128,256]{2,1,0:T(8,128)(2,1)S(1)} %pad_maximum_fusion), channel_id=1, source_target_pairs={{0,2},{1,3},{2,0},{3,1},{4,6},{5,7},{6,4},{7,5},{8,10},{9,11},{10,... | collective-permute-start | bytes 786440 | tf_op jit(solution)/shard_map/ppermute | solution.py:461
  (10 other events, 47.7 us)
